TPU v7x, 32 devices: a whole 2x2x4 slice. The times are simulated.
32 devices in a mesh: row: 8 (over y, x, core), col: 4 (over z).
Axes of the slice: x: 2, y: 2, z: 4, core: 2. Of those that a mesh axis runs over, the one named last changes fastest.
Arguments:
- displacement: bfloat16 [65536, 128], P(('row', 'col')), may hold values from -6 to 6
- connectivity: int32 [65536, 8], P(('row', 'col')), may hold values from 0 to 2303, as said below
- element_basis: bfloat16 [4, 32, 32], replicated, may hold values from -1 to 1
- material: float32 [8, 65536], P(None, ('row', 'col')), may hold values from -0.35 to 0.35
- traction: bfloat16 [49152, 128], P(('col', 'row')), may hold values from -6 to 6
- green: bfloat16 [2, 512, 196608], P(None, 'row', 'col'), may hold values from -0.013671875 to 0.013671875
- trace_node: int32 [32, 512], P(('row', 'col')), may hold values from 0 to 2047
- trace_weight: float32 [32, 512], P(('row', 'col')), may hold values from -0.4 to 0.4
- trace_count: int32 [32, 32], P(('row', 'col')), may hold values from 1 to 16
- recv_point: int32 [32, 512], P(('row', 'col')), may hold values from 0 to 3
Outputs:
- fe_out: bfloat16 [65536, 128], P(('row', 'col'))
- boundary_out: float32 [128, 128], P(('row', 'col'))
Inputs may be any that keep to these rules, and one draw needn't show every extreme that they name: `connectivity`: entries index a partition's extended numbering: below 128 the previous partition's last nodes, 128 + k its own node k, above that the next partition's first nodes; element k of a partition names only entries from k to k + 256; each partition's first element names 0 and its last names the largest value. `trace_count`: at most 16 live slots from one partition to one owner.
All inputs are finite; a program needn't handle non-finite values.
Results may differ from a plain program's by a relative error of at most 0.013.
Values may be sent and summed in bfloat16 or wider, within the bound.
No kernel may reach another device: no remote copies, remote signals or barrier semaphores. Data moves between devices by JAX's collectives and lax.ppermute only.
A program may use at most 64 MiB of HBM per device.

v0:
```python
import jax
import jax.numpy as jnp
from jax import lax
from jax.sharding import PartitionSpec as P

PTS_DEV = 4
HALO = 128


def with_halo(block, sides, width):
    for axis, dim in sides:
        count = lax.axis_size(axis)
        forward = [(i, i + 1) for i in range(count - 1)]
        backward = [(target, source) for source, target in forward]
        low = lax.ppermute(
            lax.slice_in_dim(block, block.shape[dim] - width, None, axis=dim), axis, forward
        )
        high = lax.ppermute(lax.slice_in_dim(block, 0, width, axis=dim), axis, backward)
        block = jnp.concatenate([low, block, high], axis=dim)
    return block


def element_forces(values, basis, coeffs):
    count = values.shape[0]
    lanes = values.shape[2]
    half = lanes // 8
    stacked = values.reshape(count, 32, lanes // 4)
    modes = jnp.einsum("mij,ejl->meil", basis, stacked, preferred_element_type=jnp.float32)
    real_c = coeffs[0::2][:, :, None, None]
    imag_c = coeffs[1::2][:, :, None, None]
    real_z = modes[..., :half]
    imag_z = modes[..., half:]
    real_y = jnp.sum(real_c * real_z - imag_c * imag_z, axis=0)
    imag_y = jnp.sum(real_c * imag_z + imag_c * real_z, axis=0)
    return jnp.concatenate([real_y, imag_y], axis=2).reshape(count, 8, lanes)


def complex_rows(block, panel):
    lanes = panel.shape[1] * 4
    half = lanes // 8
    flat = block.reshape(-1, block.shape[2])
    both = jnp.dot(flat, panel, preferred_element_type=jnp.float32).reshape(
        2, block.shape[1], lanes // 4
    )
    real_part = both[0, :, :half] - both[1, :, half:]
    imag_part = both[0, :, half:] + both[1, :, :half]
    return jnp.concatenate([real_part, imag_part], axis=1).reshape(-1, lanes)


def shards(
    displacement,
    connectivity,
    element_basis,
    material,
    traction,
    green,
    trace_node,
    trace_weight,
    trace_count,
    recv_point,
):
    nodes = displacement.shape[0]
    lanes = displacement.shape[1]
    devices = trace_count.shape[1]
    slots = trace_node.shape[1] // devices
    live = (lax.broadcasted_iota(jnp.int32, (devices, slots), 1) < trace_count[0][:, None]).reshape(
        -1
    )
    scale = jnp.where(live, trace_weight[0], jnp.zeros_like(trace_weight[0]))
    picked = displacement[trace_node[0]]
    outgoing = (picked.astype(jnp.float32) * scale[:, None]).astype(jnp.bfloat16)
    arrived = lax.all_to_all(
        outgoing.reshape(devices, slots, lanes),
        ("row", "col"),
        split_axis=0,
        concat_axis=0,
        tiled=True,
    ).reshape(devices * slots, lanes)
    panel = lax.all_gather(traction, "row", axis=0, tiled=True).reshape(-1, lanes // 4)
    slab_product = lax.psum_scatter(
        complex_rows(green, panel).astype(jnp.bfloat16), "col", scatter_dimension=0, tiled=True
    ).astype(jnp.float32)
    extended = with_halo(displacement, ((("row", "col"), 0),), HALO)
    ghost = (extended.shape[0] - nodes) // 2
    block_size = min(nodes, 256)
    blocks = nodes // block_size
    window = block_size + 2 * ghost
    pieces = -(-window // block_size)
    links_blocks = connectivity.reshape(blocks, block_size * 8)
    coeff_blocks = material.reshape(material.shape[0], blocks, block_size).transpose(1, 0, 2)
    columns_iota = lax.broadcasted_iota(jnp.int32, (1, window), 1)

    def one_block(carry, item):
        links, coeffs, number = item
        start = number * block_size
        rows = lax.dynamic_slice_in_dim(extended, start, window, 0)
        selector = ((links - start)[:, None] == columns_iota).astype(jnp.bfloat16)
        values = jnp.dot(selector, rows, preferred_element_type=jnp.float32).astype(jnp.bfloat16)
        forces = element_forces(
            values.reshape(block_size, 8, lanes), element_basis, coeffs
        ).reshape(-1, lanes)
        upper = forces.astype(jnp.bfloat16)
        lower = (forces - upper.astype(jnp.float32)).astype(jnp.bfloat16)
        dims = (((0,), (0,)), ((), ()))
        added = lax.dot_general(selector, upper, dims, preferred_element_type=jnp.float32)
        added = added + lax.dot_general(selector, lower, dims, preferred_element_type=jnp.float32)
        return (carry, added.reshape(pieces, block_size, lanes))

    numbers = jnp.arange(blocks, dtype=jnp.int32)
    unused, outputs = lax.scan(
        one_block, jnp.zeros((), jnp.float32), (links_blocks, coeff_blocks, numbers)
    )
    totals = jnp.zeros((blocks + pieces - 1, block_size, lanes), jnp.float32)
    for offset in range(pieces):
        shifted = jnp.pad(outputs[:, offset], ((offset, pieces - 1 - offset), (0, 0), (0, 0)))
        totals = totals + shifted
    totals = totals.reshape(-1, lanes)
    fe_out = totals[ghost : ghost + nodes].astype(jnp.bfloat16)
    onehot = (recv_point[0][:, None] == jnp.arange(PTS_DEV, dtype=jnp.int32)[None, :]).astype(
        jnp.bfloat16
    )
    trace_sum = jnp.einsum("kp,kl->pl", onehot, arrived, preferred_element_type=jnp.float32)
    boundary_out = trace_sum - slab_product
    return (fe_out, boundary_out)


def solution(mesh):
    placed = (
        P(("row", "col"), None),
        P(("row", "col"), None),
        P(),
        P(None, ("row", "col")),
        P(("col", "row"), None),
        P(None, "row", "col"),
        P(("row", "col"), None),
        P(("row", "col"), None),
        P(("row", "col"), None),
        P(("row", "col"), None),
    )
    return jax.shard_map(
        shards,
        mesh=mesh,
        in_specs=placed,
        out_specs=(P(("row", "col"), None), P(("row", "col"), None)),
        check_vma=False,
    )
```

profile of v0, /device:TPU:0, one launch (start us, length us, event | category | flops | bytes accessed | tf_op | source)
XLA Modules:
  0.0 267.1 jit_solution(14855025352061418345)
XLA Ops:
  8.0 4.9 %collective-permute-start = (bf16[128,128]{1,0:T(8,128)(2,1)S(1)}, bf16[128,128]{1,0:T(8,128)(2,1)S(1)}, u32[]{:S(2)}, u32[]{:S(2)}) collective-permute-start(bf16[128,128]{1,0:T(8,128)(2,1)S(1)} %get-tuple-element.77), channel_id=1, source_target_pairs={{0,1},{1,2},{2,3},{3,4},{4,5},{5,6},{6,7},{7,8},{8,9},{9,10},{10,1... | collective-permute-start | bytes 98312 | tf_op jit(solution)/shard_map/ppermute | solution.py:15
  20.7 6.9 %all-to-all-start = ((bf16[32,16,128]{2,1,0:T(8,128)(2,1)}), bf16[32,16,128]{2,1,0:T(8,128)(2,1)S(1)}, u32[]{:S(2)}, u32[]{:S(2)}) async-start(bf16[32,16,128]{2,1,0:T(8,128)(2,1)} %fusion.17), calls=%async_computation | async-start | bytes 262144 | tf_op jit(solution)/shard_map/all_to_all | solution.py:72
  29.8 186.8 %while.11 = (s32[]{:T(128)}, f32[8,2,256,128]{3,2,1,0:T(8,128)}, s32[8,2048]{1,0:T(8,128)S(1)}, s32[8]{0:T(128)S(1)}, f32[8,8,256]{2,1,0:T(8,128)}, /*index=5*/b...) while((s32[]{:T(128)}, f32[8,2,256,128]{3,2,1,0:T(8,128)}, ...), condition=%wide.region_3.4_spmd.clone, body=%wide.region_0.3_spmd.clone.sunk | while | flops 881395712 | bytes 22504120 | solution.py:110
  41.6 4.4 %copy.45 = f32[256,32,32]{2,1,0:T(8,128)} copy(f32[256,32,32]{0,1,2:T(8,128)S(1)} %pad_maximum_fusion.4) | data formatting | bytes 2097152 | tf_op jit(solution)/shard_map/while/body/eval_jaxpr/concatenate | solution.py:35
  46.0 3.3 %reshape.135 = f32[2048,128]{1,0:T(8,128)S(1)} reshape(f32[256,32,32]{2,1,0:T(8,128)} %copy.45) | data formatting | bytes 2097152 | tf_op jit(solution)/shard_map/while/body/eval_jaxpr/reshape;while/body/eval_jaxpr/reshape | solution.py:101
  65.0 4.4 %copy.45 = f32[256,32,32]{2,1,0:T(8,128)} copy(f32[256,32,32]{0,1,2:T(8,128)S(1)} %pad_maximum_fusion.4) | data formatting | bytes 2097152 | tf_op jit(solution)/shard_map/while/body/eval_jaxpr/concatenate | solution.py:35
  69.4 3.3 %reshape.135 = f32[2048,128]{1,0:T(8,128)S(1)} reshape(f32[256,32,32]{2,1,0:T(8,128)} %copy.45) | data formatting | bytes 2097152 | tf_op jit(solution)/shard_map/while/body/eval_jaxpr/reshape;while/body/eval_jaxpr/reshape | solution.py:101
  85.3 2.9 %subtract_reduce_fusion.2 = (f32[256,32,16]{0,1,2:T(8,128)S(1)}, f32[256,32,16]{0,1,2:T(8,128)S(1)}) fusion(f32[4,256,32,32]{1,2,0,3:T(8,128)} %convolution_bitcast_fusion.2, f32[4,256]{1,0:T(4,128)S(1)} %slice.93, f32[4,256]{1,0:T(4,128)S(1)} %slice.94), kind=kLoop, calls=%fused_computation.9.clone.1 | loop fusion | flops 3932160 | bytes 5251072 | tf_op jit(solution)/shard_map/while/body/eval_jaxpr/reduce_sum | solution.py:33
  88.3 4.4 %copy.45 = f32[256,32,32]{2,1,0:T(8,128)} copy(f32[256,32,32]{0,1,2:T(8,128)S(1)} %pad_maximum_fusion.4) | data formatting | bytes 2097152 | tf_op jit(solution)/shard_map/while/body/eval_jaxpr/concatenate | solution.py:35
  92.7 3.3 %reshape.135 = f32[2048,128]{1,0:T(8,128)S(1)} reshape(f32[256,32,32]{2,1,0:T(8,128)} %copy.45) | data formatting | bytes 2097152 | tf_op jit(solution)/shard_map/while/body/eval_jaxpr/reshape;while/body/eval_jaxpr/reshape | solution.py:101
  111.7 4.4 %copy.45 = f32[256,32,32]{2,1,0:T(8,128)} copy(f32[256,32,32]{0,1,2:T(8,128)S(1)} %pad_maximum_fusion.4) | data formatting | bytes 2097152 | tf_op jit(solution)/shard_map/while/body/eval_jaxpr/concatenate | solution.py:35
  116.1 3.3 %reshape.135 = f32[2048,128]{1,0:T(8,128)S(1)} reshape(f32[256,32,32]{2,1,0:T(8,128)} %copy.45) | data formatting | bytes 2097152 | tf_op jit(solution)/shard_map/while/body/eval_jaxpr/reshape;while/body/eval_jaxpr/reshape | solution.py:101
  132.0 2.9 %subtract_reduce_fusion.2 = (f32[256,32,16]{0,1,2:T(8,128)S(1)}, f32[256,32,16]{0,1,2:T(8,128)S(1)}) fusion(f32[4,256,32,32]{1,2,0,3:T(8,128)} %convolution_bitcast_fusion.2, f32[4,256]{1,0:T(4,128)S(1)} %slice.93, f32[4,256]{1,0:T(4,128)S(1)} %slice.94), kind=kLoop, calls=%fused_computation.9.clone.1 | loop fusion | flops 3932160 | bytes 5251072 | tf_op jit(solution)/shard_map/while/body/eval_jaxpr/reduce_sum | solution.py:33
  135.0 4.4 %copy.45 = f32[256,32,32]{2,1,0:T(8,128)} copy(f32[256,32,32]{0,1,2:T(8,128)S(1)} %pad_maximum_fusion.4) | data formatting | bytes 2097152 | tf_op jit(solution)/shard_map/while/body/eval_jaxpr/concatenate | solution.py:35
  139.4 3.3 %reshape.135 = f32[2048,128]{1,0:T(8,128)S(1)} reshape(f32[256,32,32]{2,1,0:T(8,128)} %copy.45) | data formatting | bytes 2097152 | tf_op jit(solution)/shard_map/while/body/eval_jaxpr/reshape;while/body/eval_jaxpr/reshape | solution.py:101
  158.4 4.4 %copy.45 = f32[256,32,32]{2,1,0:T(8,128)} copy(f32[256,32,32]{0,1,2:T(8,128)S(1)} %pad_maximum_fusion.4) | data formatting | bytes 2097152 | tf_op jit(solution)/shard_map/while/body/eval_jaxpr/concatenate | solution.py:35
  162.8 3.3 %reshape.135 = f32[2048,128]{1,0:T(8,128)S(1)} reshape(f32[256,32,32]{2,1,0:T(8,128)} %copy.45) | data formatting | bytes 2097152 | tf_op jit(solution)/shard_map/while/body/eval_jaxpr/reshape;while/body/eval_jaxpr/reshape | solution.py:101
  181.7 4.4 %copy.45 = f32[256,32,32]{2,1,0:T(8,128)} copy(f32[256,32,32]{0,1,2:T(8,128)S(1)} %pad_maximum_fusion.4) | data formatting | bytes 2097152 | tf_op jit(solution)/shard_map/while/body/eval_jaxpr/concatenate | solution.py:35
  186.1 3.3 %reshape.135 = f32[2048,128]{1,0:T(8,128)S(1)} reshape(f32[256,32,32]{2,1,0:T(8,128)} %copy.45) | data formatting | bytes 2097152 | tf_op jit(solution)/shard_map/while/body/eval_jaxpr/reshape;while/body/eval_jaxpr/reshape | solution.py:101
  205.0 4.4 %copy.45 = f32[256,32,32]{2,1,0:T(8,128)} copy(f32[256,32,32]{0,1,2:T(8,128)S(1)} %pad_maximum_fusion.4) | data formatting | bytes 2097152 | tf_op jit(solution)/shard_map/while/body/eval_jaxpr/concatenate | solution.py:35
  209.4 3.3 %reshape.135 = f32[2048,128]{1,0:T(8,128)S(1)} reshape(f32[256,32,32]{2,1,0:T(8,128)} %copy.45) | data formatting | bytes 2097152 | tf_op jit(solution)/shard_map/while/body/eval_jaxpr/reshape;while/body/eval_jaxpr/reshape | solution.py:101
  219.5 14.4 %reshape.107 = bf16[49152,32]{1,0:T(8,128)(2,1)} reshape(bf16[12288,128]{1,0:T(8,128)(2,1)} %all-gather.2.cloned.1.call-done) | data formatting | bytes 6291456 | tf_op jit(solution)/shard_map/reshape | solution.py:79
  234.0 13.2 %fusion.15 = f32[2,64,32]{1,2,0:T(8,128)S(1)} fusion(bf16[2,64,49152]{2,1,0:T(8,128)(2,1)} %param.17, bf16[49152,32]{1,0:T(8,128)(2,1)} %reshape.107), kind=kOutput, calls=%fused_computation.24 | convolution fusion | flops 402653184 | bytes 15745024 | tf_op jit(solution)/shard_map/dot_general | solution.py:42
  247.4 12.0 %all-reduce.2 = bf16[16,128]{1,0:T(8,128)(2,1)S(1)} all-reduce(bf16[16,128]{1,0:T(8,128)(2,1)S(1)} %convert_element_type.40), channel_id=2, replica_groups=mesh['row'=8,'col'=4] {'col'}, use_global_device_ids=true, to_apply=%region_4.5.clone | all-reduce | flops 2048 | bytes 8192
  (153 shorter events, 127.7 us)
Async XLA Ops:
  7.2 20.5 %copy-start.3 = (s32[2048,8]{0,1:T(8,128)S(1)}, s32[2048,8]{0,1:T(8,128)}, u32[]{:S(2)}) copy-start(s32[2048,8]{0,1:T(8,128)} %param.13) | copy-start | bytes 196612
  7.2 212.4 %all-gather.2.cloned.1.call-start = ((), (), s32[]{:S(2)}) async-start(), calls=%async_computation.1 | async-start | bytes 3538944 | tf_op jit(solution)/shard_map/all_gather | solution.py:79
  8.0 21.7 %collective-permute-start = (bf16[128,128]{1,0:T(8,128)(2,1)S(1)}, bf16[128,128]{1,0:T(8,128)(2,1)S(1)}, u32[]{:S(2)}, u32[]{:S(2)}) collective-permute-start(bf16[128,128]{1,0:T(8,128)(2,1)S(1)} %get-tuple-element.77), channel_id=1, source_target_pairs={{0,1},{1,2},{2,3},{3,4},{4,5},{5,6},{6,7},{7,8},{8,9},{9,10},{10,1... | collective-permute-start | bytes 98312 | tf_op jit(solution)/shard_map/ppermute | solution.py:15
  12.9 16.8 %collective-permute-start.1 = (bf16[128,128]{1,0:T(8,128)(2,1)S(1)}, bf16[128,128]{1,0:T(8,128)(2,1)S(1)}, u32[]{:S(2)}, u32[]{:S(2)}) collective-permute-start(bf16[128,128]{1,0:T(8,128)(2,1)S(1)} %get-tuple-element.78), channel_id=1, source_target_pairs={{1,0},{2,1},{3,2},{4,3},{5,4},{6,5},{7,6},{8,7},{9,8},{10,9},{11,1... | collective-permute-start | bytes 98312 | tf_op jit(solution)/shard_map/ppermute | solution.py:18
  14.3 14.2 %copy-start.5 = (u32[32]{0:T(128)S(1)}, u32[32]{0:T(128)}, u32[]{:S(2)}) copy-start(u32[32]{0:T(128)} %constant.38) | copy-start | bytes 388
  14.3 15.5 %copy-start = (bf16[2048,128]{1,0:T(8,128)(2,1)S(1)}, bf16[2048,128]{1,0:T(8,128)(2,1)}, u32[]{:S(2)}) copy-start(bf16[2048,128]{1,0:T(8,128)(2,1)} %param.12) | copy-start | bytes 1572868
  17.2 12.6 %copy-start.2 = (bf16[4,32,32]{2,1,0:T(8,128)(2,1)S(1)}, bf16[4,32,32]{2,1,0:T(8,128)(2,1)}, u32[]{:S(2)}) copy-start(bf16[4,32,32]{2,1,0:T(8,128)(2,1)} %param.14) | copy-start | bytes 24580
  20.7 238.7 %all-to-all-start = ((bf16[32,16,128]{2,1,0:T(8,128)(2,1)}), bf16[32,16,128]{2,1,0:T(8,128)(2,1)S(1)}, u32[]{:S(2)}, u32[]{:S(2)}) async-start(bf16[32,16,128]{2,1,0:T(8,128)(2,1)} %fusion.17), calls=%async_computation | async-start | bytes 262144 | tf_op jit(solution)/shard_map/all_to_all | solution.py:72
  216.6 1.9 copy-start.1
  234.0 25.4 %copy-start.4 = (s32[1,512]{1,0:T(1,128)S(1)}, s32[1,512]{1,0:T(1,128)}, u32[]{:S(2)}) copy-start(s32[1,512]{1,0:T(1,128)} %param.21) | copy-start | bytes 6148
Sparse Core Ops, SparseCore 0:
  14.4 35.7 all-gather.1
where the time goes:
time: 269 us; the launch traced here: 267 us
  local copies, waits for them, and re-layouts  124 us (46%)
  matrix products  68.9 us (26%)
  other arithmetic  28.3 us (11%)
  between operations  14.9 us (6%)
  starting transfers between devices  13.2 us (5%)
  blocking collectives  12 us (4%)
  loops' own time  5.77 us (2%)
    concatenate x8, local copies, waits for them, and re-layouts, element_forces(): return jnp.concatenate([real_y, imag_y], axis=2).reshape(count, 8, lanes)  35.2 us
    reshape x8, local copies, waits for them, and re-layouts, one_block(): forces = element_forces(values.reshape(block_size, 8, lanes), element_bas...  26.2 us
    reshape x16, local copies, waits for them, and re-layouts, element_forces(): stacked = values.reshape(count, 32, lanes // 4)  23.9 us
    reduce_sum x8, other arithmetic, element_forces(): real_y = jnp.sum(real_c * real_z - imag_c * imag_z, axis=0)  23.5 us
    dot_general x8, matrix products, element_forces(): jnp.einsum('mij,ejl->meil', basis, stacked, preferred_element_type=jnp.fl...  20.9 us
    reshape x1, local copies, waits for them, and re-layouts, shards(): lax.all_gather(traction, 'row', axis=0, tiled=True).reshape(-1, lanes // 4)  14.4 us
    dot_general x1, matrix products, complex_rows(): jnp.dot(flat, panel, preferred_element_type=jnp.float32)  13.2 us
    dot_general x8, matrix products, one_block(): lax.dot_general(selector, lower, dims, preferred_element_type=jnp.float32)  12.7 us
  transfers between devices with their start and end apart: 4, of which 0 were waited for; matrix products, arithmetic and copies ran while one was open for 82% of the time, Pallas kernels for 0%

commit v1 on v0

v1 whole, which is shorter than its diff:
```python
import functools

import jax
import jax.numpy as jnp
from jax import lax
from jax.experimental import pallas as pl
from jax.experimental.pallas import tpu as pltpu
from jax.sharding import PartitionSpec as P

PTS = 4
SLOT = 16
HALO = 128
EB = 256
WIN = EB + 2 * HALO
NT = (((1,), (1,)), ((), ()))
F32 = jnp.float32
BF16 = jnp.bfloat16
VMEM = pl.BlockSpec(memory_space=pltpu.VMEM)


def iota(shape, axis):
    return lax.broadcasted_iota(jnp.int32, shape, axis)


def fe_kernel(low, disp, high, links, basis, material, out, xt, wcat, dist, sel, vs, us, fs, acc):
    nodes = disp.shape[0]
    blocks = nodes // EB
    tiles = nodes // 128

    def place(index, rows):
        xt[:, pl.ds(index * 128, 128)] = rows.astype(F32).T.astype(BF16)

    place(0, low[...])
    for i in range(tiles):
        place(i + 1, disp[i * 128 : (i + 1) * 128, :])
    place(tiles + 1, high[...])

    spread = (iota((256, 32), 0) // 8 == iota((256, 32), 1)).astype(BF16)
    same = iota((256, 256), 0) % 8 == iota((256, 256), 1) % 8
    for m in range(4):
        tall = jnp.dot(spread, basis[m], preferred_element_type=F32).astype(BF16)
        wide = lax.dot_general(tall, spread, NT, preferred_element_type=F32)
        wcat[:, m * 256 : (m + 1) * 256] = jnp.where(same, wide, 0.0).astype(BF16)

    gap = iota((WIN, EB), 0) - iota((WIN, EB), 1)
    dist[...] = jnp.where((gap >= 0) & (gap <= 2 * HALO), gap, -1).astype(F32).astype(BF16)
    acc[...] = jnp.zeros_like(acc)

    def block(b, slot):
        at = pl.multiple_of(b * EB, EB)
        offsets = (links[:, pl.ds(at, EB)] - (at + iota((8, EB), 1))).astype(F32).astype(BF16)
        window = xt[:, pl.ds(at, WIN)]
        for n in range(8):
            hit = dist[...] == offsets[n : n + 1, :]
            chosen = jnp.where(hit, jnp.ones((), BF16), jnp.zeros((), BF16))
            sel[slot, :, n * EB : (n + 1) * EB] = chosen
            v = jnp.dot(window, chosen, preferred_element_type=F32)
            for g in range(4):
                part = jnp.concatenate([v[d * 32 + g * 8 : d * 32 + g * 8 + 8, :] for d in range(4)], axis=0)
                vs[slot, g, n * 32 : (n + 1) * 32, :] = part.astype(BF16)
        coeffs = material[:, pl.ds(at, EB)].astype(F32)
        for h in range(2):
            for n in range(8):
                rows = slice(n * 32, (n + 1) * 32)
                re = vs[slot, h, rows, :].astype(F32)
                im = vs[slot, 2 + h, rows, :].astype(F32)
                for m in range(4):
                    cr = coeffs[2 * m : 2 * m + 1, :]
                    ci = coeffs[2 * m + 1 : 2 * m + 2, :]
                    up = slice(m * 256 + n * 32, m * 256 + (n + 1) * 32)
                    us[slot, h, 0, up, :] = (cr * re - ci * im).astype(BF16)
                    us[slot, h, 1, up, :] = (cr * im + ci * re).astype(BF16)
            for p in range(2):
                f = jnp.dot(wcat[...], us[slot, h, p], preferred_element_type=F32)
                g = 2 * p + h
                for n in range(8):
                    fs[slot, g * 32 : (g + 1) * 32, n * EB : (n + 1) * EB] = f[n * 32 : (n + 1) * 32, :].astype(BF16)
        acc[:, pl.ds(at, WIN)] += lax.dot_general(fs[slot], sel[slot], NT, preferred_element_type=F32)

    def finish(i):
        tile = acc[:, pl.ds(HALO + i * 128, 128)]
        rows = [tile[(g * 4 + d) * 8 : (g * 4 + d) * 8 + 8, :] for d in range(4) for g in range(4)]
        out[pl.ds(i * 128, 128), :] = jnp.concatenate(rows, axis=0).T.astype(BF16)

    def step(i, carry):
        block(2 * i, 0)
        block(2 * i + 1, 1)
        return carry

    lax.fori_loop(0, blocks // 2, step, 0)
    for i in range(tiles):
        finish(i)


def fe_call(low, disp, high, links, basis, material):
    nodes = disp.shape[0]
    return pl.pallas_call(
        fe_kernel,
        out_shape=jax.ShapeDtypeStruct((nodes, 128), BF16),
        in_specs=[pl.BlockSpec(memory_space=pltpu.VMEM)] * 6,
        out_specs=pl.BlockSpec(memory_space=pltpu.VMEM),
        scratch_shapes=[
            pltpu.VMEM((128, nodes + 2 * HALO), BF16),
            pltpu.VMEM((256, 1024), BF16),
            pltpu.VMEM((WIN, EB), BF16),
            pltpu.VMEM((2, WIN, 8 * EB), BF16),
            pltpu.VMEM((2, 4, 256, EB), BF16),
            pltpu.VMEM((2, 2, 2, 1024, EB), BF16),
            pltpu.VMEM((2, 128, 8 * EB), BF16),
            pltpu.VMEM((128, nodes + 2 * HALO), F32),
        ],
        compiler_params=pltpu.CompilerParams(vmem_limit_bytes=24 * 2**20),
        cost_estimate=pl.CostEstimate(flops=nodes * 8000000, bytes_accessed=2**21, transcendentals=0),
    )(low, disp, high, links, basis, material)


def prepare_kernel(rows, cols, traction, disp, node, weight, count, recv, *outs):
    masks = rows // 2
    messages, points = outs[:masks], outs[masks : masks + cols]
    tail, head, slots = outs[masks + cols :]
    lines = traction.shape[0]
    row, col = lax.axis_index("row"), lax.axis_index("col")
    tail[...] = disp[disp.shape[0] - HALO :, :]
    head[...] = disp[:HALO, :]

    widen = (iota((128, 512), 1) // 4 == iota((128, 512), 0)).astype(BF16)
    comp = iota((32, 512), 1) % 4
    for i in range(lines // 128):
        flipped = traction[i * 128 : (i + 1) * 128, :].astype(F32).T.astype(BF16)
        wide = jnp.dot(flipped, widen, preferred_element_type=F32)
        line = wide[:32]
        for k in range(1, 4):
            line = jnp.where(comp == k, wide[k * 32 : (k + 1) * 32], line)
        line = line.astype(BF16)
        for message in messages:
            message[:, i * 512 : (i + 1) * 512] = line

    total = node.shape[1]
    devices = count.shape[1]
    copies = (iota((devices, total), 1) // SLOT == iota((devices, total), 0)).astype(BF16)
    counts = jnp.broadcast_to(count[...].astype(F32), (8, devices)).astype(BF16)
    live = jnp.dot(counts, copies, preferred_element_type=F32)
    scale = jnp.where((iota((8, total), 1) % SLOT).astype(F32) < live, weight[...], 0.0)
    upright = jnp.where(iota((8, total), 0) == 0, node[...].astype(F32), scale).T
    for i in range(total // 256):
        chunk = upright[i * 256 : (i + 1) * 256]
        hit = chunk[:, 0:1] == iota((256, disp.shape[0]), 1).astype(F32)
        picked = jnp.dot(jnp.where(hit, 1.0, 0.0).astype(BF16), disp[...], preferred_element_type=F32)
        slots[i * 256 : (i + 1) * 256, :] = (picked * chunk[:, 1:2]).astype(BF16)

    each = cols * SLOT
    for k in range(masks):
        for core in range(2):
            target = (row // 2 ^ k) * 2 + core
            for t in range(each // 32):
                lane = lines * 4 + (core * (each // 32) + t) * 128
                start = pl.multiple_of(target * each + t * 32, 32)
                messages[k][:, lane : lane + 128] = slots[pl.ds(start, 32), :]

    width = rows * SLOT
    source = iota((total, width), 0)
    place = iota((total, width), 1)
    values = jnp.broadcast_to(recv[...].astype(F32), (8, total)).astype(BF16)
    for s in range(cols):
        other = lax.rem(col + s, cols)
        take = source == (place // SLOT * cols + other) * SLOT + place % SLOT
        points[s][...] = jnp.dot(values, take.astype(BF16), preferred_element_type=F32)


def prepare_call(rows, cols, traction, disp, node, weight, count, recv):
    masks = rows // 2
    message = jax.ShapeDtypeStruct((32, traction.shape[0] * 4 + cols * SLOT * 8), BF16)
    point = jax.ShapeDtypeStruct((8, rows * SLOT), F32)
    halo = jax.ShapeDtypeStruct((HALO, 128), BF16)
    return pl.pallas_call(
        functools.partial(prepare_kernel, rows, cols),
        out_shape=[message] * masks + [point] * cols + [halo] * 2,
        in_specs=[VMEM] * 6,
        out_specs=[VMEM] * (masks + cols + 2),
        scratch_shapes=[pltpu.VMEM((node.shape[1], 128), BF16)],
        compiler_params=pltpu.CompilerParams(vmem_limit_bytes=40 * 2**20),
    )(traction, disp, node, weight, count, recv)


def slab_kernel(rows, cols, green, *refs):
    messages, points = refs[:rows], refs[rows : rows + cols]
    outs = refs[rows + cols : rows + 2 * cols]
    held, sent, traced, total, sems = refs[rows + 2 * cols :]
    row, col = lax.axis_index("row"), lax.axis_index("col")
    high = green.shape[1]
    length = green.shape[2] // rows
    copies = []
    for k in range(rows):
        start = pl.multiple_of((row ^ k) * length, 128)
        copy = pltpu.make_async_copy(green.at[:, :, pl.ds(start, length)], held.at[k], sems.at[k])
        copy.start()
        copies.append(copy)

    each = cols * SLOT
    core = row % 2
    for k in range(rows):
        into = pl.multiple_of((row ^ k) * SLOT, SLOT)
        for t in range(each // 32):
            lane = pl.multiple_of(length + (core * (each // 32) + t) * 128, 128)
            pair = messages[k][:, pl.ds(lane, 128)]
            sent[2 * t, pl.ds(into, SLOT), :] = pair[:SLOT]
            sent[2 * t + 1, pl.ds(into, SLOT), :] = pair[SLOT:]

    both = jnp.zeros((2 * high, 32), F32)
    for k in range(rows):
        copies[k].wait()
        flat = held[k].reshape(2 * high, length)
        both = both + lax.dot_general(flat, messages[k][:, :length], NT, preferred_element_type=F32)
    real = both[:high, :16] - both[high:, 16:]
    imag = both[:high, 16:] + both[high:, :16]
    total[...] = jnp.concatenate([real, imag, jnp.zeros((high, 96), F32)], axis=1)
    for s in range(cols):
        other = lax.rem(col + cols - s, cols)
        hot = (points[s][...] == iota(points[s].shape, 0).astype(F32)).astype(BF16)
        traced[other] = jnp.dot(hot, sent[other], preferred_element_type=F32)
    for c in range(cols):
        parts = [total[pl.ds(c * PTS * 4 + k, PTS, stride=4), :][:, :32] for k in range(4)]
        traced[c, :PTS, :] = traced[c, :PTS, :] - jnp.concatenate(parts, axis=1)
    for s in range(cols):
        outs[s][...] = traced[lax.rem(col + s, cols), :PTS, :]


def slab_call(rows, cols, green, messages, points):
    high = green.shape[1]
    length = green.shape[2] // rows
    part = jax.ShapeDtypeStruct((PTS, 128), F32)
    return pl.pallas_call(
        functools.partial(slab_kernel, rows, cols),
        out_shape=[part] * cols,
        in_specs=[pl.BlockSpec(memory_space=pl.ANY)] + [VMEM] * (rows + cols),
        out_specs=[VMEM] * cols,
        scratch_shapes=[
            pltpu.VMEM((rows, 2, high, length), BF16),
            pltpu.VMEM((cols, rows * SLOT, 128), BF16),
            pltpu.VMEM((cols, 8, 128), F32),
            pltpu.VMEM((high, 128), F32),
            pltpu.SemaphoreType.DMA((rows,)),
        ],
        compiler_params=pltpu.CompilerParams(vmem_limit_bytes=40 * 2**20),
    )(green, *messages, *points)


def shards(rows, cols, displacement, connectivity, element_basis, material, traction, green, node, weight, count, recv):
    made = prepare_call(rows, cols, traction, displacement, node, weight, count, recv)
    masks = rows // 2
    messages, points, (tail, head) = made[:masks], made[masks : masks + cols], made[masks + cols :]
    flat = ("row", "col")
    last = rows * cols - 1
    low = lax.ppermute(tail, flat, [(i, i + 1) for i in range(last)])
    high = lax.ppermute(head, flat, [(i + 1, i) for i in range(last)])

    def across(value, mask):
        return lax.ppermute(value, "row", [(i, i ^ mask) for i in range(rows)])

    def along(value, s):
        return lax.ppermute(value, "col", [(i, (i + s) % cols) for i in range(cols)])

    arrived = [messages[0]] + [across(messages[k], 2 * k) for k in range(1, masks)]
    pairs = [across(value, 1) for value in arrived]
    ordered = [value for both in zip(arrived, pairs) for value in both]
    points = [points[0]] + [along(points[s], s) for s in range(1, cols)]
    fe_out = fe_call(low, displacement, high, connectivity.T, element_basis, material)
    parts = slab_call(rows, cols, green, ordered, points)
    boundary = parts[0]
    for s in range(1, cols):
        boundary = boundary + along(parts[s], s)
    return fe_out, boundary


def solution(mesh):
    rows, cols = mesh.shape["row"], mesh.shape["col"]
    near = P(("row", "col"), None)
    placed = (near, near, P(), P(None, ("row", "col")), P(("col", "row"), None), P(None, "row", "col"), near, near, near, near)
    return jax.shard_map(
        functools.partial(shards, rows, cols),
        mesh=mesh,
        in_specs=placed,
        out_specs=(near, near),
        check_vma=False,
    )
```

time: 269 us -> 81.7 us (0.30)
  local copies, waits for them, and re-layouts: 124 us -> 4.74 us
  matrix products: 68.9 us -> 0 us
  waiting for transfers between devices: 0.03 us -> 28.2 us
  other arithmetic: 28.3 us -> 0.58 us
  Pallas kernels: 0 us -> 26.3 us
  between operations: 14.9 us -> 0.75 us
  blocking collectives: 12 us -> 0 us
  starting transfers between devices: 13.2 us -> 20.2 us
  loops' own time: 5.77 us -> 0 us
    dot_general x34 -> x0, matrix products: 68.9 us -> none  [the longest x8 20.9 us: element_forces(): jnp.einsum('mij,ejl->meil', basis, stacked, preferred_element_type=jnp.fl...]
    reshape x26 -> x0, local copies, waits for them, and re-layouts: 65.1 us -> none  [the longest x8 26.2 us: one_block(): forces = element_forces(values.reshape(block_size, 8, lanes), element_bas...]
    concatenate x9 -> x0, local copies, waits for them, and re-layouts: 35.3 us -> none  [the longest x8 35.2 us: element_forces(): return jnp.concatenate([real_y, imag_y], axis=2).reshape(count, 8, lanes)]
    ppermute x2 -> x15, waiting for transfers between devices: 0.01 us -> 28.2 us  [the longest x7 18.9 us: across(): return lax.ppermute(value, 'row', [(i, i ^ mask) for i in range(rows)])]
    pallas_call x0 -> x3, Pallas kernels: none -> 26.3 us  [the longest x1 15.8 us: fe_call(): pl.pallas_call(fe_kernel, out_shape=jax.ShapeDtypeStruct((nodes, 128), BF...]
    reduce_sum x8 -> x0, other arithmetic: 23.5 us -> none  [element_forces(): real_y = jnp.sum(real_c * real_z - imag_c * imag_z, axis=0)]
    ppermute x2 -> x15, starting transfers between devices: 6.21 us -> 20.2 us  [the longest x6 12.2 us: along(): lax.ppermute(value, 'col', [(i, (i + s) % cols) for i in range(cols)])]
    unnamed x1 -> x0, blocking collectives: 12 us -> none
  transfers between devices with their start and end apart: 4 -> 15, of which waited for: 0 -> 5; matrix products, arithmetic and copies ran while one was open for 82% -> 0% of each run, Pallas kernels for 0% -> 31%
where the time goes in v1:
time: 81.7 us; the launch traced here: 80.7 us
  waiting for transfers between devices  28.2 us (35%)
  Pallas kernels  26.3 us (32%)
  starting transfers between devices  20.2 us (25%)
  local copies, waits for them, and re-layouts  4.74 us (6%)
    ppermute x7, waiting for transfers between devices, across(): return lax.ppermute(value, 'row', [(i, i ^ mask) for i in range(rows)])  18.9 us
    pallas_call x1, Pallas kernels, fe_call(): pl.pallas_call(fe_kernel, out_shape=jax.ShapeDtypeStruct((nodes, 128), BF...  15.8 us
    ppermute x6, starting transfers between devices, along(): lax.ppermute(value, 'col', [(i, (i + s) % cols) for i in range(cols)])  12.2 us
    ppermute x6, waiting for transfers between devices, along(): lax.ppermute(value, 'col', [(i, (i + s) % cols) for i in range(cols)])  9.35 us
    pallas_call x1, Pallas kernels, slab_call(): pl.pallas_call(functools.partial(slab_kernel, rows, cols), out_shape=[par...  8.86 us
    ppermute x7, starting transfers between devices, across(): return lax.ppermute(value, 'row', [(i, i ^ mask) for i in range(rows)])  5.03 us
    unnamed x20, local copies, waits for them, and re-layouts  4.74 us
    ppermute x1, starting transfers between devices, shards(): low = lax.ppermute(tail, flat, [(i, i + 1) for i in range(last)])  1.68 us
  transfers between devices with their start and end apart: 15, of which 5 were waited for; matrix products, arithmetic and copies ran while one was open for 0% of the time, Pallas kernels for 31%

profile of v1, /device:TPU:0, one launch (start us, length us, event | category | flops | bytes accessed | tf_op | source)
XLA Modules:
  0.0 80.7 jit_solution(12894248373474139638)
XLA Ops:
  0.6 1.0 %copy-done = bf16[2048,128]{1,0:T(8,128)(2,1)S(1)} copy-done((bf16[2048,128]{1,0:T(8,128)(2,1)S(1)}, bf16[2048,128]{1,0:T(8,128)(2,1)}, u32[]{:S(2)}) %copy-start) | copy-done | bytes 524312
  1.7 1.0 %copy-done.2 = bf16[1536,128]{1,0:T(8,128)(2,1)S(1)} copy-done((bf16[1536,128]{1,0:T(8,128)(2,1)S(1)}, bf16[1536,128]{1,0:T(8,128)(2,1)}, u32[]{:S(2)}) %copy-start.2) | copy-done | bytes 393240
  2.7 0.7 copy-done.3
  3.4 0.7 copy-done.4
  4.0 0.7 copy-done.5
  4.7 0.7 copy-done.6
  5.4 1.6 %shard_map.113 = (bf16[32,6656]{1,0:T(8,128)(2,1)S(1)}, bf16[32,6656]{1,0:T(8,128)(2,1)S(1)}, bf16[32,6656]{1,0:T(8,128)(2,1)S(1)}, bf16[32,6656]{1,0:T(8,128)(2...) custom-call(bf16[1536,128]{1,0:T(8,128)(2,1)S(1)} %copy-done.2, ...), custom_call_target="tpu_custom_call" | custom-call | tf_op jit(solution)/shard_map/pallas_call | solution.py:175
  7.0 3.0 %collective-permute-start.3 = (bf16[32,6656]{1,0:T(8,128)(2,1)S(1)}, bf16[32,6656]{1,0:T(8,128)(2,1)S(1)}, u32[]{:S(2)}, u32[]{:S(2)}) collective-permute-start(bf16[32,6656]{1,0:T(8,128)(2,1)S(1)} %get-tuple-element.19), channel_id=1, source_target_pairs={{0,8},{4,12},{8,0},{12,4},{16,24},{20,28},{24,16},{28,20},{1,9},{5... | collective-permute-start | bytes 1277960 | tf_op jit(solution)/shard_map/ppermute | solution.py:258
  10.0 1.5 %collective-permute-start.5 = (bf16[32,6656]{1,0:T(8,128)(2,1)S(1)}, bf16[32,6656]{1,0:T(8,128)(2,1)S(1)}, u32[]{:S(2)}, u32[]{:S(2)}) collective-permute-start(bf16[32,6656]{1,0:T(8,128)(2,1)S(1)} %get-tuple-element.20), channel_id=1, source_target_pairs={{0,16},{4,20},{8,24},{12,28},{16,0},{20,4},{24,8},{28,12},{1,17},{... | collective-permute-start | bytes 1277960 | tf_op jit(solution)/shard_map/ppermute | solution.py:258
  11.5 9.1 %collective-permute-done.3.refs_2_ = bf16[32,6656]{1,0:T(8,128)(2,1)S(1)} collective-permute-done((bf16[32,6656]{1,0:T(8,128)(2,1)S(1)}, bf16[32,6656]{1,0:T(8,128)(2,1)S(1)}, u32[]{:S(2)}, u32[]{:S(2)}) %collective-permute-start.3) | collective-permute-done | bytes 426016 | tf_op jit(solution)/shard_map/ppermute | solution.py:258
  20.6 9.8 %collective-permute-done.5.refs_4_ = bf16[32,6656]{1,0:T(8,128)(2,1)S(1)} collective-permute-done((bf16[32,6656]{1,0:T(8,128)(2,1)S(1)}, bf16[32,6656]{1,0:T(8,128)(2,1)S(1)}, u32[]{:S(2)}, u32[]{:S(2)}) %collective-permute-start.5) | collective-permute-done | bytes 426016 | tf_op jit(solution)/shard_map/ppermute | solution.py:258
  30.9 1.6 %collective-permute-start.9 = (f32[8,128]{1,0:T(8,128)S(1)}, f32[8,128]{1,0:T(8,128)S(1)}, u32[]{:S(2)}, u32[]{:S(2)}) collective-permute-start(f32[8,128]{1,0:T(8,128)S(1)} %get-tuple-element.23), channel_id=1, source_target_pairs={{0,1},{1,2},{2,3},{3,0},{4,5},{5,6},{6,7},{7,4},{8,9},{9,10},{10,1... | collective-permute-start | bytes 12296 | tf_op jit(solution)/shard_map/ppermute | solution.py:261
  32.5 3.8 %collective-permute-done.9.refs_9_ = f32[8,128]{1,0:T(8,128)S(1)} collective-permute-done((f32[8,128]{1,0:T(8,128)S(1)}, f32[8,128]{1,0:T(8,128)S(1)}, u32[]{:S(2)}, u32[]{:S(2)}) %collective-permute-start.9) | collective-permute-done | bytes 4128 | tf_op jit(solution)/shard_map/ppermute | solution.py:261
  36.3 0.8 collective-permute-start.10
  37.1 3.7 %collective-permute-done.10.refs_10_ = f32[8,128]{1,0:T(8,128)S(1)} collective-permute-done((f32[8,128]{1,0:T(8,128)S(1)}, f32[8,128]{1,0:T(8,128)S(1)}, u32[]{:S(2)}, u32[]{:S(2)}) %collective-permute-start.10) | collective-permute-done | bytes 4128 | tf_op jit(solution)/shard_map/ppermute | solution.py:261
  40.8 1.8 %collective-permute-start.11 = (f32[8,128]{1,0:T(8,128)S(1)}, f32[8,128]{1,0:T(8,128)S(1)}, u32[]{:S(2)}, u32[]{:S(2)}) collective-permute-start(f32[8,128]{1,0:T(8,128)S(1)} %get-tuple-element.25), channel_id=1, source_target_pairs={{0,3},{1,0},{2,1},{3,2},{4,7},{5,4},{6,5},{7,6},{8,11},{9,8},{10,9... | collective-permute-start | bytes 12296 | tf_op jit(solution)/shard_map/ppermute | solution.py:261
  42.6 1.8 %collective-permute-done.11.refs_11_ = f32[8,128]{1,0:T(8,128)S(1)} collective-permute-done((f32[8,128]{1,0:T(8,128)S(1)}, f32[8,128]{1,0:T(8,128)S(1)}, u32[]{:S(2)}, u32[]{:S(2)}) %collective-permute-start.11) | collective-permute-done | bytes 4128 | tf_op jit(solution)/shard_map/ppermute | solution.py:261
  44.4 1.7 %collective-permute-start = (bf16[128,128]{1,0:T(8,128)(2,1)S(1)}, bf16[128,128]{1,0:T(8,128)(2,1)S(1)}, u32[]{:S(2)}, u32[]{:S(2)}) collective-permute-start(bf16[128,128]{1,0:T(8,128)(2,1)S(1)} %get-tuple-element.16), channel_id=1, source_target_pairs={{0,1},{1,2},{2,3},{3,4},{4,5},{5,6},{6,7},{7,8},{8,9},{9,10},{10,1... | collective-permute-start | bytes 98312 | tf_op jit(solution)/shard_map/ppermute | solution.py:254
  46.1 1.3 %collective-permute-start.1 = (bf16[128,128]{1,0:T(8,128)(2,1)S(1)}, bf16[128,128]{1,0:T(8,128)(2,1)S(1)}, u32[]{:S(2)}, u32[]{:S(2)}) collective-permute-start(bf16[128,128]{1,0:T(8,128)(2,1)S(1)} %get-tuple-element.17), channel_id=1, source_target_pairs={{1,0},{2,1},{3,2},{4,3},{5,4},{6,5},{7,6},{8,7},{9,8},{10,9},{11,1... | collective-permute-start | bytes 98312 | tf_op jit(solution)/shard_map/ppermute | solution.py:255
  47.5 8.9 %shard_map.115 = (f32[4,128]{1,0:T(4,128)S(1)}, f32[4,128]{1,0:T(4,128)S(1)}, f32[4,128]{1,0:T(4,128)S(1)}, f32[4,128]{1,0:T(4,128)S(1)}) custom-call(bf16[2,64,49152]{2,1,0:T(8,128)(2,1)} %green.1, bf16[32,6656]{1,0:T(8,128)(2,1)S(1)} %get-tuple-element.18.refs_0_, bf16[32,6656]{1,0:T(8,128)(2,1)S(1)} %collective-permute-done.2.refs_1_, ...), custom_call_target="tpu_custom_call" | custom-call | tf_op jit(solution)/shard_map/pallas_call | solution.py:232
  56.3 2.7 %collective-permute-start.12 = (f32[4,128]{1,0:T(4,128)S(1)}, f32[4,128]{1,0:T(4,128)S(1)}, u32[]{:S(2)}, u32[]{:S(2)}) collective-permute-start(f32[4,128]{1,0:T(4,128)S(1)} %get-tuple-element.27), channel_id=1, source_target_pairs={{0,1},{1,2},{2,3},{3,0},{4,5},{5,6},{6,7},{7,4},{8,9},{9,10},{10,1... | collective-permute-start | bytes 6152 | tf_op jit(solution)/shard_map/ppermute | solution.py:261
  59.0 4.4 %collective-permute-start.13 = (f32[4,128]{1,0:T(4,128)S(1)}, f32[4,128]{1,0:T(4,128)S(1)}, u32[]{:S(2)}, u32[]{:S(2)}) collective-permute-start(f32[4,128]{1,0:T(4,128)S(1)} %get-tuple-element.28), channel_id=1, source_target_pairs={{0,2},{1,3},{2,0},{3,1},{4,6},{5,7},{6,4},{7,5},{8,10},{9,11},{10,... | collective-permute-start | bytes 6152 | tf_op jit(solution)/shard_map/ppermute | solution.py:261
  63.4 0.9 %collective-permute-start.14 = (f32[4,128]{1,0:T(4,128)S(1)}, f32[4,128]{1,0:T(4,128)S(1)}, u32[]{:S(2)}, u32[]{:S(2)}) collective-permute-start(f32[4,128]{1,0:T(4,128)S(1)} %get-tuple-element.29), channel_id=1, source_target_pairs={{0,3},{1,0},{2,1},{3,2},{4,7},{5,4},{6,5},{7,6},{8,11},{9,8},{10,9... | collective-permute-start | bytes 6152 | tf_op jit(solution)/shard_map/ppermute | solution.py:261
  64.4 15.8 %shard_map.114 = bf16[2048,128]{1,0:T(8,128)(2,1)} custom-call(bf16[128,128]{1,0:T(8,128)(2,1)S(1)} %collective-permute-done.low, bf16[2048,128]{1,0:T(8,128)(2,1)S(1)} %copy-done.1, bf16[128,128]{1,0:T(8,128)(2,1)S(1)} %collective-permute-done.1.high, s32[8,2048]{1,0:T(8,128)S(1)} %bitcast.1, bf16[4,32,32]{2,1,0:T(8,128)(2,1)S(1)} %copy-done.9, ...), custom_call_target="tpu_custom_call" | custom-call | flops 16384000000 | bytes 2097152 | tf_op jit(solution)/shard_map/pallas_call | solution.py:97
  (30 shorter events, 1.2 us)
Async XLA Ops:
  0.6 1.0 %copy-start = (bf16[2048,128]{1,0:T(8,128)(2,1)S(1)}, bf16[2048,128]{1,0:T(8,128)(2,1)}, u32[]{:S(2)}) copy-start(bf16[2048,128]{1,0:T(8,128)(2,1)} %disp.3) | copy-start | bytes 1572868
  1.7 1.0 %copy-start.2 = (bf16[1536,128]{1,0:T(8,128)(2,1)S(1)}, bf16[1536,128]{1,0:T(8,128)(2,1)}, u32[]{:S(2)}) copy-start(bf16[1536,128]{1,0:T(8,128)(2,1)} %traction.1) | copy-start | bytes 1179652
  2.7 0.7 copy-start.3
  3.4 0.7 copy-start.4
  4.0 0.7 copy-start.5
  5.4 59.0 %copy-start.1 = (bf16[2048,128]{1,0:T(8,128)(2,1)S(1)}, bf16[2048,128]{1,0:T(8,128)(2,1)}, u32[]{:S(2)}) copy-start(bf16[2048,128]{1,0:T(8,128)(2,1)} %disp.3) | copy-start | bytes 1572868
  5.4 59.0 %copy-start.7 = (s32[2048,8]{0,1:T(8,128)S(1)}, s32[2048,8]{0,1:T(8,128)}, u32[]{:S(2)}) copy-start(s32[2048,8]{0,1:T(8,128)} %param.11) | copy-start | bytes 196612
  5.4 59.0 %copy-start.8 = (f32[8,2048]{1,0:T(8,128)S(1)}, f32[8,2048]{1,0:T(8,128)}, u32[]{:S(2)}) copy-start(f32[8,2048]{1,0:T(8,128)} %material.1) | copy-start | bytes 196612
  5.4 59.0 %copy-start.9 = (bf16[4,32,32]{2,1,0:T(8,128)(2,1)S(1)}, bf16[4,32,32]{2,1,0:T(8,128)(2,1)}, u32[]{:S(2)}) copy-start(bf16[4,32,32]{2,1,0:T(8,128)(2,1)} %basis.1) | copy-start | bytes 24580
  7.0 13.6 %collective-permute-start.3 = (bf16[32,6656]{1,0:T(8,128)(2,1)S(1)}, bf16[32,6656]{1,0:T(8,128)(2,1)S(1)}, u32[]{:S(2)}, u32[]{:S(2)}) collective-permute-start(bf16[32,6656]{1,0:T(8,128)(2,1)S(1)} %get-tuple-element.19), channel_id=1, source_target_pairs={{0,8},{4,12},{8,0},{12,4},{16,24},{20,28},{24,16},{28,20},{1,9},{5... | collective-permute-start | bytes 1277960 | tf_op jit(solution)/shard_map/ppermute | solution.py:258
  10.0 20.4 %collective-permute-start.5 = (bf16[32,6656]{1,0:T(8,128)(2,1)S(1)}, bf16[32,6656]{1,0:T(8,128)(2,1)S(1)}, u32[]{:S(2)}, u32[]{:S(2)}) collective-permute-start(bf16[32,6656]{1,0:T(8,128)(2,1)S(1)} %get-tuple-element.20), channel_id=1, source_target_pairs={{0,16},{4,20},{8,24},{12,28},{16,0},{20,4},{24,8},{28,12},{1,17},{... | collective-permute-start | bytes 1277960 | tf_op jit(solution)/shard_map/ppermute | solution.py:258
  11.5 18.9 %collective-permute-start.7 = (bf16[32,6656]{1,0:T(8,128)(2,1)S(1)}, bf16[32,6656]{1,0:T(8,128)(2,1)S(1)}, u32[]{:S(2)}, u32[]{:S(2)}) collective-permute-start(bf16[32,6656]{1,0:T(8,128)(2,1)S(1)} %get-tuple-element.21), channel_id=1, source_target_pairs={{0,24},{4,28},{8,16},{12,20},{16,8},{20,12},{24,0},{28,4},{1,25},{... | collective-permute-start | bytes 1277960 | tf_op jit(solution)/shard_map/ppermute | solution.py:258
  11.5 34.6 %collective-permute-start.2 = (bf16[32,6656]{1,0:T(8,128)(2,1)S(1)}, bf16[32,6656]{1,0:T(8,128)(2,1)S(1)}, u32[]{:S(2)}, u32[]{:S(2)}) collective-permute-start(bf16[32,6656]{1,0:T(8,128)(2,1)S(1)} %get-tuple-element.18.refs_0_), channel_id=1, source_target_pairs={{0,4},{4,0},{8,12},{12,8},{16,20},{20,16},{24,28},{28,24},{1,5},{5... | collective-permute-start | bytes 1277960 | tf_op jit(solution)/shard_map/ppermute | solution.py:258
  20.6 26.8 %collective-permute-start.4 = (bf16[32,6656]{1,0:T(8,128)(2,1)S(1)}, bf16[32,6656]{1,0:T(8,128)(2,1)S(1)}, u32[]{:S(2)}, u32[]{:S(2)}) collective-permute-start(bf16[32,6656]{1,0:T(8,128)(2,1)S(1)} %collective-permute-done.3.refs_2_), channel_id=1, source_target_pairs={{0,4},{4,0},{8,12},{12,8},{16,20},{20,16},{24,28},{28,24},{1,5},{5... | collective-permute-start | bytes 1277960 | tf_op jit(solution)/shard_map/ppermute | solution.py:258
  30.4 17.0 %collective-permute-start.6 = (bf16[32,6656]{1,0:T(8,128)(2,1)S(1)}, bf16[32,6656]{1,0:T(8,128)(2,1)S(1)}, u32[]{:S(2)}, u32[]{:S(2)}) collective-permute-start(bf16[32,6656]{1,0:T(8,128)(2,1)S(1)} %collective-permute-done.5.refs_4_), channel_id=1, source_target_pairs={{0,4},{4,0},{8,12},{12,8},{16,20},{20,16},{24,28},{28,24},{1,5},{5... | collective-permute-start | bytes 1277960 | tf_op jit(solution)/shard_map/ppermute | solution.py:258
  30.4 17.0 %collective-permute-start.8 = (bf16[32,6656]{1,0:T(8,128)(2,1)S(1)}, bf16[32,6656]{1,0:T(8,128)(2,1)S(1)}, u32[]{:S(2)}, u32[]{:S(2)}) collective-permute-start(bf16[32,6656]{1,0:T(8,128)(2,1)S(1)} %collective-permute-done.7.refs_6_), channel_id=1, source_target_pairs={{0,4},{4,0},{8,12},{12,8},{16,20},{20,16},{24,28},{28,24},{1,5},{5... | collective-permute-start | bytes 1277960 | tf_op jit(solution)/shard_map/ppermute | solution.py:258
  30.9 5.4 %collective-permute-start.9 = (f32[8,128]{1,0:T(8,128)S(1)}, f32[8,128]{1,0:T(8,128)S(1)}, u32[]{:S(2)}, u32[]{:S(2)}) collective-permute-start(f32[8,128]{1,0:T(8,128)S(1)} %get-tuple-element.23), channel_id=1, source_target_pairs={{0,1},{1,2},{2,3},{3,0},{4,5},{5,6},{6,7},{7,4},{8,9},{9,10},{10,1... | collective-permute-start | bytes 12296 | tf_op jit(solution)/shard_map/ppermute | solution.py:261
  36.3 4.5 %collective-permute-start.10 = (f32[8,128]{1,0:T(8,128)S(1)}, f32[8,128]{1,0:T(8,128)S(1)}, u32[]{:S(2)}, u32[]{:S(2)}) collective-permute-start(f32[8,128]{1,0:T(8,128)S(1)} %get-tuple-element.24), channel_id=1, source_target_pairs={{0,2},{1,3},{2,0},{3,1},{4,6},{5,7},{6,4},{7,5},{8,10},{9,11},{10,... | collective-permute-start | bytes 12296 | tf_op jit(solution)/shard_map/ppermute | solution.py:261
  40.8 3.6 %collective-permute-start.11 = (f32[8,128]{1,0:T(8,128)S(1)}, f32[8,128]{1,0:T(8,128)S(1)}, u32[]{:S(2)}, u32[]{:S(2)}) collective-permute-start(f32[8,128]{1,0:T(8,128)S(1)} %get-tuple-element.25), channel_id=1, source_target_pairs={{0,3},{1,0},{2,1},{3,2},{4,7},{5,4},{6,5},{7,6},{8,11},{9,8},{10,9... | collective-permute-start | bytes 12296 | tf_op jit(solution)/shard_map/ppermute | solution.py:261
  44.4 19.9 %collective-permute-start = (bf16[128,128]{1,0:T(8,128)(2,1)S(1)}, bf16[128,128]{1,0:T(8,128)(2,1)S(1)}, u32[]{:S(2)}, u32[]{:S(2)}) collective-permute-start(bf16[128,128]{1,0:T(8,128)(2,1)S(1)} %get-tuple-element.16), channel_id=1, source_target_pairs={{0,1},{1,2},{2,3},{3,4},{4,5},{5,6},{6,7},{7,8},{8,9},{9,10},{10,1... | collective-permute-start | bytes 98312 | tf_op jit(solution)/shard_map/ppermute | solution.py:254
  46.1 18.2 %collective-permute-start.1 = (bf16[128,128]{1,0:T(8,128)(2,1)S(1)}, bf16[128,128]{1,0:T(8,128)(2,1)S(1)}, u32[]{:S(2)}, u32[]{:S(2)}) collective-permute-start(bf16[128,128]{1,0:T(8,128)(2,1)S(1)} %get-tuple-element.17), channel_id=1, source_target_pairs={{1,0},{2,1},{3,2},{4,3},{5,4},{6,5},{7,6},{8,7},{9,8},{10,9},{11,1... | collective-permute-start | bytes 98312 | tf_op jit(solution)/shard_map/ppermute | solution.py:255
  56.3 23.8 %collective-permute-start.12 = (f32[4,128]{1,0:T(4,128)S(1)}, f32[4,128]{1,0:T(4,128)S(1)}, u32[]{:S(2)}, u32[]{:S(2)}) collective-permute-start(f32[4,128]{1,0:T(4,128)S(1)} %get-tuple-element.27), channel_id=1, source_target_pairs={{0,1},{1,2},{2,3},{3,0},{4,5},{5,6},{6,7},{7,4},{8,9},{9,10},{10,1... | collective-permute-start | bytes 6152 | tf_op jit(solution)/shard_map/ppermute | solution.py:261
  59.0 21.1 %collective-permute-start.13 = (f32[4,128]{1,0:T(4,128)S(1)}, f32[4,128]{1,0:T(4,128)S(1)}, u32[]{:S(2)}, u32[]{:S(2)}) collective-permute-start(f32[4,128]{1,0:T(4,128)S(1)} %get-tuple-element.28), channel_id=1, source_target_pairs={{0,2},{1,3},{2,0},{3,1},{4,6},{5,7},{6,4},{7,5},{8,10},{9,11},{10,... | collective-permute-start | bytes 6152 | tf_op jit(solution)/shard_map/ppermute | solution.py:261
  63.4 16.7 %collective-permute-start.14 = (f32[4,128]{1,0:T(4,128)S(1)}, f32[4,128]{1,0:T(4,128)S(1)}, u32[]{:S(2)}, u32[]{:S(2)}) collective-permute-start(f32[4,128]{1,0:T(4,128)S(1)} %get-tuple-element.29), channel_id=1, source_target_pairs={{0,3},{1,0},{2,1},{3,2},{4,7},{5,4},{6,5},{7,6},{8,11},{9,8},{10,9... | collective-permute-start | bytes 6152 | tf_op jit(solution)/shard_map/ppermute | solution.py:261
  (1 other events, 0.7 us)

commit v2 on v1

v2 whole, which is shorter than its diff:
```python
import functools

import jax
import jax.numpy as jnp
from jax import lax
from jax.experimental import pallas as pl
from jax.experimental.pallas import tpu as pltpu
from jax.sharding import PartitionSpec as P

PTS = 4
COST = 10**8
SLOT = 16
HALO = 128
EB = 256
WIN = EB + 2 * HALO
NT = (((1,), (1,)), ((), ()))
F32 = jnp.float32
BF16 = jnp.bfloat16
VMEM = pl.BlockSpec(memory_space=pltpu.VMEM)
HBM = pl.BlockSpec(memory_space=pltpu.HBM)


def iota(shape, axis):
    return lax.broadcasted_iota(jnp.int32, shape, axis)


def spread_basis(basis, wcat):
    spread = (iota((256, 32), 0) // 8 == iota((256, 32), 1)).astype(BF16)
    same = iota((256, 256), 0) % 8 == iota((256, 256), 1) % 8
    for m in range(4):
        tall = jnp.dot(spread, basis[m], preferred_element_type=F32).astype(BF16)
        wide = lax.dot_general(tall, spread, NT, preferred_element_type=F32)
        wcat[:, m * 256 : (m + 1) * 256] = jnp.where(same, wide, 0.0).astype(BF16)


def node_gaps():
    gap = iota((WIN, EB), 0) - iota((WIN, EB), 1)
    return jnp.where((gap >= 0) & (gap <= 2 * HALO), gap, -1).astype(F32).astype(BF16)


def flip(rows):
    return rows.astype(F32).T.astype(BF16)


def upright(tile):
    rows = [tile[(g * 4 + d) * 8 : (g * 4 + d) * 8 + 8, :] for d in range(4) for g in range(4)]
    return jnp.concatenate(rows, axis=0).T.astype(BF16)


def element_block(at, window, links, material, wcat, dist, sel, vs, us, fs):
    offsets = (links[:, pl.ds(at, EB)] - (at + iota((8, EB), 1))).astype(F32).astype(BF16)
    for n in range(8):
        hit = dist[...] == offsets[n : n + 1, :]
        chosen = jnp.where(hit, jnp.ones((), BF16), jnp.zeros((), BF16))
        sel[:, n * EB : (n + 1) * EB] = chosen
        v = jnp.dot(window, chosen, preferred_element_type=F32)
        for g in range(4):
            part = jnp.concatenate([v[d * 32 + g * 8 : d * 32 + g * 8 + 8, :] for d in range(4)], axis=0)
            vs[g, n * 32 : (n + 1) * 32, :] = part.astype(BF16)
    coeffs = material[:, pl.ds(at, EB)]
    for h in range(2):
        for n in range(8):
            rows = slice(n * 32, (n + 1) * 32)
            re = vs[h, rows, :].astype(F32)
            im = vs[2 + h, rows, :].astype(F32)
            for m in range(4):
                cr = coeffs[2 * m : 2 * m + 1, :]
                ci = coeffs[2 * m + 1 : 2 * m + 2, :]
                up = slice(m * 256 + n * 32, m * 256 + (n + 1) * 32)
                us[h, 0, up, :] = (cr * re - ci * im).astype(BF16)
                us[h, 1, up, :] = (cr * im + ci * re).astype(BF16)
        for p in range(2):
            f = jnp.dot(wcat[...], us[h, p], preferred_element_type=F32)
            g = 2 * p + h
            for n in range(8):
                fs[g * 32 : (g + 1) * 32, n * EB : (n + 1) * EB] = f[n * 32 : (n + 1) * 32, :].astype(BF16)
    return lax.dot_general(fs[...], sel[...], NT, preferred_element_type=F32)


def inner_kernel(disp, links, basis, material, green, acc, wcat, dist, held, out, xt, sel, vs, us, fs, sems):
    nodes = disp.shape[0]
    pieces = held.shape[0]
    row = lax.axis_index("row")
    copies = []
    for k in range(pieces):
        start = pl.multiple_of((row ^ k) * held.shape[3], 128)
        copy = pltpu.make_async_copy(green.at[:, :, pl.ds(start, held.shape[3])], held.at[k], sems.at[k])
        copy.start()
        copies.append(copy)
    for i in range(nodes // 128):
        xt[:, HALO + i * 128 : HALO + (i + 1) * 128] = flip(disp[i * 128 : (i + 1) * 128, :])
    spread_basis(basis, wcat)
    dist[...] = node_gaps()
    acc[...] = jnp.zeros_like(acc)

    def block(b, k):
        at = pl.multiple_of(b * EB, EB)
        acc[:, pl.ds(at, WIN)] += element_block(
            at, xt[:, pl.ds(at, WIN)], links, material, wcat, dist, sel.at[k], vs.at[k], us.at[k], fs.at[k]
        )

    def step(i, carry):
        block(2 * i + 1, 0)
        block(2 * i + 2, 1)
        return carry

    lax.fori_loop(0, (nodes // EB - 2) // 2, step, 0)
    for i in range((WIN - HALO) // 128, (nodes - WIN + HALO) // 128):
        out[i * 128 : (i + 1) * 128, :] = upright(acc[:, HALO + i * 128 : HALO + (i + 1) * 128])
    for copy in copies:
        copy.wait()


def outer_kernel(before, near, disp, edge, links, material, acc, wcat, dist, out, sel, vs, us, fs, done, sems):
    nodes = disp.shape[0]
    keep = WIN - HALO
    even = lax.axis_index("col") % 2 == 0
    low = jnp.where(even, edge[...], near[:HALO, :])
    high = jnp.where(even, near[:HALO, :], edge[...])
    copies = []
    for e in range(2):
        first = (nodes - keep) * e
        rows = [disp[first + i * 128 : first + (i + 1) * 128, :] for i in range(keep // 128)]
        rows = rows + [high] if e else [low] + rows
        window = jnp.concatenate([flip(tile) for tile in rows], axis=1)
        at = (nodes - EB) * e
        total = acc[:, at : at + WIN] + element_block(
            at, window, links, material, wcat, dist, sel.at[e], vs.at[e], us.at[e], fs.at[e]
        )
        for i in range(keep // 128):
            start = i * 128 if e else HALO + i * 128
            done[e, i * 128 : (i + 1) * 128, :] = upright(total[:, start : start + 128])
        copy = pltpu.make_async_copy(done.at[e], out.at[pl.ds(first, keep), :], sems.at[e])
        copy.start()
        copies.append(copy)
    for copy in copies:
        copy.wait()


def block_scratch():
    return [
        pltpu.VMEM((2, WIN, 8 * EB), BF16),
        pltpu.VMEM((2, 4, 256, EB), BF16),
        pltpu.VMEM((2, 2, 2, 1024, EB), BF16),
        pltpu.VMEM((2, 128, 8 * EB), BF16),
    ]


def element_params(blocks):
    return dict(
        compiler_params=pltpu.CompilerParams(vmem_limit_bytes=16 * 2**20),
        cost_estimate=pl.CostEstimate(flops=blocks * COST, bytes_accessed=2**20, transcendentals=0),
    )


def inner_call(rows, disp, links, basis, material, green):
    nodes = disp.shape[0]
    return pl.pallas_call(
        inner_kernel,
        out_shape=[
            jax.ShapeDtypeStruct((128, nodes + 2 * HALO), F32),
            jax.ShapeDtypeStruct((256, 1024), BF16),
            jax.ShapeDtypeStruct((WIN, EB), BF16),
            jax.ShapeDtypeStruct((rows, 2, green.shape[1], green.shape[2] // rows), BF16),
            jax.ShapeDtypeStruct((nodes, 128), BF16),
        ],
        in_specs=[VMEM] * 4 + [HBM],
        out_specs=[VMEM] * 5,
        scratch_shapes=[pltpu.VMEM((128, nodes + 2 * HALO), BF16)]
        + block_scratch()
        + [pltpu.SemaphoreType.DMA((rows,))],
        **element_params(nodes // EB - 2),
    )(disp, links, basis, material, green)


def outer_call(before, near, disp, edge, links, material, acc, wcat, dist):
    return pl.pallas_call(
        outer_kernel,
        out_shape=jax.ShapeDtypeStruct(before.shape, BF16),
        in_specs=[HBM] + [VMEM] * 8,
        out_specs=HBM,
        scratch_shapes=block_scratch()
        + [pltpu.VMEM((2, WIN - HALO, 128), BF16), pltpu.SemaphoreType.DMA((2,))],
        input_output_aliases={0: 0},
        **element_params(2),
    )(before, near, disp, edge, links, material, acc, wcat, dist)


def prepare_kernel(rows, cols, *refs):
    masks = rows // 2
    sources = refs[:9]
    messages = refs[9 : 9 + masks]
    near, edge, points, disp, links, basis, material, slots, traction, node, weight, count, recv, sems = refs[9 + masks :]
    lines = traction.shape[0]
    row, col = lax.axis_index("row"), lax.axis_index("col")
    pieces = 3 if lines // 128 % 3 == 0 else 1
    share = lines // pieces
    copies = [
        pltpu.make_async_copy(
            sources[0].at[pl.ds(i * share, share), :], traction.at[pl.ds(i * share, share), :], sems.at[8 + i]
        )
        for i in range(pieces)
    ]
    others = [
        pltpu.make_async_copy(sources[i + 1], target, sems.at[i])
        for i, target in enumerate((disp, node, weight, count, recv, links, basis, material))
    ]
    for copy in copies + others:
        copy.start()

    widen = (iota((128, 512), 1) // 4 == iota((128, 512), 0)).astype(BF16)
    comp = iota((32, 512), 1) % 4
    for i in range(lines // 128):
        if i * 128 % share == 0:
            copies[i * 128 // share].wait()
        wide = jnp.dot(flip(traction[i * 128 : (i + 1) * 128, :]), widen, preferred_element_type=F32)
        line = wide[:32]
        for k in range(1, 4):
            line = jnp.where(comp == k, wide[k * 32 : (k + 1) * 32], line)
        line = line.astype(BF16)
        for message in messages:
            message[:, i * 512 : (i + 1) * 512] = line

    for copy in others:
        copy.wait()
    tail, head = disp[disp.shape[0] - HALO :, :], disp[:HALO, :]
    even = col % 2 == 0
    near[:HALO, :] = jnp.where(even, tail, head)
    edge[...] = jnp.where(even, head, tail)
    total = node.shape[1]
    devices = count.shape[1]
    copies = (iota((devices, total), 1) // SLOT == iota((devices, total), 0)).astype(BF16)
    counts = jnp.broadcast_to(count[...].astype(F32), (8, devices)).astype(BF16)
    live = jnp.dot(counts, copies, preferred_element_type=F32)
    scale = jnp.where((iota((8, total), 1) % SLOT).astype(F32) < live, weight[...], 0.0)
    columns = jnp.where(iota((8, total), 0) == 0, node[...].astype(F32), scale).T
    for i in range(total // 256):
        chunk = columns[i * 256 : (i + 1) * 256]
        hit = chunk[:, 0:1] == iota((256, disp.shape[0]), 1).astype(F32)
        picked = jnp.dot(jnp.where(hit, 1.0, 0.0).astype(BF16), disp[...], preferred_element_type=F32)
        slots[i * 256 : (i + 1) * 256, :] = (picked * chunk[:, 1:2]).astype(BF16)

    each = cols * SLOT
    for k in range(masks):
        message, lane = messages[k], lines * 4
        for core in range(2):
            target = (row // 2 ^ k) * 2 + core
            for t in range(each // 32):
                start = pl.multiple_of(target * each + t * 32, 32)
                message[:, lane : lane + 128] = slots[pl.ds(start, 32), :]
                lane += 128

    for t in range(total // 128):
        feeds = recv[:, t * 128 : (t + 1) * 128].astype(F32)
        feeds = jnp.broadcast_to(feeds, (16, 128)).astype(BF16)
        points[t * 16 : (t + 1) * 16, :] = feeds
        near[HALO + t * 16 : HALO + (t + 1) * 16, :] = feeds


def prepare_call(rows, cols, traction, disp, node, weight, count, recv, links, basis, material):
    masks = rows // 2
    message = jax.ShapeDtypeStruct((32, traction.shape[0] * 4 + cols * SLOT * 8), BF16)
    near = jax.ShapeDtypeStruct((HALO + node.shape[1] // 8, 128), BF16)
    edge = jax.ShapeDtypeStruct((HALO, 128), BF16)
    points = jax.ShapeDtypeStruct((node.shape[1] // 8, 128), BF16)
    same = [jax.ShapeDtypeStruct(value.shape, value.dtype) for value in (disp, links, basis, material)]
    return pl.pallas_call(
        functools.partial(prepare_kernel, rows, cols),
        out_shape=[message] * masks + [near, edge, points] + same,
        in_specs=[HBM] * 9,
        out_specs=[VMEM] * (masks + 7),
        scratch_shapes=[pltpu.VMEM((node.shape[1], 128), BF16)]
        + [pltpu.VMEM(value.shape, value.dtype) for value in (traction, node, weight, count, recv)]
        + [pltpu.SemaphoreType.DMA((11,))],
        compiler_params=pltpu.CompilerParams(vmem_limit_bytes=24 * 2**20),
    )(traction, disp, node, weight, count, recv, links, basis, material)


def slab_sum(high, pieces, green, messages, start):
    both = start
    length = green.shape[3]
    for k, message in zip(pieces, messages):
        flat = green[k].reshape(2 * high, length)
        both = both + lax.dot_general(flat, message[:, :length], NT, preferred_element_type=F32)
    return both


def early_kernel(pieces, green, *refs):
    high = green.shape[2]
    refs[-1][...] = slab_sum(high, pieces, green, refs[:-1], jnp.zeros((2 * high, 32), F32))


def early_call(pieces, green, messages):
    return pl.pallas_call(
        functools.partial(early_kernel, pieces),
        out_shape=jax.ShapeDtypeStruct((2 * green.shape[2], 32), F32),
        in_specs=[VMEM] * (1 + len(messages)),
        out_specs=VMEM,
        compiler_params=pltpu.CompilerParams(vmem_limit_bytes=8 * 2**20),
        cost_estimate=pl.CostEstimate(flops=COST, bytes_accessed=2**20, transcendentals=0),
    )(green, *messages)


def late_kernel(rows, cols, pieces, green, before, *refs):
    messages, points = refs[:rows], refs[rows : -cols - 3]
    outs = refs[-cols - 3 : -3]
    sent, traced, total = refs[-3:]
    row, col = lax.axis_index("row"), lax.axis_index("col")
    high = green.shape[2]
    each = cols * SLOT
    for k in range(rows):
        into = pl.multiple_of((row ^ k) * SLOT, SLOT)
        for t in range(each // 32):
            at = pl.multiple_of(green.shape[3] + (row % 2 * (each // 32) + t) * 128, 128)
            pair = messages[k][:, pl.ds(at, 128)]
            sent[2 * t, pl.ds(into, SLOT), :] = pair[:SLOT]
            sent[2 * t + 1, pl.ds(into, SLOT), :] = pair[SLOT:]
    width = rows * SLOT
    length = width * cols
    source, place = iota((length, width), 0), iota((length, width), 1)
    take = (source == (place // SLOT * cols + col) * SLOT + place % SLOT).astype(BF16)
    tall = length // 8
    owners = [block[i * tall : (i + 1) * tall, :] for block in points for i in range(block.shape[0] // tall)]
    for s in range(cols):
        values = jnp.concatenate([owners[s][t * 16 : (t + 1) * 16, :] for t in range(length // 128)], axis=1)
        mine = jnp.dot(values, take, preferred_element_type=F32)[:8]
        hot = (mine == iota(mine.shape, 0).astype(F32)).astype(BF16)
        traced[col ^ s] = jnp.dot(hot, sent[col ^ s], preferred_element_type=F32)

    both = slab_sum(high, pieces, green, [messages[k] for k in pieces], before[...])
    real = both[:high, :16] - both[high:, 16:]
    imag = both[:high, 16:] + both[high:, :16]
    total[...] = jnp.concatenate([real, imag, jnp.zeros((high, 96), F32)], axis=1)
    for c in range(cols):
        parts = [total[pl.ds(c * PTS * 4 + k, PTS, stride=4), :][:, :32] for k in range(4)]
        traced[c, :PTS, :] = traced[c, :PTS, :] - jnp.concatenate(parts, axis=1)
    for s in range(cols):
        outs[s][...] = traced[col ^ s, :PTS, :]


def late_call(rows, cols, pieces, green, before, messages, points):
    return pl.pallas_call(
        functools.partial(late_kernel, rows, cols, pieces),
        out_shape=[jax.ShapeDtypeStruct((PTS, 128), F32)] * cols,
        in_specs=[VMEM] * (2 + rows + len(points)),
        out_specs=[VMEM] * cols,
        scratch_shapes=[
            pltpu.VMEM((cols, rows * SLOT, 128), BF16),
            pltpu.VMEM((cols, 8, 128), F32),
            pltpu.VMEM((green.shape[2], 128), F32),
        ],
        compiler_params=pltpu.CompilerParams(vmem_limit_bytes=8 * 2**20),
        cost_estimate=pl.CostEstimate(flops=COST, bytes_accessed=2**20, transcendentals=0),
    )(green, before, *messages, *points)


def shards(rows, cols, displacement, connectivity, element_basis, material, traction, green, node, weight, count, recv):
    masks = rows // 2
    given = (traction, displacement, node, weight, count, recv, connectivity.T, element_basis, material, green)
    *given, green = [pltpu.with_memory_space_constraint(value, pltpu.HBM) for value in given]
    made = prepare_call(rows, cols, *given)
    messages, (near, edge, points, disp, links, basis, coeffs) = made[:masks], made[masks:]
    flat = ("row", "col")
    last = rows * cols - 1

    def across(value, mask):
        return lax.ppermute(value, "row", [(i, i ^ mask) for i in range(rows)])

    def along(value, s):
        return lax.ppermute(value, "col", [(i, i ^ s) for i in range(cols)])

    chips = [across(messages[k], 2 * k) for k in range(1, masks)]
    near = along(near, 1)
    steps = [(i, i + 1) for i in range(1, last, 2)]
    edge = lax.ppermute(edge, flat, steps + [(b, a) for a, b in steps])
    inner = inner_call(rows, disp, links, basis, coeffs, green)
    own, near, edge, points, inner = lax.optimization_barrier((messages[0], near, edge, points, inner))
    acc, wcat, dist, held, before = inner
    known = [jnp.concatenate([points, near[HALO:]], axis=0)]
    while len(known) < cols // 2:
        known += [along(value, 2 * len(known)) for value in known]
    fe_out = outer_call(before, near, disp, edge, links, coeffs, acc, wcat, dist)
    chips, fe_out, known = lax.optimization_barrier((chips, fe_out, known))
    pair = across(own, 1)
    early = early_call((0,), held, (own,))
    ordered = [own, pair]
    for value in chips:
        ordered += [value, across(value, 1)]
    parts = late_call(rows, cols, tuple(range(1, rows)), held, early, ordered, known)
    boundary = parts[0]
    for value in [along(parts[s], s) for s in range(1, cols)]:
        boundary = boundary + value
    return fe_out, boundary


def solution(mesh):
    rows, cols = mesh.shape["row"], mesh.shape["col"]
    near = P(("row", "col"), None)
    placed = (near, near, P(), P(None, ("row", "col")), P(("col", "row"), None), P(None, "row", "col"), near, near, near, near)
    return jax.shard_map(
        functools.partial(shards, rows, cols),
        mesh=mesh,
        in_specs=placed,
        out_specs=(near, near),
        check_vma=False,
    )
```

time: 81.7 us -> 48.5 us (0.59); the launches traced: 80.7 us -> 48.4 us
  waiting for transfers between devices: 28.2 us -> 6.09 us
  local copies, waits for them, and re-layouts: 4.74 us -> 0.01 us
  starting transfers between devices: 20.2 us -> 17 us
  Pallas kernels: 26.3 us -> 23.9 us
    ppermute x7, waiting for transfers between devices: 18.9 us -> 1.85 us  [across(): return lax.ppermute(value, 'row', [(i, i ^ mask) for i in range(rows)])]
    ppermute x8 -> x6, waiting for transfers between devices: 9.36 us -> 4.24 us  [the longest x5 4.23 us: along(): return lax.ppermute(value, 'col', [(i, i ^ s) for i in range(cols)])]
    unnamed x20 -> x0, local copies, waits for them, and re-layouts: 4.74 us -> none
    ppermute x8 -> x6, starting transfers between devices: 15.1 us -> 11.1 us  [the longest x5 10.5 us: along(): return lax.ppermute(value, 'col', [(i, i ^ s) for i in range(cols)])]
    pallas_call x2 -> x4, Pallas kernels: 24.6 us -> 20.8 us  [the longest x1 12.3 us: inner_call(): pl.pallas_call(inner_kernel, out_shape=[jax.ShapeDtypeStruct((128, nodes...]
    pallas_call x1, Pallas kernels: 1.63 us -> 3.13 us  [prepare_call(): pl.pallas_call(functools.partial(prepare_kernel, rows, cols), out_shape=[...]
    ppermute x7, starting transfers between devices: 5.03 us -> 5.89 us  [across(): return lax.ppermute(value, 'row', [(i, i ^ mask) for i in range(rows)])]
  transfers between devices with their start and end apart: 15 -> 13, of which waited for: 5 -> 5; matrix products, arithmetic and copies ran while one was open for 0% -> 0% of each run, Pallas kernels for 31% -> 35%
where the time goes in v2:
time: 48.5 us; the launch traced here: 48.4 us
  Pallas kernels  23.9 us (49%)
  starting transfers between devices  17 us (35%)
  waiting for transfers between devices  6.09 us (13%)
  between operations  0.77 us (2%)
  other arithmetic  0.59 us (1%)
    pallas_call x1, Pallas kernels, inner_call(): pl.pallas_call(inner_kernel, out_shape=[jax.ShapeDtypeStruct((128, nodes...  12.3 us
    ppermute x5, starting transfers between devices, along(): return lax.ppermute(value, 'col', [(i, i ^ s) for i in range(cols)])  10.5 us
    ppermute x7, starting transfers between devices, across(): return lax.ppermute(value, 'row', [(i, i ^ mask) for i in range(rows)])  5.89 us
    pallas_call x1, Pallas kernels, outer_call(): pl.pallas_call(outer_kernel, out_shape=jax.ShapeDtypeStruct(before.shape,...  4.28 us
    ppermute x5, waiting for transfers between devices, along(): return lax.ppermute(value, 'col', [(i, i ^ s) for i in range(cols)])  4.23 us
    pallas_call x1, Pallas kernels, late_call(): pl.pallas_call(functools.partial(late_kernel, rows, cols, pieces), out_sh...  3.65 us
    pallas_call x1, Pallas kernels, prepare_call(): pl.pallas_call(functools.partial(prepare_kernel, rows, cols), out_shape=[...  3.13 us
    ppermute x7, waiting for transfers between devices, across(): return lax.ppermute(value, 'row', [(i, i ^ mask) for i in range(rows)])  1.85 us
  transfers between devices with their start and end apart: 13, of which 5 were waited for; matrix products, arithmetic and copies ran while one was open for 0% of the time, Pallas kernels for 35%

profile of v2, /device:TPU:0, one launch (start us, length us, event | category | flops | bytes accessed | tf_op | source)
XLA Modules:
  0.0 48.4 jit_solution(15619070994553769432)
XLA Ops:
  0.6 3.1 %shard_map.113 = (bf16[32,6656]{1,0:T(8,128)(2,1)S(1)}, bf16[32,6656]{1,0:T(8,128)(2,1)S(1)}, bf16[32,6656]{1,0:T(8,128)(2,1)S(1)}, bf16[32,6656]{1,0:T(8,128)(2...) custom-call(bf16[1536,128]{1,0:T(8,128)(2,1)} %refs_0_.1, ...), custom_call_target="tpu_custom_call" | custom-call | tf_op jit(solution)/shard_map/pallas_call | solution.py:267
  3.8 3.0 %collective-permute-start = (bf16[32,6656]{1,0:T(8,128)(2,1)S(1)}, bf16[32,6656]{1,0:T(8,128)(2,1)S(1)}, u32[]{:S(2)}, u32[]{:S(2)}) collective-permute-start(bf16[32,6656]{1,0:T(8,128)(2,1)S(1)} %get-tuple-element.37), channel_id=1, source_target_pairs={{0,8},{4,12},{8,0},{12,4},{16,24},{20,28},{24,16},{28,20},{1,9},{5... | collective-permute-start | bytes 1277960 | tf_op jit(solution)/shard_map/ppermute | solution.py:367
  6.8 1.5 %collective-permute-start.1 = (bf16[32,6656]{1,0:T(8,128)(2,1)S(1)}, bf16[32,6656]{1,0:T(8,128)(2,1)S(1)}, u32[]{:S(2)}, u32[]{:S(2)}) collective-permute-start(bf16[32,6656]{1,0:T(8,128)(2,1)S(1)} %get-tuple-element.38), channel_id=1, source_target_pairs={{0,16},{4,20},{8,24},{12,28},{16,0},{20,4},{24,8},{28,12},{1,17},{... | collective-permute-start | bytes 1277960 | tf_op jit(solution)/shard_map/ppermute | solution.py:367
  8.3 0.0 collective-permute-start.2
  8.3 0.7 %collective-permute-start.4 = (bf16[128,128]{1,0:T(8,128)(2,1)S(1)}, bf16[128,128]{1,0:T(8,128)(2,1)S(1)}, u32[]{:S(2)}, u32[]{:S(2)}) collective-permute-start(bf16[128,128]{1,0:T(8,128)(2,1)S(1)} %get-tuple-element.42), channel_id=1, source_target_pairs={{1,2},{3,4},{5,6},{7,8},{9,10},{11,12},{13,14},{15,16},{17,18},{19... | collective-permute-start | bytes 98312 | tf_op jit(solution)/shard_map/ppermute | solution.py:375
  9.0 4.9 %collective-permute-start.3 = (bf16[192,128]{1,0:T(8,128)(2,1)S(1)}, bf16[192,128]{1,0:T(8,128)(2,1)S(1)}, u32[]{:S(2)}, u32[]{:S(2)}) collective-permute-start(bf16[192,128]{1,0:T(8,128)(2,1)S(1)} %get-tuple-element.41), channel_id=1, source_target_pairs={{0,1},{1,0},{2,3},{3,2},{4,5},{5,4},{6,7},{7,6},{8,9},{9,8},{10,11... | collective-permute-start | bytes 147464 | tf_op jit(solution)/shard_map/ppermute | solution.py:370
  13.9 12.3 %shard_map.114 = (f32[128,2304]{1,0:T(8,128)S(1)}, bf16[256,1024]{1,0:T(8,128)(2,1)S(1)}, bf16[512,256]{1,0:T(8,128)(2,1)S(1)}, bf16[8,2,64,6144]{3,2,1,0:T(8,128)(2,1)S(1)}, bf16[2048,128]{1,0:T(8,128)(2,1)}) custom-call(bf16[2048,128]{1,0:T(8,128)(2,1)S(1)} %get-tuple-element.44.disp, s32[8,2048]{1,0:T(8,128)S(1)} %get-tuple-element.45.links, ...), custom_call_target="tpu_custom_call" | custom-call | flops 600000000 | bytes 1048576 | tf_op jit(solution)/shard_map/pallas_call | solution.py:158
  26.3 1.1 %collective-permute-start.5 = (bf16[128,128]{1,0:T(8,128)(2,1)S(1)}, bf16[128,128]{1,0:T(8,128)(2,1)S(1)}, u32[]{:S(2)}, u32[]{:S(2)}) collective-permute-start(bf16[128,128]{1,0:T(8,128)(2,1)S(1)} %pad_maximum_fusion.refs_8_), channel_id=1, source_target_pairs={{0,2},{1,3},{2,0},{3,1},{4,6},{5,7},{6,4},{7,5},{8,10},{9,11},{10,... | collective-permute-start | bytes 98312 | tf_op jit(solution)/shard_map/ppermute | solution.py:370
  27.3 0.7 %collective-permute-start.6 = (bf16[32,6656]{1,0:T(8,128)(2,1)S(1)}, bf16[32,6656]{1,0:T(8,128)(2,1)S(1)}, u32[]{:S(2)}, u32[]{:S(2)}) collective-permute-start(bf16[32,6656]{1,0:T(8,128)(2,1)S(1)} %get-tuple-element.62.refs_0_), channel_id=1, source_target_pairs={{0,4},{4,0},{8,12},{12,8},{16,20},{20,16},{24,28},{28,24},{1,5},{5... | collective-permute-start | bytes 1277960 | tf_op jit(solution)/shard_map/ppermute | solution.py:367
  28.0 4.3 %shard_map.115 = bf16[2048,128]{1,0:T(8,128)(2,1)} custom-call(bf16[2048,128]{1,0:T(8,128)(2,1)} %get-tuple-element.53.before, bf16[192,128]{1,0:T(8,128)(2,1)S(1)} %collective-permute-done.3.near, bf16[2048,128]{1,0:T(8,128)(2,1)S(1)} %get-tuple-element.44.disp, bf16[128,128]{1,0:T(8,128)(2,1)S(1)} %collective-permute-done.4.edge, ...), custom_call_target="tpu_custom_call", output_to_operand_aliasing={{}: (0, {})} | custom-call | flops 200000000 | bytes 1048576 | tf_op jit(solution)/shard_map/pallas_call | solution.py:177
  32.4 0.1 collective-permute-start.7
  32.5 0.5 %collective-permute-start.8 = (bf16[32,6656]{1,0:T(8,128)(2,1)S(1)}, bf16[32,6656]{1,0:T(8,128)(2,1)S(1)}, u32[]{:S(2)}, u32[]{:S(2)}) collective-permute-start(bf16[32,6656]{1,0:T(8,128)(2,1)S(1)} %collective-permute-done.1.refs_4_), channel_id=1, source_target_pairs={{0,4},{4,0},{8,12},{12,8},{16,20},{20,16},{24,28},{28,24},{1,5},{5... | collective-permute-start | bytes 1277960 | tf_op jit(solution)/shard_map/ppermute | solution.py:367
  33.0 0.1 collective-permute-start.9
  33.0 0.5 %shard_map.116.before = f32[128,32]{1,0:T(8,128)S(1)} custom-call(bf16[8,2,64,6144]{3,2,1,0:T(8,128)(2,1)S(1)} %get-tuple-element.61.green, bf16[32,6656]{1,0:T(8,128)(2,1)S(1)} %get-tuple-element.62.refs_0_), custom_call_target="tpu_custom_call" | custom-call | flops 100000000 | bytes 1048576 | tf_op jit(solution)/shard_map/pallas_call | solution.py:294
  33.6 0.6 %collective-permute-done.7.refs_3_ = bf16[32,6656]{1,0:T(8,128)(2,1)S(1)} collective-permute-done((bf16[32,6656]{1,0:T(8,128)(2,1)S(1)}, bf16[32,6656]{1,0:T(8,128)(2,1)S(1)}, u32[]{:S(2)}, u32[]{:S(2)}) %collective-permute-start.7) | collective-permute-done | bytes 426016 | tf_op jit(solution)/shard_map/ppermute | solution.py:367
  34.2 0.6 %collective-permute-done.8.refs_5_ = bf16[32,6656]{1,0:T(8,128)(2,1)S(1)} collective-permute-done((bf16[32,6656]{1,0:T(8,128)(2,1)S(1)}, bf16[32,6656]{1,0:T(8,128)(2,1)S(1)}, u32[]{:S(2)}, u32[]{:S(2)}) %collective-permute-start.8) | collective-permute-done | bytes 426016 | tf_op jit(solution)/shard_map/ppermute | solution.py:367
  34.8 0.6 %collective-permute-done.9.refs_7_ = bf16[32,6656]{1,0:T(8,128)(2,1)S(1)} collective-permute-done((bf16[32,6656]{1,0:T(8,128)(2,1)S(1)}, bf16[32,6656]{1,0:T(8,128)(2,1)S(1)}, u32[]{:S(2)}, u32[]{:S(2)}) %collective-permute-start.9) | collective-permute-done | bytes 426016 | tf_op jit(solution)/shard_map/ppermute | solution.py:367
  35.4 3.7 %shard_map.117 = (f32[4,128]{1,0:T(4,128)S(1)}, f32[4,128]{1,0:T(4,128)S(1)}, f32[4,128]{1,0:T(4,128)S(1)}, f32[4,128]{1,0:T(4,128)S(1)}) custom-call(bf16[8,2,64,6144]{3,2,1,0:T(8,128)(2,1)S(1)} %get-tuple-element.61.green, f32[128,32]{1,0:T(8,128)S(1)} %shard_map.116.before, bf16[32,6656]{1,0:T(8,128)(2,1)S(1)} %get-tuple-element.62.refs_0_, ...), custom_call_target="tpu_custom_call" | custom-call | flops 100000000 | bytes 1048576 | tf_op jit(solution)/shard_map/pallas_call | solution.py:342
  39.1 0.7 %collective-permute-start.10 = (f32[4,128]{1,0:T(4,128)S(1)}, f32[4,128]{1,0:T(4,128)S(1)}, u32[]{:S(2)}, u32[]{:S(2)}) collective-permute-start(f32[4,128]{1,0:T(4,128)S(1)} %get-tuple-element.69), channel_id=1, source_target_pairs={{0,1},{1,0},{2,3},{3,2},{4,5},{5,4},{6,7},{7,6},{8,9},{9,8},{10,11... | collective-permute-start | bytes 6152 | tf_op jit(solution)/shard_map/ppermute | solution.py:370
  39.8 2.6 %collective-permute-start.11 = (f32[4,128]{1,0:T(4,128)S(1)}, f32[4,128]{1,0:T(4,128)S(1)}, u32[]{:S(2)}, u32[]{:S(2)}) collective-permute-start(f32[4,128]{1,0:T(4,128)S(1)} %get-tuple-element.70), channel_id=1, source_target_pairs={{0,2},{1,3},{2,0},{3,1},{4,6},{5,7},{6,4},{7,5},{8,10},{9,11},{10,... | collective-permute-start | bytes 6152 | tf_op jit(solution)/shard_map/ppermute | solution.py:370
  42.4 1.2 %collective-permute-start.12 = (f32[4,128]{1,0:T(4,128)S(1)}, f32[4,128]{1,0:T(4,128)S(1)}, u32[]{:S(2)}, u32[]{:S(2)}) collective-permute-start(f32[4,128]{1,0:T(4,128)S(1)} %get-tuple-element.71), channel_id=1, source_target_pairs={{0,3},{1,2},{2,1},{3,0},{4,7},{5,6},{6,5},{7,4},{8,11},{9,10},{10,... | collective-permute-start | bytes 6152 | tf_op jit(solution)/shard_map/ppermute | solution.py:370
  43.5 0.8 %collective-permute-done.11 = f32[4,128]{1,0:T(4,128)S(1)} collective-permute-done((f32[4,128]{1,0:T(4,128)S(1)}, f32[4,128]{1,0:T(4,128)S(1)}, u32[]{:S(2)}, u32[]{:S(2)}) %collective-permute-start.11) | collective-permute-done | bytes 2080 | tf_op jit(solution)/shard_map/ppermute | solution.py:370
  44.3 3.5 %collective-permute-done.12 = f32[4,128]{1,0:T(4,128)S(1)} collective-permute-done((f32[4,128]{1,0:T(4,128)S(1)}, f32[4,128]{1,0:T(4,128)S(1)}, u32[]{:S(2)}, u32[]{:S(2)}) %collective-permute-start.12) | collective-permute-done | bytes 2080 | tf_op jit(solution)/shard_map/ppermute | solution.py:370
  47.8 0.6 %add_add_fusion = f32[4,128]{1,0:T(4,128)} fusion(f32[4,128]{1,0:T(4,128)S(1)} %collective-permute-done.12, f32[4,128]{1,0:T(4,128)S(1)} %collective-permute-done.11, f32[4,128]{1,0:T(4,128)S(1)} %get-tuple-element.68, f32[4,128]{1,0:T(4,128)S(1)} %collective-permute-done.10), kind=kLoop, calls=%fused_computation.1 | loop fusion | flops 1536 | bytes 10240 | tf_op jit(solution)/shard_map/add | solution.py:392
  (10 shorter events, 0.0 us)
Async XLA Ops:
  3.8 28.6 %collective-permute-start = (bf16[32,6656]{1,0:T(8,128)(2,1)S(1)}, bf16[32,6656]{1,0:T(8,128)(2,1)S(1)}, u32[]{:S(2)}, u32[]{:S(2)}) collective-permute-start(bf16[32,6656]{1,0:T(8,128)(2,1)S(1)} %get-tuple-element.37), channel_id=1, source_target_pairs={{0,8},{4,12},{8,0},{12,4},{16,24},{20,28},{24,16},{28,20},{1,9},{5... | collective-permute-start | bytes 1277960 | tf_op jit(solution)/shard_map/ppermute | solution.py:367
  6.8 25.6 %collective-permute-start.1 = (bf16[32,6656]{1,0:T(8,128)(2,1)S(1)}, bf16[32,6656]{1,0:T(8,128)(2,1)S(1)}, u32[]{:S(2)}, u32[]{:S(2)}) collective-permute-start(bf16[32,6656]{1,0:T(8,128)(2,1)S(1)} %get-tuple-element.38), channel_id=1, source_target_pairs={{0,16},{4,20},{8,24},{12,28},{16,0},{20,4},{24,8},{28,12},{1,17},{... | collective-permute-start | bytes 1277960 | tf_op jit(solution)/shard_map/ppermute | solution.py:367
  8.3 24.1 %collective-permute-start.2 = (bf16[32,6656]{1,0:T(8,128)(2,1)S(1)}, bf16[32,6656]{1,0:T(8,128)(2,1)S(1)}, u32[]{:S(2)}, u32[]{:S(2)}) collective-permute-start(bf16[32,6656]{1,0:T(8,128)(2,1)S(1)} %get-tuple-element.39), channel_id=1, source_target_pairs={{0,24},{4,28},{8,16},{12,20},{16,8},{20,12},{24,0},{28,4},{1,25},{... | collective-permute-start | bytes 1277960 | tf_op jit(solution)/shard_map/ppermute | solution.py:367
  8.3 17.9 %collective-permute-start.4 = (bf16[128,128]{1,0:T(8,128)(2,1)S(1)}, bf16[128,128]{1,0:T(8,128)(2,1)S(1)}, u32[]{:S(2)}, u32[]{:S(2)}) collective-permute-start(bf16[128,128]{1,0:T(8,128)(2,1)S(1)} %get-tuple-element.42), channel_id=1, source_target_pairs={{1,2},{3,4},{5,6},{7,8},{9,10},{11,12},{13,14},{15,16},{17,18},{19... | collective-permute-start | bytes 98312 | tf_op jit(solution)/shard_map/ppermute | solution.py:375
  9.0 17.2 %collective-permute-start.3 = (bf16[192,128]{1,0:T(8,128)(2,1)S(1)}, bf16[192,128]{1,0:T(8,128)(2,1)S(1)}, u32[]{:S(2)}, u32[]{:S(2)}) collective-permute-start(bf16[192,128]{1,0:T(8,128)(2,1)S(1)} %get-tuple-element.41), channel_id=1, source_target_pairs={{0,1},{1,0},{2,3},{3,2},{4,5},{5,4},{6,7},{7,6},{8,9},{9,8},{10,11... | collective-permute-start | bytes 147464 | tf_op jit(solution)/shard_map/ppermute | solution.py:370
  26.3 6.1 %collective-permute-start.5 = (bf16[128,128]{1,0:T(8,128)(2,1)S(1)}, bf16[128,128]{1,0:T(8,128)(2,1)S(1)}, u32[]{:S(2)}, u32[]{:S(2)}) collective-permute-start(bf16[128,128]{1,0:T(8,128)(2,1)S(1)} %pad_maximum_fusion.refs_8_), channel_id=1, source_target_pairs={{0,2},{1,3},{2,0},{3,1},{4,6},{5,7},{6,4},{7,5},{8,10},{9,11},{10,... | collective-permute-start | bytes 98312 | tf_op jit(solution)/shard_map/ppermute | solution.py:370
  27.3 6.2 %collective-permute-start.6 = (bf16[32,6656]{1,0:T(8,128)(2,1)S(1)}, bf16[32,6656]{1,0:T(8,128)(2,1)S(1)}, u32[]{:S(2)}, u32[]{:S(2)}) collective-permute-start(bf16[32,6656]{1,0:T(8,128)(2,1)S(1)} %get-tuple-element.62.refs_0_), channel_id=1, source_target_pairs={{0,4},{4,0},{8,12},{12,8},{16,20},{20,16},{24,28},{28,24},{1,5},{5... | collective-permute-start | bytes 1277960 | tf_op jit(solution)/shard_map/ppermute | solution.py:367
  32.4 1.8 %collective-permute-start.7 = (bf16[32,6656]{1,0:T(8,128)(2,1)S(1)}, bf16[32,6656]{1,0:T(8,128)(2,1)S(1)}, u32[]{:S(2)}, u32[]{:S(2)}) collective-permute-start(bf16[32,6656]{1,0:T(8,128)(2,1)S(1)} %collective-permute-done.refs_2_), channel_id=1, source_target_pairs={{0,4},{4,0},{8,12},{12,8},{16,20},{20,16},{24,28},{28,24},{1,5},{5... | collective-permute-start | bytes 1277960 | tf_op jit(solution)/shard_map/ppermute | solution.py:367
  32.5 2.4 %collective-permute-start.8 = (bf16[32,6656]{1,0:T(8,128)(2,1)S(1)}, bf16[32,6656]{1,0:T(8,128)(2,1)S(1)}, u32[]{:S(2)}, u32[]{:S(2)}) collective-permute-start(bf16[32,6656]{1,0:T(8,128)(2,1)S(1)} %collective-permute-done.1.refs_4_), channel_id=1, source_target_pairs={{0,4},{4,0},{8,12},{12,8},{16,20},{20,16},{24,28},{28,24},{1,5},{5... | collective-permute-start | bytes 1277960 | tf_op jit(solution)/shard_map/ppermute | solution.py:367
  33.0 2.5 %collective-permute-start.9 = (bf16[32,6656]{1,0:T(8,128)(2,1)S(1)}, bf16[32,6656]{1,0:T(8,128)(2,1)S(1)}, u32[]{:S(2)}, u32[]{:S(2)}) collective-permute-start(bf16[32,6656]{1,0:T(8,128)(2,1)S(1)} %collective-permute-done.2.refs_6_), channel_id=1, source_target_pairs={{0,4},{4,0},{8,12},{12,8},{16,20},{20,16},{24,28},{28,24},{1,5},{5... | collective-permute-start | bytes 1277960 | tf_op jit(solution)/shard_map/ppermute | solution.py:367
  39.1 4.5 %collective-permute-start.10 = (f32[4,128]{1,0:T(4,128)S(1)}, f32[4,128]{1,0:T(4,128)S(1)}, u32[]{:S(2)}, u32[]{:S(2)}) collective-permute-start(f32[4,128]{1,0:T(4,128)S(1)} %get-tuple-element.69), channel_id=1, source_target_pairs={{0,1},{1,0},{2,3},{3,2},{4,5},{5,4},{6,7},{7,6},{8,9},{9,8},{10,11... | collective-permute-start | bytes 6152 | tf_op jit(solution)/shard_map/ppermute | solution.py:370
  39.8 4.5 %collective-permute-start.11 = (f32[4,128]{1,0:T(4,128)S(1)}, f32[4,128]{1,0:T(4,128)S(1)}, u32[]{:S(2)}, u32[]{:S(2)}) collective-permute-start(f32[4,128]{1,0:T(4,128)S(1)} %get-tuple-element.70), channel_id=1, source_target_pairs={{0,2},{1,3},{2,0},{3,1},{4,6},{5,7},{6,4},{7,5},{8,10},{9,11},{10,... | collective-permute-start | bytes 6152 | tf_op jit(solution)/shard_map/ppermute | solution.py:370
  42.4 5.4 %collective-permute-start.12 = (f32[4,128]{1,0:T(4,128)S(1)}, f32[4,128]{1,0:T(4,128)S(1)}, u32[]{:S(2)}, u32[]{:S(2)}) collective-permute-start(f32[4,128]{1,0:T(4,128)S(1)} %get-tuple-element.71), channel_id=1, source_target_pairs={{0,3},{1,2},{2,1},{3,0},{4,7},{5,6},{6,5},{7,4},{8,11},{9,10},{10,... | collective-permute-start | bytes 6152 | tf_op jit(solution)/shard_map/ppermute | solution.py:370

commit v3 on v2

v3 whole, which is shorter than its diff:
```python
import functools

import jax
import jax.numpy as jnp
from jax import lax
from jax.experimental import pallas as pl
from jax.experimental.pallas import tpu as pltpu
from jax.sharding import PartitionSpec as P

PTS = 4
COST = 10**8
SLOT = 16
SPLIT = 5
HALO = 128
EB = 256
WIN = EB + 2 * HALO
NT = (((1,), (1,)), ((), ()))
F32 = jnp.float32
BF16 = jnp.bfloat16
VMEM = pl.BlockSpec(memory_space=pltpu.VMEM)
HBM = pl.BlockSpec(memory_space=pltpu.HBM)


def iota(shape, axis):
    return lax.broadcasted_iota(jnp.int32, shape, axis)


def lane_order():
    row, lane = iota((128, 128), 0), iota((128, 128), 1)
    return (lane == row % 8 // 2 * 32 + row // 8 * 2 + row % 2).astype(F32).astype(BF16)


def spread_basis(basis, wcat):
    spread = (iota((64, 32), 0) // 2 == iota((64, 32), 1)).astype(F32).astype(BF16)
    same = iota((64, 64), 0) % 2 == iota((64, 64), 1) % 2
    wide = []
    for m in range(4):
        tall = jnp.dot(spread, basis[m], preferred_element_type=F32).astype(BF16)
        full = lax.dot_general(tall, spread, NT, preferred_element_type=F32)
        wide.append(jnp.where(same, full, 0.0).astype(BF16))
    wcat[...] = jnp.concatenate(wide, axis=1)


def node_gaps():
    gap = iota((WIN, EB), 0) - iota((WIN, EB), 1)
    return jnp.where((gap >= 0) & (gap <= 2 * HALO), gap, -1).astype(F32).astype(BF16)


def flip(rows, order):
    return lax.dot_general(order, rows, NT, preferred_element_type=F32).astype(BF16)


def upright(tile, order):
    return jnp.dot(tile.T.astype(BF16), order, preferred_element_type=F32).astype(BF16)


def element_gaps():
    gap = iota((EB, WIN), 1) - iota((EB, WIN), 0)
    return jnp.where((gap >= 0) & (gap <= 2 * HALO), gap, -1).astype(F32).astype(BF16)


def gather_steps(at, window, links, dist, dist_t, selt, vs):
    across = links[:, at : at + EB] - (at + iota((8, EB), 1))
    down = across.astype(F32).T.astype(BF16)
    across = across.astype(F32).astype(BF16)
    one, zero = jnp.ones((), BF16), jnp.zeros((), BF16)

    def step(n):
        chosen = jnp.where(dist[...] == across[n : n + 1, :], one, zero)
        vs[n] = jnp.dot(window(), chosen, preferred_element_type=F32)
        selt[n * EB : (n + 1) * EB, :] = jnp.where(dist_t[...] == down[:, n : n + 1], one, zero)

    return [functools.partial(step, n) for n in range(8)]


def force_steps(at, material, wcat, vs, us, fs):
    coeffs = material[:, at : at + EB]
    kept = {}

    def step(cp):
        for n in range(0, 8, 2):
            re = jnp.concatenate([vs[n + i, cp * 8 : cp * 8 + 8, :] for i in range(2)], axis=0)
            im = jnp.concatenate([vs[n + i, 64 + cp * 8 : 72 + cp * 8, :] for i in range(2)], axis=0)
            for m in range(4):
                cr = coeffs[2 * m : 2 * m + 1, :]
                ci = coeffs[2 * m + 1 : 2 * m + 2, :]
                up = slice(m * 64 + n * 8, m * 64 + n * 8 + 16)
                us[cp, up, :EB] = (cr * re - ci * im).astype(BF16)
                us[cp, up, EB:] = (cr * im + ci * re).astype(BF16)
        kept[cp % 2] = jnp.dot(wcat[...], us[cp], preferred_element_type=F32)
        if cp % 2:
            for p in range(2):
                for n in range(8):
                    both = [kept[i][n * 8 : n * 8 + 8, p * EB : (p + 1) * EB] for i in range(2)]
                    rows = slice(p * 64 + cp * 8 - 8, p * 64 + cp * 8 + 8)
                    fs[rows, n * EB : (n + 1) * EB] = jnp.concatenate(both, axis=0).astype(BF16)

    return [functools.partial(step, cp) for cp in range(8)]


def scatter_steps(at, selt, fs, acc):
    def step(i):
        span = slice(i * 2 * EB, (i + 1) * 2 * EB)
        acc[:, at : at + WIN] += jnp.dot(fs[:, span], selt[span, :], preferred_element_type=F32)

    return [functools.partial(step, i) for i in range(4)]


def run_blocks(starts, windows, links, material, wcat, dist, dist_t, selt, vs, us, fs, accs):
    count = len(starts)
    for t in range(count + 2):
        lanes = []
        if t < count:
            lanes.append(gather_steps(starts[t], windows[t], links, dist, dist_t, selt.at[t % 3], vs.at[t % 2]))
        if 0 <= t - 1 < count:
            k = t - 1
            lanes.append(force_steps(starts[k], material, wcat, vs.at[k % 2], us.at[k % 2], fs.at[k % 2]))
        if 0 <= t - 2 < count:
            k = t - 2
            target, at = accs(k)
            lanes.append(scatter_steps(at, selt.at[k % 3], fs.at[k % 2], target))
        for i in range(8):
            for lane in lanes:
                if len(lane) == 8:
                    lane[i]()
                elif i % 2:
                    lane[i // 2]()


def fetch(parity, green, held, sems):
    row = lax.axis_index("row")
    length = held.shape[3]
    copies = []
    for k in range(held.shape[0]):
        start = pl.multiple_of((row ^ (2 * k + parity)) * length, 128)
        copies.append(pltpu.make_async_copy(green.at[:, :, pl.ds(start, length)], held.at[k], sems.at[k]))
    for copy in copies:
        copy.start()
    return copies


def first_kernel(split, disp, links, basis, material, green, acc, xt, wcat, dist, dist_t, held, selt, vs, us, fs, sems):
    nodes = disp.shape[0]
    copies = fetch(0, green, held, sems)
    @pl.when(lax.axis_index("row") >= 0)
    def blocks():
        order = lane_order()
        for i in range(nodes // 256):
            xt[:, HALO + i * 256 : HALO + (i + 1) * 256] = flip(disp[i * 256 : (i + 1) * 256, :], order)
        spread_basis(basis, wcat)
        dist[...] = node_gaps()
        dist_t[...] = element_gaps()
        acc[...] = jnp.zeros_like(acc)
        starts = [b * EB for b in range(1, split)]
        windows = [lambda at=at: xt[:, at : at + WIN] for at in starts]
        run_blocks(starts, windows, links, material, wcat, dist, dist_t, selt, vs, us, fs, lambda k: (acc, starts[k]))

    for copy in copies:
        copy.wait()


def second_kernel(
    split, links, material, before, xt, wcat, dist, dist_t, near, edge, green, acc, out, held, low, selt, vs, us, fs, sems
):
    nodes = links.shape[1]
    copies = fetch(1, green, held, sems)
    @pl.when(lax.axis_index("row") >= 0)
    def blocks():
        order = lane_order()
        even = lax.axis_index("col") % 2 == 0
        low[:, :HALO] = flip(jnp.where(even, edge[...], near[:HALO, :]), order)
        low[:, HALO:] = xt[:, HALO:WIN]
        starts = [b * EB for b in range(split, nodes // EB - 1)] + [0]
        windows = [lambda at=at: xt[:, at : at + WIN] for at in starts[:-1]] + [lambda: low[...]]
        run_blocks(starts, windows, links, material, wcat, dist, dist_t, selt, vs, us, fs, lambda k: (acc, starts[k]))
        for i in range((nodes - WIN + HALO) // 128):
            out[i * 128 : (i + 1) * 128, :] = upright(acc[:, HALO + i * 128 : HALO + (i + 1) * 128], order)

    for copy in copies:
        copy.wait()


def third_kernel(
    before, links, material, acc, xt, wcat, dist, dist_t, near, edge, out, high, last, selt, vs, us, fs, done, sem
):
    nodes = links.shape[1]
    keep = WIN - HALO
    at = nodes - EB
    order = lane_order()
    even = lax.axis_index("col") % 2 == 0
    high[:, :keep] = xt[:, at : at + keep]
    high[:, keep:] = flip(jnp.where(even, near[:HALO, :], edge[...]), order)
    last[...] = acc[:, at : at + WIN]
    windows = [lambda: high[...]]
    run_blocks([at], windows, links, material, wcat, dist, dist_t, selt, vs, us, fs, lambda k: (last, 0))
    for i in range(keep // 128):
        done[i * 128 : (i + 1) * 128, :] = upright(last[:, i * 128 : (i + 1) * 128], order)
    copy = pltpu.make_async_copy(done, out.at[pl.ds(nodes - keep, keep), :], sem)
    copy.start()
    copy.wait()


def block_scratch():
    return [
        pltpu.VMEM((3, 8 * EB, WIN), BF16),
        pltpu.VMEM((2, 8, 128, EB), F32),
        pltpu.VMEM((2, 8, 256, 2 * EB), BF16),
        pltpu.VMEM((2, 128, 8 * EB), BF16),
    ]


def element_params(blocks):
    return dict(
        compiler_params=pltpu.CompilerParams(vmem_limit_bytes=18 * 2**20),
        cost_estimate=pl.CostEstimate(flops=blocks * COST, bytes_accessed=2**20, transcendentals=0),
    )


def held_shape(rows, green):
    return jax.ShapeDtypeStruct((rows // 2, 2, green.shape[1], green.shape[2] // rows), BF16)


def first_call(rows, split, disp, links, basis, material, green):
    wide = disp.shape[0] + 2 * HALO
    return pl.pallas_call(
        functools.partial(first_kernel, split),
        out_shape=[
            jax.ShapeDtypeStruct((128, wide), F32),
            jax.ShapeDtypeStruct((128, wide), BF16),
            jax.ShapeDtypeStruct((64, 256), BF16),
            jax.ShapeDtypeStruct((WIN, EB), BF16),
            jax.ShapeDtypeStruct((EB, WIN), BF16),
            held_shape(rows, green),
        ],
        in_specs=[VMEM] * 4 + [HBM],
        out_specs=[VMEM] * 6,
        scratch_shapes=block_scratch() + [pltpu.SemaphoreType.DMA((rows // 2,))],
        **element_params(split - 1),
    )(disp, links, basis, material, green)


def second_call(rows, split, links, material, acc, shared, near, edge, green):
    nodes = links.shape[1]
    return pl.pallas_call(
        functools.partial(second_kernel, split),
        out_shape=[
            jax.ShapeDtypeStruct(acc.shape, F32),
            jax.ShapeDtypeStruct((nodes, 128), BF16),
            held_shape(rows, green),
        ],
        in_specs=[VMEM] * 9 + [HBM],
        out_specs=[VMEM] * 3,
        scratch_shapes=[pltpu.VMEM((128, WIN), BF16)] + block_scratch() + [pltpu.SemaphoreType.DMA((rows // 2,))],
        input_output_aliases={2: 0},
        **element_params(nodes // EB - split),
    )(links, material, acc, *shared, near, edge, green)


def third_call(before, links, material, acc, shared, near, edge):
    return pl.pallas_call(
        third_kernel,
        out_shape=jax.ShapeDtypeStruct(before.shape, BF16),
        in_specs=[HBM] + [VMEM] * 9,
        out_specs=HBM,
        scratch_shapes=[pltpu.VMEM((128, WIN), BF16), pltpu.VMEM((128, WIN), F32)]
        + block_scratch()
        + [pltpu.VMEM((WIN - HALO, 128), BF16), pltpu.SemaphoreType.DMA],
        input_output_aliases={0: 0},
        **element_params(1),
    )(before, links, material, acc, *shared, near, edge)


def prepare_kernel(rows, cols, *refs):
    masks = rows // 2
    sources = refs[:9]
    messages = refs[9 : 8 + masks]
    near, edge, points, disp, links, basis, material, slots, traction, node, weight, count, recv, sems = refs[8 + masks :]
    lines = traction.shape[0]
    row, col = lax.axis_index("row"), lax.axis_index("col")
    pieces = 3 if lines // 128 % 3 == 0 else 1
    share = lines // pieces
    copies = [
        pltpu.make_async_copy(
            sources[0].at[pl.ds(i * share, share), :], traction.at[pl.ds(i * share, share), :], sems.at[8 + i]
        )
        for i in range(pieces)
    ]
    others = [
        pltpu.make_async_copy(sources[i + 1], target, sems.at[i])
        for i, target in enumerate((disp, node, weight, count, recv, links, basis, material))
    ]
    for copy in copies + others:
        copy.start()

    gap = cols * SLOT * 8
    widen = (iota((128, 512), 1) // 4 == iota((128, 512), 0)).astype(BF16)
    comp = iota((32, 512), 1) % 4
    for i in range(lines // 128):
        if i * 128 % share == 0:
            copies[i * 128 // share].wait()
        wide = jnp.dot(traction[i * 128 : (i + 1) * 128, :].astype(F32).T.astype(BF16), widen, preferred_element_type=F32)
        line = wide[:32]
        for k in range(1, 4):
            line = jnp.where(comp == k, wide[k * 32 : (k + 1) * 32], line)
        line = line.astype(BF16)
        for t in range(2):
            lane = i * 512 + t * 256
            for k, message in enumerate(messages):
                into = lane + gap if k == 1 and lane >= lines * 2 else lane
                message[:, into : into + 256] = line[:, t * 256 : (t + 1) * 256]

    for copy in others:
        copy.wait()
    tail, head = disp[disp.shape[0] - HALO :, :], disp[:HALO, :]
    even = col % 2 == 0
    near[:HALO, :] = jnp.where(even, tail, head)
    edge[...] = jnp.where(even, head, tail)
    total = node.shape[1]
    devices = count.shape[1]
    copies = (iota((devices, total), 1) // SLOT == iota((devices, total), 0)).astype(BF16)
    counts = jnp.broadcast_to(count[...].astype(F32), (8, devices)).astype(BF16)
    live = jnp.dot(counts, copies, preferred_element_type=F32)
    scale = jnp.where((iota((8, total), 1) % SLOT).astype(F32) < live, weight[...], 0.0)
    columns = jnp.where(iota((8, total), 0) == 0, node[...].astype(F32), scale).T
    for i in range(total // 256):
        chunk = columns[i * 256 : (i + 1) * 256]
        hit = chunk[:, 0:1] == iota((256, disp.shape[0]), 1).astype(F32)
        picked = jnp.dot(jnp.where(hit, 1.0, 0.0).astype(BF16), disp[...], preferred_element_type=F32)
        slots[i * 256 : (i + 1) * 256, :] = (picked * chunk[:, 1:2]).astype(BF16)

    each = cols * SLOT
    places = [(messages[k], lines * 4) for k in range(3)] + [(messages[1], lines * 2)]
    places[1] = (messages[1], lines * 4 + gap)
    places += [(message, lines * 4) for message in messages[3:]]
    for k, (message, lane) in enumerate(places):
        for core in range(2):
            target = (row // 2 ^ k) * 2 + core
            for t in range(each // 32):
                start = pl.multiple_of(target * each + t * 32, 32)
                message[:, lane : lane + 128] = slots[pl.ds(start, 32), :]
                lane += 128

    for t in range(total // 128):
        feeds = recv[:, t * 128 : (t + 1) * 128].astype(F32)
        feeds = jnp.broadcast_to(feeds, (16, 128)).astype(BF16)
        points[t * 16 : (t + 1) * 16, :] = feeds
        near[HALO + t * 16 : HALO + (t + 1) * 16, :] = feeds


def prepare_call(rows, cols, traction, disp, node, weight, count, recv, links, basis, material):
    masks = rows // 2
    width = traction.shape[0] * 4 + cols * SLOT * 8
    widths = [width, width + cols * SLOT * 8] + [width] * (masks - 3)
    near = jax.ShapeDtypeStruct((HALO + node.shape[1] // 8, 128), BF16)
    edge = jax.ShapeDtypeStruct((HALO, 128), BF16)
    points = jax.ShapeDtypeStruct((node.shape[1] // 8, 128), BF16)
    same = [jax.ShapeDtypeStruct(value.shape, value.dtype) for value in (disp, links, basis, material)]
    return pl.pallas_call(
        functools.partial(prepare_kernel, rows, cols),
        out_shape=[jax.ShapeDtypeStruct((32, width), BF16) for width in widths] + [near, edge, points] + same,
        in_specs=[HBM] * 9,
        out_specs=[VMEM] * (masks + 6),
        scratch_shapes=[pltpu.VMEM((node.shape[1], 128), BF16)]
        + [pltpu.VMEM(value.shape, value.dtype) for value in (traction, node, weight, count, recv)]
        + [pltpu.SemaphoreType.DMA((11,))],
        compiler_params=pltpu.CompilerParams(vmem_limit_bytes=24 * 2**20),
    )(traction, disp, node, weight, count, recv, links, basis, material)


def slab_sum(high, plan, green, messages, start):
    both = start
    for which, lane, width, k, into in plan:
        flat = green[k // 2, :, :, into : into + width].reshape(2 * high, width)
        both = both + lax.dot_general(flat, messages[which][:, lane : lane + width], NT, preferred_element_type=F32)
    return both


def early_kernel(plan, green, *refs):
    high = green.shape[2]
    refs[-1][...] = slab_sum(high, plan, green, refs[:-1], jnp.zeros((2 * high, 32), F32))


def early_call(plan, green, messages):
    return pl.pallas_call(
        functools.partial(early_kernel, plan),
        out_shape=jax.ShapeDtypeStruct((2 * green.shape[2], 32), F32),
        in_specs=[VMEM] * (1 + len(messages)),
        out_specs=VMEM,
        compiler_params=pltpu.CompilerParams(vmem_limit_bytes=8 * 2**20),
        cost_estimate=pl.CostEstimate(flops=COST, bytes_accessed=2**20, transcendentals=0),
    )(green, *messages)


def late_kernel(rows, cols, plan, slots, green, before, *refs):
    count = 2 * (max(entry[0] for entry in plan) + 1)
    messages, points = refs[:count], refs[count : -cols - 3]
    outs = refs[-cols - 3 : -3]
    sent, traced, total = refs[-3:]
    row, col = lax.axis_index("row"), lax.axis_index("col")
    high = green.shape[2]
    each = cols * SLOT
    for which, lane, k in slots:
        for core in range(2):
            into = pl.multiple_of((row ^ k ^ core) * SLOT, SLOT)
            for t in range(each // 32):
                at = pl.multiple_of(lane + (row % 2 * (each // 32) + t) * 128, 128)
                pair = messages[which + core * (count // 2)][:, pl.ds(at, 128)]
                sent[2 * t, pl.ds(into, SLOT), :] = pair[:SLOT]
                sent[2 * t + 1, pl.ds(into, SLOT), :] = pair[SLOT:]
    width = rows * SLOT
    length = width * cols
    source, place = iota((length, width), 0), iota((length, width), 1)
    take = (source == (place // SLOT * cols + col) * SLOT + place % SLOT).astype(BF16)
    tall = length // 8
    owners = [block[i * tall : (i + 1) * tall, :] for block in points for i in range(block.shape[0] // tall)]
    for s in range(cols):
        values = jnp.concatenate([owners[s][t * 16 : (t + 1) * 16, :] for t in range(length // 128)], axis=1)
        mine = jnp.dot(values, take, preferred_element_type=F32)[:8]
        hot = (mine == iota(mine.shape, 0).astype(F32)).astype(BF16)
        traced[col ^ s] = jnp.dot(hot, sent[col ^ s], preferred_element_type=F32)

    both = slab_sum(high, plan, green, messages[count // 2 :], before[...])
    real = both[:high, :16] - both[high:, 16:]
    imag = both[:high, 16:] + both[high:, :16]
    total[...] = jnp.concatenate([real, imag, jnp.zeros((high, 96), F32)], axis=1)
    for c in range(cols):
        parts = [total[pl.ds(c * PTS * 4 + k, PTS, stride=4), :][:, :32] for k in range(4)]
        traced[c, :PTS, :] = traced[c, :PTS, :] - jnp.concatenate(parts, axis=1)
    for s in range(cols):
        outs[s][...] = traced[col ^ s, :PTS, :]


def late_call(rows, cols, plan, slots, green, before, messages, points):
    return pl.pallas_call(
        functools.partial(late_kernel, rows, cols, plan, slots),
        out_shape=[jax.ShapeDtypeStruct((PTS, 128), F32)] * cols,
        in_specs=[VMEM] * (2 + len(messages) + len(points)),
        out_specs=[VMEM] * cols,
        scratch_shapes=[
            pltpu.VMEM((cols, rows * SLOT, 128), BF16),
            pltpu.VMEM((cols, 8, 128), F32),
            pltpu.VMEM((green.shape[2], 128), F32),
        ],
        compiler_params=pltpu.CompilerParams(vmem_limit_bytes=8 * 2**20),
        cost_estimate=pl.CostEstimate(flops=COST, bytes_accessed=2**20, transcendentals=0),
    )(green, before, *messages, *points)


def shards(rows, cols, displacement, connectivity, element_basis, material, traction, green, node, weight, count, recv):
    masks = rows // 2
    given = (traction, displacement, node, weight, count, recv, connectivity.T, element_basis, material, green)
    *given, green = [pltpu.with_memory_space_constraint(value, pltpu.HBM) for value in given]
    made = prepare_call(rows, cols, *given)
    messages, (near, edge, points, disp, links, basis, coeffs) = made[: masks - 1], made[masks - 1 :]
    flat = ("row", "col")
    last = rows * cols - 1
    half = traction.shape[0] * 2
    each = cols * SLOT * 8

    def across(value, mask):
        return lax.ppermute(value, "row", [(i, i ^ mask) for i in range(rows)])

    def along(value, s):
        return lax.ppermute(value, "col", [(i, i ^ s) for i in range(cols)])

    own = messages[0]
    beside, below = across(messages[1], 2), across(messages[2], 4)
    far = [across(messages[k], 2 * k + 2) for k in range(3, masks - 1)]
    near = along(near, 1)
    steps = [(i, i + 1) for i in range(1, last, 2)]
    edge = lax.ppermute(edge, flat, steps + [(b, a) for a, b in steps])
    made = first_call(rows, SPLIT, disp, links, basis, coeffs, green)
    own, beside, below, near, edge, points, made = lax.optimization_barrier(
        (own, beside, below, near, edge, points, made)
    )
    acc, *shared, held = made
    cross = [across(beside[:, : half + each], 4), across(below[:, half : 2 * half], 2)]
    known = [jnp.concatenate([points, near[HALO:]], axis=0)]
    while len(known) < cols // 2:
        known += [along(value, 2 * len(known)) for value in known]
    acc, before, held_pair = second_call(rows, SPLIT, links, coeffs, acc, shared, near, edge, green)
    own, beside, below, cross, far, known, before, held_pair = lax.optimization_barrier(
        (own, beside, below, cross, far, known, before, held_pair)
    )
    here = [own, beside, below] + cross + far
    there = [across(value, 1) for value in here]
    plan = [(0, 0, 2 * half, 0, 0), (1, 0, half, 2, 0), (1, half + each, half, 2, half), (2, 0, 2 * half, 4, 0)]
    plan += [(3, 0, half, 6, 0), (4, 0, half, 6, half)]
    slots = [(0, 2 * half, 0), (1, 2 * half + each, 2), (2, 2 * half, 4), (3, half, 6)]
    for i in range(len(far)):
        plan.append((5 + i, 0, 2 * half, 8 + 2 * i, 0))
        slots.append((5 + i, 2 * half, 8 + 2 * i))
    early = early_call(plan, held, here)
    early, there = lax.optimization_barrier((early, there))
    plan = [(which, lane, width, k + 1, into) for which, lane, width, k, into in plan]
    parts = late_call(rows, cols, plan, slots, held_pair, early, here + there, known)
    sums = [along(parts[s], s) for s in range(1, cols)]
    before, total = lax.optimization_barrier((before, parts[0]))
    fe_out = third_call(before, links, coeffs, acc, shared, near, edge)
    sums, fe_out = lax.optimization_barrier((sums, fe_out))
    boundary = total
    for value in sums:
        boundary = boundary + value
    return fe_out, boundary


def solution(mesh):
    rows, cols = mesh.shape["row"], mesh.shape["col"]
    near = P(("row", "col"), None)
    placed = (near, near, P(), P(None, ("row", "col")), P(("col", "row"), None), P(None, "row", "col"), near, near, near, near)
    return jax.shard_map(
        functools.partial(shards, rows, cols),
        mesh=mesh,
        in_specs=placed,
        out_specs=(near, near),
        check_vma=False,
    )
```

time: 48.5 us -> 42.9 us (0.88)
  Pallas kernels: 23.9 us -> 20.6 us
  waiting for transfers between devices: 6.09 us -> 3.14 us
  starting transfers between devices: 17 us -> 17.6 us
    ppermute x5, waiting for transfers between devices: 4.23 us -> 0.43 us  [along(): return lax.ppermute(value, 'col', [(i, i ^ s) for i in range(cols)])]
    pallas_call x4 -> x5, Pallas kernels: 20.8 us -> 17.5 us  [the longest x1 5.6 us: first_call(): pl.pallas_call(functools.partial(first_kernel, split), out_shape=[jax.Sha...]
    ppermute x7 -> x9, starting transfers between devices: 5.89 us -> 8.66 us  [across(): return lax.ppermute(value, 'row', [(i, i ^ mask) for i in range(rows)])]
    ppermute x5, starting transfers between devices: 10.5 us -> 8.26 us  [along(): return lax.ppermute(value, 'col', [(i, i ^ s) for i in range(cols)])]
    ppermute x7 -> x9, waiting for transfers between devices: 1.85 us -> 2.7 us  [across(): return lax.ppermute(value, 'row', [(i, i ^ mask) for i in range(rows)])]
  transfers between devices with their start and end apart: 13 -> 15, of which waited for: 5 -> 3; matrix products, arithmetic and copies ran while one was open for 0% -> 0% of each run, Pallas kernels for 35% -> 35%
where the time goes in v3:
time: 42.9 us; the launch traced here: 42.7 us
  Pallas kernels  20.6 us (48%)
  starting transfers between devices  17.6 us (41%)
  waiting for transfers between devices  3.14 us (7%)
  between operations  0.78 us (2%)
  other arithmetic  0.59 us (1%)
    ppermute x9, starting transfers between devices, across(): return lax.ppermute(value, 'row', [(i, i ^ mask) for i in range(rows)])  8.66 us
    ppermute x5, starting transfers between devices, along(): return lax.ppermute(value, 'col', [(i, i ^ s) for i in range(cols)])  8.26 us
    pallas_call x1, Pallas kernels, first_call(): pl.pallas_call(functools.partial(first_kernel, split), out_shape=[jax.Sha...  5.6 us
    pallas_call x1, Pallas kernels, second_call(): pl.pallas_call(functools.partial(second_kernel, split), out_shape=[jax.Sh...  5.17 us
    pallas_call x1, Pallas kernels, prepare_call(): pl.pallas_call(functools.partial(prepare_kernel, rows, cols), out_shape=[...  3.12 us
    ppermute x9, waiting for transfers between devices, across(): return lax.ppermute(value, 'row', [(i, i ^ mask) for i in range(rows)])  2.7 us
    pallas_call x1, Pallas kernels, third_call(): pl.pallas_call(third_kernel, out_shape=jax.ShapeDtypeStruct(before.shape,...  2.51 us
    pallas_call x1, Pallas kernels, late_call(): pl.pallas_call(functools.partial(late_kernel, rows, cols, plan, slots), o...  2.45 us
  transfers between devices with their start and end apart: 15, of which 3 were waited for; matrix products, arithmetic and copies ran while one was open for 0% of the time, Pallas kernels for 35%

profile of v3, /device:TPU:0, one launch (start us, length us, event | category | flops | bytes accessed | tf_op | source)
XLA Modules:
  0.0 42.7 jit_solution(8023337340126856603)
XLA Ops:
  0.6 3.1 %shard_map.113 = (bf16[32,6656]{1,0:T(8,128)(2,1)S(1)}, bf16[32,7168]{1,0:T(8,128)(2,1)S(1)}, bf16[32,6656]{1,0:T(8,128)(2,1)S(1)}, bf16[192,128]{1,0:T(8,128)(2...) custom-call(bf16[1536,128]{1,0:T(8,128)(2,1)} %refs_0_.1, ...), custom_call_target="tpu_custom_call" | custom-call | tf_op jit(solution)/shard_map/pallas_call | solution.py:358
  3.8 3.0 %collective-permute-start = (bf16[32,7168]{1,0:T(8,128)(2,1)S(1)}, bf16[32,7168]{1,0:T(8,128)(2,1)S(1)}, u32[]{:S(2)}, u32[]{:S(2)}) collective-permute-start(bf16[32,7168]{1,0:T(8,128)(2,1)S(1)} %get-tuple-element.59), channel_id=1, source_target_pairs={{0,8},{4,12},{8,0},{12,4},{16,24},{20,28},{24,16},{28,20},{1,9},{5... | collective-permute-start | bytes 1376264 | tf_op jit(solution)/shard_map/ppermute | solution.py:461
  6.8 1.5 %collective-permute-start.1 = (bf16[32,6656]{1,0:T(8,128)(2,1)S(1)}, bf16[32,6656]{1,0:T(8,128)(2,1)S(1)}, u32[]{:S(2)}, u32[]{:S(2)}) collective-permute-start(bf16[32,6656]{1,0:T(8,128)(2,1)S(1)} %get-tuple-element.60), channel_id=1, source_target_pairs={{0,16},{4,20},{8,24},{12,28},{16,0},{20,4},{24,8},{28,12},{1,17},{... | collective-permute-start | bytes 1277960 | tf_op jit(solution)/shard_map/ppermute | solution.py:461
  8.3 1.6 %collective-permute-start.2 = (bf16[192,128]{1,0:T(8,128)(2,1)S(1)}, bf16[192,128]{1,0:T(8,128)(2,1)S(1)}, u32[]{:S(2)}, u32[]{:S(2)}) collective-permute-start(bf16[192,128]{1,0:T(8,128)(2,1)S(1)} %get-tuple-element.61), channel_id=1, source_target_pairs={{0,1},{1,0},{2,3},{3,2},{4,5},{5,4},{6,7},{7,6},{8,9},{9,8},{10,11... | collective-permute-start | bytes 147464 | tf_op jit(solution)/shard_map/ppermute | solution.py:464
  9.9 0.7 %collective-permute-start.3 = (bf16[128,128]{1,0:T(8,128)(2,1)S(1)}, bf16[128,128]{1,0:T(8,128)(2,1)S(1)}, u32[]{:S(2)}, u32[]{:S(2)}) collective-permute-start(bf16[128,128]{1,0:T(8,128)(2,1)S(1)} %get-tuple-element.62), channel_id=1, source_target_pairs={{1,2},{3,4},{5,6},{7,8},{9,10},{11,12},{13,14},{15,16},{17,18},{19... | collective-permute-start | bytes 98312 | tf_op jit(solution)/shard_map/ppermute | solution.py:471
  10.5 5.6 %shard_map.114 = (f32[128,2304]{1,0:T(8,128)S(1)}, bf16[128,2304]{1,0:T(8,128)(2,1)S(1)}, bf16[64,256]{1,0:T(8,128)(2,1)S(1)}, bf16[512,256]{1,0:T(8,128)(2,1)S(...) custom-call(bf16[2048,128]{1,0:T(8,128)(2,1)S(1)} %get-tuple-element.64.disp, ...), custom_call_target="tpu_custom_call" | custom-call | flops 400000000 | bytes 1048576 | tf_op jit(solution)/shard_map/pallas_call | solution.py:225
  16.2 1.9 %collective-permute-done.1.refs_2_ = bf16[32,6656]{1,0:T(8,128)(2,1)S(1)} collective-permute-done((bf16[32,6656]{1,0:T(8,128)(2,1)S(1)}, bf16[32,6656]{1,0:T(8,128)(2,1)S(1)}, u32[]{:S(2)}, u32[]{:S(2)}) %collective-permute-start.1) | collective-permute-done | bytes 426016 | tf_op jit(solution)/shard_map/ppermute | solution.py:461
  18.1 1.9 %collective-permute-start.4 = (bf16[32,3584]{1,0:T(8,128)(2,1)S(1)}, bf16[32,3584]{1,0:T(8,128)(2,1)S(1)}, u32[]{:S(2)}, u32[]{:S(2)}) collective-permute-start(bf16[32,3584]{1,0:T(8,128)(2,1)S(1)} %slice.9), channel_id=1, source_target_pairs={{0,16},{4,20},{8,24},{12,28},{16,0},{20,4},{24,8},{28,12},{1,17},{... | collective-permute-start | bytes 688136 | tf_op jit(solution)/shard_map/ppermute | solution.py:461
  20.0 1.0 %collective-permute-start.5 = (bf16[32,3072]{1,0:T(8,128)(2,1)S(1)}, bf16[32,3072]{1,0:T(8,128)(2,1)S(1)}, u32[]{:S(2)}, u32[]{:S(2)}) collective-permute-start(bf16[32,3072]{1,0:T(8,128)(2,1)S(1)} %slice.10), channel_id=1, source_target_pairs={{0,8},{4,12},{8,0},{12,4},{16,24},{20,28},{24,16},{28,20},{1,9},{5... | collective-permute-start | bytes 589832 | tf_op jit(solution)/shard_map/ppermute | solution.py:461
  21.1 2.2 %collective-permute-start.6 = (bf16[128,128]{1,0:T(8,128)(2,1)S(1)}, bf16[128,128]{1,0:T(8,128)(2,1)S(1)}, u32[]{:S(2)}, u32[]{:S(2)}) collective-permute-start(bf16[128,128]{1,0:T(8,128)(2,1)S(1)} %pad_maximum_fusion.refs_10_), channel_id=1, source_target_pairs={{0,2},{1,3},{2,0},{3,1},{4,6},{5,7},{6,4},{7,5},{8,10},{9,11},{10,... | collective-permute-start | bytes 98312 | tf_op jit(solution)/shard_map/ppermute | solution.py:464
  23.3 5.2 %shard_map.115 = (f32[128,2304]{1,0:T(8,128)S(1)}, bf16[2048,128]{1,0:T(8,128)(2,1)}, bf16[4,2,64,6144]{3,2,1,0:T(8,128)(2,1)S(1)}) custom-call(s32[8,2048]{1,0:T(8,128)S(1)} %get-tuple-element.65.links, f32[8,2048]{1,0:T(8,128)S(1)} %get-tuple-element.67.material, f32[128,2304]{1,0:T(8,128)S(1)} %get-tuple-element.79.before, ...), custom_call_target="tpu_custom_call", output_to_operand_aliasing={{0}: (2, {})} | custom-call | flops 300000000 | bytes 1048576 | tf_op jit(solution)/shard_map/pallas_call | solution.py:244
  28.5 0.1 collective-permute-start.8
  28.6 0.5 %collective-permute-start.7 = (bf16[32,6656]{1,0:T(8,128)(2,1)S(1)}, bf16[32,6656]{1,0:T(8,128)(2,1)S(1)}, u32[]{:S(2)}, u32[]{:S(2)}) collective-permute-start(bf16[32,6656]{1,0:T(8,128)(2,1)S(1)} %get-tuple-element.89.refs_0_), channel_id=1, source_target_pairs={{0,4},{4,0},{8,12},{12,8},{16,20},{20,16},{24,28},{28,24},{1,5},{5... | collective-permute-start | bytes 1277960 | tf_op jit(solution)/shard_map/ppermute | solution.py:461
  29.1 0.1 collective-permute-start.9
  29.2 0.4 %collective-permute-start.10 = (bf16[32,3584]{1,0:T(8,128)(2,1)S(1)}, bf16[32,3584]{1,0:T(8,128)(2,1)S(1)}, u32[]{:S(2)}, u32[]{:S(2)}) collective-permute-start(bf16[32,3584]{1,0:T(8,128)(2,1)S(1)} %collective-permute-done.4.refs_3_), channel_id=1, source_target_pairs={{0,4},{4,0},{8,12},{12,8},{16,20},{20,16},{24,28},{28,24},{1,5},{5... | collective-permute-start | bytes 688136 | tf_op jit(solution)/shard_map/ppermute | solution.py:461
  29.6 0.1 collective-permute-start.11
  29.7 1.8 %shard_map.116.before = f32[128,32]{1,0:T(8,128)S(1)} custom-call(bf16[4,2,64,6144]{3,2,1,0:T(8,128)(2,1)S(1)} %get-tuple-element.88.green, bf16[32,6656]{1,0:T(8,128)(2,1)S(1)} %get-tuple-element.89.refs_0_, bf16[32,7168]{1,0:T(8,128)(2,1)S(1)} %collective-permute-done.refs_1_, bf16[32,6656]{1,0:T(8,128)(2,1)S(1)} %collective-permute-done.1.refs_2_, ...), custom_call_target="tpu_custom_call" | custom-call | flops 100000000 | bytes 1048576 | tf_op jit(solution)/shard_map/pallas_call | solution.py:384
  31.5 0.8 %collective-permute-done.11.refs_9_ = bf16[32,3072]{1,0:T(8,128)(2,1)S(1)} collective-permute-done((bf16[32,3072]{1,0:T(8,128)(2,1)S(1)}, bf16[32,3072]{1,0:T(8,128)(2,1)S(1)}, u32[]{:S(2)}, u32[]{:S(2)}) %collective-permute-start.11) | collective-permute-done | bytes 196640 | tf_op jit(solution)/shard_map/ppermute | solution.py:461
  32.3 2.4 %shard_map.117 = (f32[4,128]{1,0:T(4,128)S(1)}, f32[4,128]{1,0:T(4,128)S(1)}, f32[4,128]{1,0:T(4,128)S(1)}, f32[4,128]{1,0:T(4,128)S(1)}) custom-call(bf16[4,2,64,6144]{3,2,1,0:T(8,128)(2,1)S(1)} %get-tuple-element.87.green, f32[128,32]{1,0:T(8,128)S(1)} %shard_map.116.before, bf16[32,6656]{1,0:T(8,128)(2,1)S(1)} %get-tuple-element.89.refs_0_, ...), custom_call_target="tpu_custom_call" | custom-call | flops 100000000 | bytes 1048576 | tf_op jit(solution)/shard_map/pallas_call | solution.py:434
  34.7 2.0 %collective-permute-start.12 = (f32[4,128]{1,0:T(4,128)S(1)}, f32[4,128]{1,0:T(4,128)S(1)}, u32[]{:S(2)}, u32[]{:S(2)}) collective-permute-start(f32[4,128]{1,0:T(4,128)S(1)} %get-tuple-element.102), channel_id=1, source_target_pairs={{0,1},{1,0},{2,3},{3,2},{4,5},{5,4},{6,7},{7,6},{8,9},{9,8},{10,11... | collective-permute-start | bytes 6152 | tf_op jit(solution)/shard_map/ppermute | solution.py:464
  36.8 2.4 %collective-permute-start.14 = (f32[4,128]{1,0:T(4,128)S(1)}, f32[4,128]{1,0:T(4,128)S(1)}, u32[]{:S(2)}, u32[]{:S(2)}) collective-permute-start(f32[4,128]{1,0:T(4,128)S(1)} %get-tuple-element.104), channel_id=1, source_target_pairs={{0,3},{1,2},{2,1},{3,0},{4,7},{5,6},{6,5},{7,4},{8,11},{9,10},{10,... | collective-permute-start | bytes 6152 | tf_op jit(solution)/shard_map/ppermute | solution.py:464
  39.2 2.5 %shard_map.118 = bf16[2048,128]{1,0:T(8,128)(2,1)} custom-call(bf16[2048,128]{1,0:T(8,128)(2,1)} %get-tuple-element.107.before, s32[8,2048]{1,0:T(8,128)S(1)} %get-tuple-element.65.links, f32[8,2048]{1,0:T(8,128)S(1)} %get-tuple-element.67.material, f32[128,2304]{1,0:T(8,128)S(1)} %get-tuple-element.108.acc, ...), custom_call_target="tpu_custom_call", output_to_operand_aliasing={{}: (0, {})} | custom-call | flops 100000000 | bytes 1048576 | tf_op jit(solution)/shard_map/pallas_call | solution.py:260
  41.7 0.4 collective-permute-done.14
  42.1 0.6 %add_add_fusion = f32[4,128]{1,0:T(4,128)} fusion(f32[4,128]{1,0:T(4,128)S(1)} %collective-permute-done.14, f32[4,128]{1,0:T(4,128)S(1)} %collective-permute-done.13, f32[4,128]{1,0:T(4,128)S(1)} %get-tuple-element.110, f32[4,128]{1,0:T(4,128)S(1)} %collective-permute-done.12), kind=kLoop, calls=%fused_computation.1 | loop fusion | flops 1536 | bytes 10240 | tf_op jit(solution)/shard_map/add | solution.py:503
  (17 shorter events, 0.1 us)
Async XLA Ops:
  3.8 14.3 %collective-permute-start = (bf16[32,7168]{1,0:T(8,128)(2,1)S(1)}, bf16[32,7168]{1,0:T(8,128)(2,1)S(1)}, u32[]{:S(2)}, u32[]{:S(2)}) collective-permute-start(bf16[32,7168]{1,0:T(8,128)(2,1)S(1)} %get-tuple-element.59), channel_id=1, source_target_pairs={{0,8},{4,12},{8,0},{12,4},{16,24},{20,28},{24,16},{28,20},{1,9},{5... | collective-permute-start | bytes 1376264 | tf_op jit(solution)/shard_map/ppermute | solution.py:461
  6.8 11.3 %collective-permute-start.1 = (bf16[32,6656]{1,0:T(8,128)(2,1)S(1)}, bf16[32,6656]{1,0:T(8,128)(2,1)S(1)}, u32[]{:S(2)}, u32[]{:S(2)}) collective-permute-start(bf16[32,6656]{1,0:T(8,128)(2,1)S(1)} %get-tuple-element.60), channel_id=1, source_target_pairs={{0,16},{4,20},{8,24},{12,28},{16,0},{20,4},{24,8},{28,12},{1,17},{... | collective-permute-start | bytes 1277960 | tf_op jit(solution)/shard_map/ppermute | solution.py:461
  8.3 7.9 %collective-permute-start.2 = (bf16[192,128]{1,0:T(8,128)(2,1)S(1)}, bf16[192,128]{1,0:T(8,128)(2,1)S(1)}, u32[]{:S(2)}, u32[]{:S(2)}) collective-permute-start(bf16[192,128]{1,0:T(8,128)(2,1)S(1)} %get-tuple-element.61), channel_id=1, source_target_pairs={{0,1},{1,0},{2,3},{3,2},{4,5},{5,4},{6,7},{7,6},{8,9},{9,8},{10,11... | collective-permute-start | bytes 147464 | tf_op jit(solution)/shard_map/ppermute | solution.py:464
  9.9 6.3 %collective-permute-start.3 = (bf16[128,128]{1,0:T(8,128)(2,1)S(1)}, bf16[128,128]{1,0:T(8,128)(2,1)S(1)}, u32[]{:S(2)}, u32[]{:S(2)}) collective-permute-start(bf16[128,128]{1,0:T(8,128)(2,1)S(1)} %get-tuple-element.62), channel_id=1, source_target_pairs={{1,2},{3,4},{5,6},{7,8},{9,10},{11,12},{13,14},{15,16},{17,18},{19... | collective-permute-start | bytes 98312 | tf_op jit(solution)/shard_map/ppermute | solution.py:471
  18.1 10.4 %collective-permute-start.4 = (bf16[32,3584]{1,0:T(8,128)(2,1)S(1)}, bf16[32,3584]{1,0:T(8,128)(2,1)S(1)}, u32[]{:S(2)}, u32[]{:S(2)}) collective-permute-start(bf16[32,3584]{1,0:T(8,128)(2,1)S(1)} %slice.9), channel_id=1, source_target_pairs={{0,16},{4,20},{8,24},{12,28},{16,0},{20,4},{24,8},{28,12},{1,17},{... | collective-permute-start | bytes 688136 | tf_op jit(solution)/shard_map/ppermute | solution.py:461
  20.0 8.5 %collective-permute-start.5 = (bf16[32,3072]{1,0:T(8,128)(2,1)S(1)}, bf16[32,3072]{1,0:T(8,128)(2,1)S(1)}, u32[]{:S(2)}, u32[]{:S(2)}) collective-permute-start(bf16[32,3072]{1,0:T(8,128)(2,1)S(1)} %slice.10), channel_id=1, source_target_pairs={{0,8},{4,12},{8,0},{12,4},{16,24},{20,28},{24,16},{28,20},{1,9},{5... | collective-permute-start | bytes 589832 | tf_op jit(solution)/shard_map/ppermute | solution.py:461
  21.1 7.4 %collective-permute-start.6 = (bf16[128,128]{1,0:T(8,128)(2,1)S(1)}, bf16[128,128]{1,0:T(8,128)(2,1)S(1)}, u32[]{:S(2)}, u32[]{:S(2)}) collective-permute-start(bf16[128,128]{1,0:T(8,128)(2,1)S(1)} %pad_maximum_fusion.refs_10_), channel_id=1, source_target_pairs={{0,2},{1,3},{2,0},{3,1},{4,6},{5,7},{6,4},{7,5},{8,10},{9,11},{10,... | collective-permute-start | bytes 98312 | tf_op jit(solution)/shard_map/ppermute | solution.py:464
  28.5 3.7 %collective-permute-start.8 = (bf16[32,7168]{1,0:T(8,128)(2,1)S(1)}, bf16[32,7168]{1,0:T(8,128)(2,1)S(1)}, u32[]{:S(2)}, u32[]{:S(2)}) collective-permute-start(bf16[32,7168]{1,0:T(8,128)(2,1)S(1)} %collective-permute-done.refs_1_), channel_id=1, source_target_pairs={{0,4},{4,0},{8,12},{12,8},{16,20},{20,16},{24,28},{28,24},{1,5},{5... | collective-permute-start | bytes 1376264 | tf_op jit(solution)/shard_map/ppermute | solution.py:461
  28.6 3.6 %collective-permute-start.7 = (bf16[32,6656]{1,0:T(8,128)(2,1)S(1)}, bf16[32,6656]{1,0:T(8,128)(2,1)S(1)}, u32[]{:S(2)}, u32[]{:S(2)}) collective-permute-start(bf16[32,6656]{1,0:T(8,128)(2,1)S(1)} %get-tuple-element.89.refs_0_), channel_id=1, source_target_pairs={{0,4},{4,0},{8,12},{12,8},{16,20},{20,16},{24,28},{28,24},{1,5},{5... | collective-permute-start | bytes 1277960 | tf_op jit(solution)/shard_map/ppermute | solution.py:461
  29.1 3.1 %collective-permute-start.9 = (bf16[32,6656]{1,0:T(8,128)(2,1)S(1)}, bf16[32,6656]{1,0:T(8,128)(2,1)S(1)}, u32[]{:S(2)}, u32[]{:S(2)}) collective-permute-start(bf16[32,6656]{1,0:T(8,128)(2,1)S(1)} %collective-permute-done.1.refs_2_), channel_id=1, source_target_pairs={{0,4},{4,0},{8,12},{12,8},{16,20},{20,16},{24,28},{28,24},{1,5},{5... | collective-permute-start | bytes 1277960 | tf_op jit(solution)/shard_map/ppermute | solution.py:461
  29.2 3.1 %collective-permute-start.10 = (bf16[32,3584]{1,0:T(8,128)(2,1)S(1)}, bf16[32,3584]{1,0:T(8,128)(2,1)S(1)}, u32[]{:S(2)}, u32[]{:S(2)}) collective-permute-start(bf16[32,3584]{1,0:T(8,128)(2,1)S(1)} %collective-permute-done.4.refs_3_), channel_id=1, source_target_pairs={{0,4},{4,0},{8,12},{12,8},{16,20},{20,16},{24,28},{28,24},{1,5},{5... | collective-permute-start | bytes 688136 | tf_op jit(solution)/shard_map/ppermute | solution.py:461
  29.6 2.6 %collective-permute-start.11 = (bf16[32,3072]{1,0:T(8,128)(2,1)S(1)}, bf16[32,3072]{1,0:T(8,128)(2,1)S(1)}, u32[]{:S(2)}, u32[]{:S(2)}) collective-permute-start(bf16[32,3072]{1,0:T(8,128)(2,1)S(1)} %collective-permute-done.5.refs_4_), channel_id=1, source_target_pairs={{0,4},{4,0},{8,12},{12,8},{16,20},{20,16},{24,28},{28,24},{1,5},{5... | collective-permute-start | bytes 589832 | tf_op jit(solution)/shard_map/ppermute | solution.py:461
  34.7 7.0 %collective-permute-start.12 = (f32[4,128]{1,0:T(4,128)S(1)}, f32[4,128]{1,0:T(4,128)S(1)}, u32[]{:S(2)}, u32[]{:S(2)}) collective-permute-start(f32[4,128]{1,0:T(4,128)S(1)} %get-tuple-element.102), channel_id=1, source_target_pairs={{0,1},{1,0},{2,3},{3,2},{4,5},{5,4},{6,7},{7,6},{8,9},{9,8},{10,11... | collective-permute-start | bytes 6152 | tf_op jit(solution)/shard_map/ppermute | solution.py:464
  36.7 5.0 %collective-permute-start.13 = (f32[4,128]{1,0:T(4,128)S(1)}, f32[4,128]{1,0:T(4,128)S(1)}, u32[]{:S(2)}, u32[]{:S(2)}) collective-permute-start(f32[4,128]{1,0:T(4,128)S(1)} %get-tuple-element.103), channel_id=1, source_target_pairs={{0,2},{1,3},{2,0},{3,1},{4,6},{5,7},{6,4},{7,5},{8,10},{9,11},{10,... | collective-permute-start | bytes 6152 | tf_op jit(solution)/shard_map/ppermute | solution.py:464
  36.8 5.4 %collective-permute-start.14 = (f32[4,128]{1,0:T(4,128)S(1)}, f32[4,128]{1,0:T(4,128)S(1)}, u32[]{:S(2)}, u32[]{:S(2)}) collective-permute-start(f32[4,128]{1,0:T(4,128)S(1)} %get-tuple-element.104), channel_id=1, source_target_pairs={{0,3},{1,2},{2,1},{3,0},{4,7},{5,6},{6,5},{7,4},{8,11},{9,10},{10,... | collective-permute-start | bytes 6152 | tf_op jit(solution)/shard_map/ppermute | solution.py:464

commit v4 on v3

--- a/solution.py
+++ b/solution.py
@@ -10,7 +10,7 @@
 PTS = 4
 COST = 10**8
 SLOT = 16
-SPLIT = 5
+SPLIT = 6
 HALO = 128
 EB = 256
 WIN = EB + 2 * HALO
@@ -160,7 +160,7 @@
 
 
 def second_kernel(
-    split, links, material, before, xt, wcat, dist, dist_t, near, edge, green, acc, out, held, low, selt, vs, us, fs, sems
+    split, links, material, before, xt, wcat, dist, dist_t, near, edge, green, acc, held, low, selt, vs, us, fs, sems
 ):
     nodes = links.shape[1]
     copies = fetch(1, green, held, sems)
@@ -173,15 +173,12 @@
         starts = [b * EB for b in range(split, nodes // EB - 1)] + [0]
         windows = [lambda at=at: xt[:, at : at + WIN] for at in starts[:-1]] + [lambda: low[...]]
         run_blocks(starts, windows, links, material, wcat, dist, dist_t, selt, vs, us, fs, lambda k: (acc, starts[k]))
-        for i in range((nodes - WIN + HALO) // 128):
-            out[i * 128 : (i + 1) * 128, :] = upright(acc[:, HALO + i * 128 : HALO + (i + 1) * 128], order)
-
     for copy in copies:
         copy.wait()
 
 
 def third_kernel(
-    before, links, material, acc, xt, wcat, dist, dist_t, near, edge, out, high, last, selt, vs, us, fs, done, sem
+    links, material, acc, xt, wcat, dist, dist_t, near, edge, out, high, last, selt, vs, us, fs, done, sems
 ):
     nodes = links.shape[1]
     keep = WIN - HALO
@@ -191,13 +188,21 @@
     high[:, :keep] = xt[:, at : at + keep]
     high[:, keep:] = flip(jnp.where(even, near[:HALO, :], edge[...]), order)
     last[...] = acc[:, at : at + WIN]
+    split = nodes - keep
+    for i in range(split // 128):
+        done[i * 128 : (i + 1) * 128, :] = upright(acc[:, HALO + i * 128 : HALO + (i + 1) * 128], order)
+    copies = [
+        pltpu.make_async_copy(done.at[pl.ds(0, split), :], out.at[pl.ds(0, split), :], sems.at[0]),
+        pltpu.make_async_copy(done.at[pl.ds(split, keep), :], out.at[pl.ds(split, keep), :], sems.at[1]),
+    ]
+    copies[0].start()
     windows = [lambda: high[...]]
     run_blocks([at], windows, links, material, wcat, dist, dist_t, selt, vs, us, fs, lambda k: (last, 0))
     for i in range(keep // 128):
-        done[i * 128 : (i + 1) * 128, :] = upright(last[:, i * 128 : (i + 1) * 128], order)
-    copy = pltpu.make_async_copy(done, out.at[pl.ds(nodes - keep, keep), :], sem)
-    copy.start()
-    copy.wait()
+        done[split + i * 128 : split + (i + 1) * 128, :] = upright(last[:, i * 128 : (i + 1) * 128], order)
+    copies[1].start()
+    for copy in copies:
+        copy.wait()
 
 
 def block_scratch():
@@ -245,29 +250,28 @@
         functools.partial(second_kernel, split),
         out_shape=[
             jax.ShapeDtypeStruct(acc.shape, F32),
-            jax.ShapeDtypeStruct((nodes, 128), BF16),
             held_shape(rows, green),
         ],
         in_specs=[VMEM] * 9 + [HBM],
-        out_specs=[VMEM] * 3,
+        out_specs=[VMEM] * 2,
         scratch_shapes=[pltpu.VMEM((128, WIN), BF16)] + block_scratch() + [pltpu.SemaphoreType.DMA((rows // 2,))],
         input_output_aliases={2: 0},
         **element_params(nodes // EB - split),
     )(links, material, acc, *shared, near, edge, green)
 
 
-def third_call(before, links, material, acc, shared, near, edge):
+def third_call(links, material, acc, shared, near, edge):
+    nodes = links.shape[1]
     return pl.pallas_call(
         third_kernel,
-        out_shape=jax.ShapeDtypeStruct(before.shape, BF16),
-        in_specs=[HBM] + [VMEM] * 9,
+        out_shape=jax.ShapeDtypeStruct((nodes, 128), BF16),
+        in_specs=[VMEM] * 9,
         out_specs=HBM,
         scratch_shapes=[pltpu.VMEM((128, WIN), BF16), pltpu.VMEM((128, WIN), F32)]
         + block_scratch()
-        + [pltpu.VMEM((WIN - HALO, 128), BF16), pltpu.SemaphoreType.DMA],
-        input_output_aliases={0: 0},
+        + [pltpu.VMEM((nodes, 128), BF16), pltpu.SemaphoreType.DMA((2,))],
         **element_params(1),
-    )(before, links, material, acc, *shared, near, edge)
+    )(links, material, acc, *shared, near, edge)
 
 
 def prepare_kernel(rows, cols, *refs):
@@ -375,20 +379,21 @@
     return both
 
 
-def early_kernel(plan, green, *refs):
+def early_kernel(plan, count, green, *refs):
     high = green.shape[2]
-    refs[-1][...] = slab_sum(high, plan, green, refs[:-1], jnp.zeros((2 * high, 32), F32))
-
-
-def early_call(plan, green, messages):
+    start = refs[count][...] if len(refs) > count + 1 else jnp.zeros((2 * high, 32), F32)
+    refs[-1][...] = slab_sum(high, plan, green, refs[:count], start)
+
+
+def early_call(plan, green, messages, start=()):
     return pl.pallas_call(
-        functools.partial(early_kernel, plan),
+        functools.partial(early_kernel, plan, len(messages)),
         out_shape=jax.ShapeDtypeStruct((2 * green.shape[2], 32), F32),
-        in_specs=[VMEM] * (1 + len(messages)),
+        in_specs=[VMEM] * (1 + len(messages) + len(start)),
         out_specs=VMEM,
         compiler_params=pltpu.CompilerParams(vmem_limit_bytes=8 * 2**20),
         cost_estimate=pl.CostEstimate(flops=COST, bytes_accessed=2**20, transcendentals=0),
-    )(green, *messages)
+    )(green, *messages, *start)
 
 
 def late_kernel(rows, cols, plan, slots, green, before, *refs):
@@ -478,25 +483,29 @@
     known = [jnp.concatenate([points, near[HALO:]], axis=0)]
     while len(known) < cols // 2:
         known += [along(value, 2 * len(known)) for value in known]
-    acc, before, held_pair = second_call(rows, SPLIT, links, coeffs, acc, shared, near, edge, green)
-    own, beside, below, cross, far, known, before, held_pair = lax.optimization_barrier(
-        (own, beside, below, cross, far, known, before, held_pair)
+    there = [across(own, 1), across(beside, 1)]
+    acc, held_pair = second_call(rows, SPLIT, links, coeffs, acc, shared, near, edge, green)
+    there, acc, held_pair = lax.optimization_barrier((there, acc, held_pair))
+    plan = [(0, 0, 2 * half, 1, 0), (1, 0, half, 3, 0), (1, half + each, half, 3, half)]
+    early = early_call(plan, held_pair, there)
+    own, beside, below, cross, far, known, there, acc, held_pair, early = lax.optimization_barrier(
+        (own, beside, below, cross, far, known, there, acc, held_pair, early)
     )
     here = [own, beside, below] + cross + far
-    there = [across(value, 1) for value in here]
+    there += [across(value, 1) for value in here[2:]]
     plan = [(0, 0, 2 * half, 0, 0), (1, 0, half, 2, 0), (1, half + each, half, 2, half), (2, 0, 2 * half, 4, 0)]
     plan += [(3, 0, half, 6, 0), (4, 0, half, 6, half)]
     slots = [(0, 2 * half, 0), (1, 2 * half + each, 2), (2, 2 * half, 4), (3, half, 6)]
     for i in range(len(far)):
         plan.append((5 + i, 0, 2 * half, 8 + 2 * i, 0))
         slots.append((5 + i, 2 * half, 8 + 2 * i))
-    early = early_call(plan, held, here)
+    early = early_call(plan, held, here, (early,))
     early, there = lax.optimization_barrier((early, there))
-    plan = [(which, lane, width, k + 1, into) for which, lane, width, k, into in plan]
+    plan = [(which, lane, width, k + 1, into) for which, lane, width, k, into in plan if which > 1]
     parts = late_call(rows, cols, plan, slots, held_pair, early, here + there, known)
     sums = [along(parts[s], s) for s in range(1, cols)]
-    before, total = lax.optimization_barrier((before, parts[0]))
-    fe_out = third_call(before, links, coeffs, acc, shared, near, edge)
+    acc, total = lax.optimization_barrier((acc, parts[0]))
+    fe_out = third_call(links, coeffs, acc, shared, near, edge)
     sums, fe_out = lax.optimization_barrier((sums, fe_out))
     boundary = total
     for value in sums:

time: 42.9 us -> 41.4 us (0.965)
  Pallas kernels: 20.6 us -> 19.7 us
    pallas_call x1, Pallas kernels: 5.17 us -> 2.91 us  [second_call(): pl.pallas_call(functools.partial(second_kernel, split), out_shape=[jax.Sh...]
    pallas_call x1, Pallas kernels: 5.6 us -> 6.71 us  [first_call(): pl.pallas_call(functools.partial(first_kernel, split), out_shape=[jax.Sha...]
    pallas_call x2 -> x3, Pallas kernels: 4.26 us -> 5.32 us  [the longest x2 2.7 us: early_call(): pl.pallas_call(functools.partial(early_kernel, plan, len(messages)), out_...]
    ppermute x5, starting transfers between devices: 8.26 us -> 7.35 us  [along(): return lax.ppermute(value, 'col', [(i, i ^ s) for i in range(cols)])]
    pallas_call x1, Pallas kernels: 2.45 us -> 1.64 us  [late_call(): pl.pallas_call(functools.partial(late_kernel, rows, cols, plan, slots), o...]
    ppermute x9, starting transfers between devices: 8.66 us -> 9.44 us  [across(): return lax.ppermute(value, 'row', [(i, i ^ mask) for i in range(rows)])]
  transfers between devices with their start and end apart: 15 -> 15, of which waited for: 3 -> 5; matrix products, arithmetic and copies ran while one was open for 0% -> 0% of each run, Pallas kernels for 35% -> 36%
where the time goes in v4:
time: 41.4 us; the launch traced here: 41.3 us
  Pallas kernels  19.7 us (48%)
  starting transfers between devices  17.4 us (42%)
  waiting for transfers between devices  2.73 us (7%)
  between operations  0.77 us (2%)
  other arithmetic  0.59 us (1%)
    ppermute x9, starting transfers between devices, across(): return lax.ppermute(value, 'row', [(i, i ^ mask) for i in range(rows)])  9.44 us
    ppermute x5, starting transfers between devices, along(): return lax.ppermute(value, 'col', [(i, i ^ s) for i in range(cols)])  7.35 us
    pallas_call x1, Pallas kernels, first_call(): pl.pallas_call(functools.partial(first_kernel, split), out_shape=[jax.Sha...  6.71 us
    pallas_call x1, Pallas kernels, prepare_call(): pl.pallas_call(functools.partial(prepare_kernel, rows, cols), out_shape=[...  3.12 us
    pallas_call x1, Pallas kernels, second_call(): pl.pallas_call(functools.partial(second_kernel, split), out_shape=[jax.Sh...  2.91 us
    pallas_call x2, Pallas kernels, early_call(): pl.pallas_call(functools.partial(early_kernel, plan, len(messages)), out_...  2.7 us
    pallas_call x1, Pallas kernels, third_call(): pl.pallas_call(third_kernel, out_shape=jax.ShapeDtypeStruct((nodes, 128),...  2.62 us
    ppermute x9, waiting for transfers between devices, across(): return lax.ppermute(value, 'row', [(i, i ^ mask) for i in range(rows)])  2.48 us
  transfers between devices with their start and end apart: 15, of which 5 were waited for; matrix products, arithmetic and copies ran while one was open for 0% of the time, Pallas kernels for 36%

profile of v4, /device:TPU:0, one launch (start us, length us, event | category | flops | bytes accessed | tf_op | source)
XLA Modules:
  0.0 41.3 jit_solution(7797835182174326511)
XLA Ops:
  0.6 3.1 %shard_map.113 = (bf16[32,6656]{1,0:T(8,128)(2,1)S(1)}, bf16[32,7168]{1,0:T(8,128)(2,1)S(1)}, bf16[32,6656]{1,0:T(8,128)(2,1)S(1)}, bf16[192,128]{1,0:T(8,128)(2...) custom-call(bf16[1536,128]{1,0:T(8,128)(2,1)} %refs_0_.1, ...), custom_call_target="tpu_custom_call" | custom-call | tf_op jit(solution)/shard_map/pallas_call | solution.py:362
  3.8 3.0 %collective-permute-start = (bf16[32,7168]{1,0:T(8,128)(2,1)S(1)}, bf16[32,7168]{1,0:T(8,128)(2,1)S(1)}, u32[]{:S(2)}, u32[]{:S(2)}) collective-permute-start(bf16[32,7168]{1,0:T(8,128)(2,1)S(1)} %get-tuple-element.65), channel_id=1, source_target_pairs={{0,8},{4,12},{8,0},{12,4},{16,24},{20,28},{24,16},{28,20},{1,9},{5... | collective-permute-start | bytes 1376264 | tf_op jit(solution)/shard_map/ppermute | solution.py:466
  6.8 1.5 %collective-permute-start.1 = (bf16[32,6656]{1,0:T(8,128)(2,1)S(1)}, bf16[32,6656]{1,0:T(8,128)(2,1)S(1)}, u32[]{:S(2)}, u32[]{:S(2)}) collective-permute-start(bf16[32,6656]{1,0:T(8,128)(2,1)S(1)} %get-tuple-element.66), channel_id=1, source_target_pairs={{0,16},{4,20},{8,24},{12,28},{16,0},{20,4},{24,8},{28,12},{1,17},{... | collective-permute-start | bytes 1277960 | tf_op jit(solution)/shard_map/ppermute | solution.py:466
  8.3 1.6 %collective-permute-start.2 = (bf16[192,128]{1,0:T(8,128)(2,1)S(1)}, bf16[192,128]{1,0:T(8,128)(2,1)S(1)}, u32[]{:S(2)}, u32[]{:S(2)}) collective-permute-start(bf16[192,128]{1,0:T(8,128)(2,1)S(1)} %get-tuple-element.67), channel_id=1, source_target_pairs={{0,1},{1,0},{2,3},{3,2},{4,5},{5,4},{6,7},{7,6},{8,9},{9,8},{10,11... | collective-permute-start | bytes 147464 | tf_op jit(solution)/shard_map/ppermute | solution.py:469
  9.9 0.7 %collective-permute-start.3 = (bf16[128,128]{1,0:T(8,128)(2,1)S(1)}, bf16[128,128]{1,0:T(8,128)(2,1)S(1)}, u32[]{:S(2)}, u32[]{:S(2)}) collective-permute-start(bf16[128,128]{1,0:T(8,128)(2,1)S(1)} %get-tuple-element.68), channel_id=1, source_target_pairs={{1,2},{3,4},{5,6},{7,8},{9,10},{11,12},{13,14},{15,16},{17,18},{19... | collective-permute-start | bytes 98312 | tf_op jit(solution)/shard_map/ppermute | solution.py:476
  10.5 6.7 %shard_map.114 = (f32[128,2304]{1,0:T(8,128)S(1)}, bf16[128,2304]{1,0:T(8,128)(2,1)S(1)}, bf16[64,256]{1,0:T(8,128)(2,1)S(1)}, bf16[512,256]{1,0:T(8,128)(2,1)S(...) custom-call(bf16[2048,128]{1,0:T(8,128)(2,1)S(1)} %get-tuple-element.70.disp, ...), custom_call_target="tpu_custom_call" | custom-call | flops 500000000 | bytes 1048576 | tf_op jit(solution)/shard_map/pallas_call | solution.py:230
  17.3 0.8 %collective-permute-done.1.refs_2_ = bf16[32,6656]{1,0:T(8,128)(2,1)S(1)} collective-permute-done((bf16[32,6656]{1,0:T(8,128)(2,1)S(1)}, bf16[32,6656]{1,0:T(8,128)(2,1)S(1)}, u32[]{:S(2)}, u32[]{:S(2)}) %collective-permute-start.1) | collective-permute-done | bytes 426016 | tf_op jit(solution)/shard_map/ppermute | solution.py:466
  18.1 3.1 %collective-permute-start.8 = (bf16[32,7168]{1,0:T(8,128)(2,1)S(1)}, bf16[32,7168]{1,0:T(8,128)(2,1)S(1)}, u32[]{:S(2)}, u32[]{:S(2)}) collective-permute-start(bf16[32,7168]{1,0:T(8,128)(2,1)S(1)} %collective-permute-done.refs_1_), channel_id=1, source_target_pairs={{0,4},{4,0},{8,12},{12,8},{16,20},{20,16},{24,28},{28,24},{1,5},{5... | collective-permute-start | bytes 1376264 | tf_op jit(solution)/shard_map/ppermute | solution.py:466
  21.3 0.6 %collective-permute-start.4 = (bf16[32,3584]{1,0:T(8,128)(2,1)S(1)}, bf16[32,3584]{1,0:T(8,128)(2,1)S(1)}, u32[]{:S(2)}, u32[]{:S(2)}) collective-permute-start(bf16[32,3584]{1,0:T(8,128)(2,1)S(1)} %slice.9), channel_id=1, source_target_pairs={{0,16},{4,20},{8,24},{12,28},{16,0},{20,4},{24,8},{28,12},{1,17},{... | collective-permute-start | bytes 688136 | tf_op jit(solution)/shard_map/ppermute | solution.py:466
  21.9 0.6 %collective-permute-start.5 = (bf16[32,3072]{1,0:T(8,128)(2,1)S(1)}, bf16[32,3072]{1,0:T(8,128)(2,1)S(1)}, u32[]{:S(2)}, u32[]{:S(2)}) collective-permute-start(bf16[32,3072]{1,0:T(8,128)(2,1)S(1)} %slice.10), channel_id=1, source_target_pairs={{0,8},{4,12},{8,0},{12,4},{16,24},{20,28},{24,16},{28,20},{1,9},{5... | collective-permute-start | bytes 589832 | tf_op jit(solution)/shard_map/ppermute | solution.py:466
  22.5 1.3 %collective-permute-start.6 = (bf16[128,128]{1,0:T(8,128)(2,1)S(1)}, bf16[128,128]{1,0:T(8,128)(2,1)S(1)}, u32[]{:S(2)}, u32[]{:S(2)}) collective-permute-start(bf16[128,128]{1,0:T(8,128)(2,1)S(1)} %pad_maximum_fusion.refs_10_), channel_id=1, source_target_pairs={{0,2},{1,3},{2,0},{3,1},{4,6},{5,7},{6,4},{7,5},{8,10},{9,11},{10,... | collective-permute-start | bytes 98312 | tf_op jit(solution)/shard_map/ppermute | solution.py:469
  23.8 2.9 %shard_map.115 = (f32[128,2304]{1,0:T(8,128)S(1)}, bf16[4,2,64,6144]{3,2,1,0:T(8,128)(2,1)S(1)}) custom-call(s32[8,2048]{1,0:T(8,128)S(1)} %get-tuple-element.71.links, f32[8,2048]{1,0:T(8,128)S(1)} %get-tuple-element.73.material, f32[128,2304]{1,0:T(8,128)S(1)} %get-tuple-element.85.before, ...), custom_call_target="tpu_custom_call", output_to_operand_aliasing={{0}: (2, {})} | custom-call | flops 200000000 | bytes 1048576 | tf_op jit(solution)/shard_map/pallas_call | solution.py:249
  26.8 0.9 %shard_map.116.refs_5_ = f32[128,32]{1,0:T(8,128)S(1)} custom-call(bf16[4,2,64,6144]{3,2,1,0:T(8,128)(2,1)S(1)} %get-tuple-element.97.green, bf16[32,6656]{1,0:T(8,128)(2,1)S(1)} %collective-permute-done.7.refs_0_.refs_5_, bf16[32,7168]{1,0:T(8,128)(2,1)S(1)} %collective-permute-done.8.refs_1_.refs_6_), custom_call_target="tpu_custom_call" | custom-call | flops 100000000 | bytes 1048576 | tf_op jit(solution)/shard_map/pallas_call | solution.py:389
  27.7 1.2 %collective-permute-done.5.refs_4_ = bf16[32,3072]{1,0:T(8,128)(2,1)S(1)} collective-permute-done((bf16[32,3072]{1,0:T(8,128)(2,1)S(1)}, bf16[32,3072]{1,0:T(8,128)(2,1)S(1)}, u32[]{:S(2)}, u32[]{:S(2)}) %collective-permute-start.5) | collective-permute-done | bytes 196640 | tf_op jit(solution)/shard_map/ppermute | solution.py:466
  28.9 0.4 collective-permute-done.4.refs_3_
  29.3 0.5 %collective-permute-start.10 = (bf16[32,3584]{1,0:T(8,128)(2,1)S(1)}, bf16[32,3584]{1,0:T(8,128)(2,1)S(1)}, u32[]{:S(2)}, u32[]{:S(2)}) collective-permute-start(bf16[32,3584]{1,0:T(8,128)(2,1)S(1)} %collective-permute-done.4.refs_3_), channel_id=1, source_target_pairs={{0,4},{4,0},{8,12},{12,8},{16,20},{20,16},{24,28},{28,24},{1,5},{5... | collective-permute-start | bytes 688136 | tf_op jit(solution)/shard_map/ppermute | solution.py:466
  29.8 1.8 %shard_map.117.before = f32[128,32]{1,0:T(8,128)S(1)} custom-call(bf16[4,2,64,6144]{3,2,1,0:T(8,128)(2,1)S(1)} %get-tuple-element.98.green, bf16[32,6656]{1,0:T(8,128)(2,1)S(1)} %get-tuple-element.99.refs_0_, bf16[32,7168]{1,0:T(8,128)(2,1)S(1)} %collective-permute-done.refs_1_, bf16[32,6656]{1,0:T(8,128)(2,1)S(1)} %collective-permute-done.1.refs_2_, ...), custom_call_target="tpu_custom_call" | custom-call | flops 100000000 | bytes 1048576 | tf_op jit(solution)/shard_map/pallas_call | solution.py:389
  31.7 1.6 %shard_map.118 = (f32[4,128]{1,0:T(4,128)S(1)}, f32[4,128]{1,0:T(4,128)S(1)}, f32[4,128]{1,0:T(4,128)S(1)}, f32[4,128]{1,0:T(4,128)S(1)}) custom-call(bf16[4,2,64,6144]{3,2,1,0:T(8,128)(2,1)S(1)} %get-tuple-element.97.green, f32[128,32]{1,0:T(8,128)S(1)} %shard_map.117.before, bf16[32,6656]{1,0:T(8,128)(2,1)S(1)} %get-tuple-element.99.refs_0_, ...), custom_call_target="tpu_custom_call" | custom-call | flops 100000000 | bytes 1048576 | tf_op jit(solution)/shard_map/pallas_call | solution.py:439
  33.3 0.7 %collective-permute-start.12 = (f32[4,128]{1,0:T(4,128)S(1)}, f32[4,128]{1,0:T(4,128)S(1)}, u32[]{:S(2)}, u32[]{:S(2)}) collective-permute-start(f32[4,128]{1,0:T(4,128)S(1)} %get-tuple-element.115), channel_id=1, source_target_pairs={{0,1},{1,0},{2,3},{3,2},{4,5},{5,4},{6,7},{7,6},{8,9},{9,8},{10,11... | collective-permute-start | bytes 6152 | tf_op jit(solution)/shard_map/ppermute | solution.py:469
  34.0 1.3 %collective-permute-start.13 = (f32[4,128]{1,0:T(4,128)S(1)}, f32[4,128]{1,0:T(4,128)S(1)}, u32[]{:S(2)}, u32[]{:S(2)}) collective-permute-start(f32[4,128]{1,0:T(4,128)S(1)} %get-tuple-element.116), channel_id=1, source_target_pairs={{0,2},{1,3},{2,0},{3,1},{4,6},{5,7},{6,4},{7,5},{8,10},{9,11},{10,... | collective-permute-start | bytes 6152 | tf_op jit(solution)/shard_map/ppermute | solution.py:469
  35.3 2.5 %collective-permute-start.14 = (f32[4,128]{1,0:T(4,128)S(1)}, f32[4,128]{1,0:T(4,128)S(1)}, u32[]{:S(2)}, u32[]{:S(2)}) collective-permute-start(f32[4,128]{1,0:T(4,128)S(1)} %get-tuple-element.117), channel_id=1, source_target_pairs={{0,3},{1,2},{2,1},{3,0},{4,7},{5,6},{6,5},{7,4},{8,11},{9,10},{10,... | collective-permute-start | bytes 6152 | tf_op jit(solution)/shard_map/ppermute | solution.py:469
  37.8 2.6 %shard_map.119 = bf16[2048,128]{1,0:T(8,128)(2,1)} custom-call(s32[8,2048]{1,0:T(8,128)S(1)} %get-tuple-element.71.links, f32[8,2048]{1,0:T(8,128)S(1)} %get-tuple-element.73.material, f32[128,2304]{1,0:T(8,128)S(1)} %get-tuple-element.120.acc, bf16[128,2304]{1,0:T(8,128)(2,1)S(1)} %get-tuple-element.86.xt, bf16[64,256]{1,0:T(8,128)(2,1)S(1)} %get-tuple-element.87.wcat, ...), custom_call_target="tpu_custom_call" | custom-call | flops 100000000 | bytes 1048576 | tf_op jit(solution)/shard_map/pallas_call | solution.py:265
  40.4 0.2 collective-permute-done.14
  40.7 0.6 %add_add_fusion = f32[4,128]{1,0:T(4,128)} fusion(f32[4,128]{1,0:T(4,128)S(1)} %collective-permute-done.14, f32[4,128]{1,0:T(4,128)S(1)} %collective-permute-done.13, f32[4,128]{1,0:T(4,128)S(1)} %get-tuple-element.122, f32[4,128]{1,0:T(4,128)S(1)} %collective-permute-done.12), kind=kLoop, calls=%fused_computation.1 | loop fusion | flops 1536 | bytes 10240 | tf_op jit(solution)/shard_map/add | solution.py:512
  (18 shorter events, 0.3 us)
Async XLA Ops:
  3.8 14.3 %collective-permute-start = (bf16[32,7168]{1,0:T(8,128)(2,1)S(1)}, bf16[32,7168]{1,0:T(8,128)(2,1)S(1)}, u32[]{:S(2)}, u32[]{:S(2)}) collective-permute-start(bf16[32,7168]{1,0:T(8,128)(2,1)S(1)} %get-tuple-element.65), channel_id=1, source_target_pairs={{0,8},{4,12},{8,0},{12,4},{16,24},{20,28},{24,16},{28,20},{1,9},{5... | collective-permute-start | bytes 1376264 | tf_op jit(solution)/shard_map/ppermute | solution.py:466
  6.8 11.3 %collective-permute-start.1 = (bf16[32,6656]{1,0:T(8,128)(2,1)S(1)}, bf16[32,6656]{1,0:T(8,128)(2,1)S(1)}, u32[]{:S(2)}, u32[]{:S(2)}) collective-permute-start(bf16[32,6656]{1,0:T(8,128)(2,1)S(1)} %get-tuple-element.66), channel_id=1, source_target_pairs={{0,16},{4,20},{8,24},{12,28},{16,0},{20,4},{24,8},{28,12},{1,17},{... | collective-permute-start | bytes 1277960 | tf_op jit(solution)/shard_map/ppermute | solution.py:466
  8.3 9.0 %collective-permute-start.2 = (bf16[192,128]{1,0:T(8,128)(2,1)S(1)}, bf16[192,128]{1,0:T(8,128)(2,1)S(1)}, u32[]{:S(2)}, u32[]{:S(2)}) collective-permute-start(bf16[192,128]{1,0:T(8,128)(2,1)S(1)} %get-tuple-element.67), channel_id=1, source_target_pairs={{0,1},{1,0},{2,3},{3,2},{4,5},{5,4},{6,7},{7,6},{8,9},{9,8},{10,11... | collective-permute-start | bytes 147464 | tf_op jit(solution)/shard_map/ppermute | solution.py:469
  9.9 7.4 %collective-permute-start.3 = (bf16[128,128]{1,0:T(8,128)(2,1)S(1)}, bf16[128,128]{1,0:T(8,128)(2,1)S(1)}, u32[]{:S(2)}, u32[]{:S(2)}) collective-permute-start(bf16[128,128]{1,0:T(8,128)(2,1)S(1)} %get-tuple-element.68), channel_id=1, source_target_pairs={{1,2},{3,4},{5,6},{7,8},{9,10},{11,12},{13,14},{15,16},{17,18},{19... | collective-permute-start | bytes 98312 | tf_op jit(solution)/shard_map/ppermute | solution.py:476
  18.1 8.7 %collective-permute-start.8 = (bf16[32,7168]{1,0:T(8,128)(2,1)S(1)}, bf16[32,7168]{1,0:T(8,128)(2,1)S(1)}, u32[]{:S(2)}, u32[]{:S(2)}) collective-permute-start(bf16[32,7168]{1,0:T(8,128)(2,1)S(1)} %collective-permute-done.refs_1_), channel_id=1, source_target_pairs={{0,4},{4,0},{8,12},{12,8},{16,20},{20,16},{24,28},{28,24},{1,5},{5... | collective-permute-start | bytes 1376264 | tf_op jit(solution)/shard_map/ppermute | solution.py:466
  21.2 5.6 %collective-permute-start.7 = (bf16[32,6656]{1,0:T(8,128)(2,1)S(1)}, bf16[32,6656]{1,0:T(8,128)(2,1)S(1)}, u32[]{:S(2)}, u32[]{:S(2)}) collective-permute-start(bf16[32,6656]{1,0:T(8,128)(2,1)S(1)} %get-tuple-element.99.refs_0_), channel_id=1, source_target_pairs={{0,4},{4,0},{8,12},{12,8},{16,20},{20,16},{24,28},{28,24},{1,5},{5... | collective-permute-start | bytes 1277960 | tf_op jit(solution)/shard_map/ppermute | solution.py:466
  21.3 8.0 %collective-permute-start.4 = (bf16[32,3584]{1,0:T(8,128)(2,1)S(1)}, bf16[32,3584]{1,0:T(8,128)(2,1)S(1)}, u32[]{:S(2)}, u32[]{:S(2)}) collective-permute-start(bf16[32,3584]{1,0:T(8,128)(2,1)S(1)} %slice.9), channel_id=1, source_target_pairs={{0,16},{4,20},{8,24},{12,28},{16,0},{20,4},{24,8},{28,12},{1,17},{... | collective-permute-start | bytes 688136 | tf_op jit(solution)/shard_map/ppermute | solution.py:466
  21.9 7.0 %collective-permute-start.5 = (bf16[32,3072]{1,0:T(8,128)(2,1)S(1)}, bf16[32,3072]{1,0:T(8,128)(2,1)S(1)}, u32[]{:S(2)}, u32[]{:S(2)}) collective-permute-start(bf16[32,3072]{1,0:T(8,128)(2,1)S(1)} %slice.10), channel_id=1, source_target_pairs={{0,8},{4,12},{8,0},{12,4},{16,24},{20,28},{24,16},{28,20},{1,9},{5... | collective-permute-start | bytes 589832 | tf_op jit(solution)/shard_map/ppermute | solution.py:466
  22.5 5.2 %collective-permute-start.6 = (bf16[128,128]{1,0:T(8,128)(2,1)S(1)}, bf16[128,128]{1,0:T(8,128)(2,1)S(1)}, u32[]{:S(2)}, u32[]{:S(2)}) collective-permute-start(bf16[128,128]{1,0:T(8,128)(2,1)S(1)} %pad_maximum_fusion.refs_10_), channel_id=1, source_target_pairs={{0,2},{1,3},{2,0},{3,1},{4,6},{5,7},{6,4},{7,5},{8,10},{9,11},{10,... | collective-permute-start | bytes 98312 | tf_op jit(solution)/shard_map/ppermute | solution.py:469
  29.3 2.4 %collective-permute-start.9 = (bf16[32,6656]{1,0:T(8,128)(2,1)S(1)}, bf16[32,6656]{1,0:T(8,128)(2,1)S(1)}, u32[]{:S(2)}, u32[]{:S(2)}) collective-permute-start(bf16[32,6656]{1,0:T(8,128)(2,1)S(1)} %collective-permute-done.1.refs_2_), channel_id=1, source_target_pairs={{0,4},{4,0},{8,12},{12,8},{16,20},{20,16},{24,28},{28,24},{1,5},{5... | collective-permute-start | bytes 1277960 | tf_op jit(solution)/shard_map/ppermute | solution.py:466
  29.3 2.4 %collective-permute-start.10 = (bf16[32,3584]{1,0:T(8,128)(2,1)S(1)}, bf16[32,3584]{1,0:T(8,128)(2,1)S(1)}, u32[]{:S(2)}, u32[]{:S(2)}) collective-permute-start(bf16[32,3584]{1,0:T(8,128)(2,1)S(1)} %collective-permute-done.4.refs_3_), channel_id=1, source_target_pairs={{0,4},{4,0},{8,12},{12,8},{16,20},{20,16},{24,28},{28,24},{1,5},{5... | collective-permute-start | bytes 688136 | tf_op jit(solution)/shard_map/ppermute | solution.py:466
  29.8 1.9 %collective-permute-start.11 = (bf16[32,3072]{1,0:T(8,128)(2,1)S(1)}, bf16[32,3072]{1,0:T(8,128)(2,1)S(1)}, u32[]{:S(2)}, u32[]{:S(2)}) collective-permute-start(bf16[32,3072]{1,0:T(8,128)(2,1)S(1)} %collective-permute-done.5.refs_4_), channel_id=1, source_target_pairs={{0,4},{4,0},{8,12},{12,8},{16,20},{20,16},{24,28},{28,24},{1,5},{5... | collective-permute-start | bytes 589832 | tf_op jit(solution)/shard_map/ppermute | solution.py:466
  33.3 7.1 %collective-permute-start.12 = (f32[4,128]{1,0:T(4,128)S(1)}, f32[4,128]{1,0:T(4,128)S(1)}, u32[]{:S(2)}, u32[]{:S(2)}) collective-permute-start(f32[4,128]{1,0:T(4,128)S(1)} %get-tuple-element.115), channel_id=1, source_target_pairs={{0,1},{1,0},{2,3},{3,2},{4,5},{5,4},{6,7},{7,6},{8,9},{9,8},{10,11... | collective-permute-start | bytes 6152 | tf_op jit(solution)/shard_map/ppermute | solution.py:469
  34.0 6.4 %collective-permute-start.13 = (f32[4,128]{1,0:T(4,128)S(1)}, f32[4,128]{1,0:T(4,128)S(1)}, u32[]{:S(2)}, u32[]{:S(2)}) collective-permute-start(f32[4,128]{1,0:T(4,128)S(1)} %get-tuple-element.116), channel_id=1, source_target_pairs={{0,2},{1,3},{2,0},{3,1},{4,6},{5,7},{6,4},{7,5},{8,10},{9,11},{10,... | collective-permute-start | bytes 6152 | tf_op jit(solution)/shard_map/ppermute | solution.py:469
  35.3 5.4 %collective-permute-start.14 = (f32[4,128]{1,0:T(4,128)S(1)}, f32[4,128]{1,0:T(4,128)S(1)}, u32[]{:S(2)}, u32[]{:S(2)}) collective-permute-start(f32[4,128]{1,0:T(4,128)S(1)} %get-tuple-element.117), channel_id=1, source_target_pairs={{0,3},{1,2},{2,1},{3,0},{4,7},{5,6},{6,5},{7,4},{8,11},{9,10},{10,... | collective-permute-start | bytes 6152 | tf_op jit(solution)/shard_map/ppermute | solution.py:469

commit v5 on v4

--- a/solution.py
+++ b/solution.py
@@ -295,13 +295,13 @@
     ]
     for copy in copies + others:
         copy.start()
+    for copy in copies + others:
+        copy.wait()
 
     gap = cols * SLOT * 8
     widen = (iota((128, 512), 1) // 4 == iota((128, 512), 0)).astype(BF16)
     comp = iota((32, 512), 1) % 4
     for i in range(lines // 128):
-        if i * 128 % share == 0:
-            copies[i * 128 // share].wait()
         wide = jnp.dot(traction[i * 128 : (i + 1) * 128, :].astype(F32).T.astype(BF16), widen, preferred_element_type=F32)
         line = wide[:32]
         for k in range(1, 4):
@@ -313,8 +313,6 @@
                 into = lane + gap if k == 1 and lane >= lines * 2 else lane
                 message[:, into : into + 256] = line[:, t * 256 : (t + 1) * 256]
 
-    for copy in others:
-        copy.wait()
     tail, head = disp[disp.shape[0] - HALO :, :], disp[:HALO, :]
     even = col % 2 == 0
     near[:HALO, :] = jnp.where(even, tail, head)

time: 41.4 us -> 41.3 us (level)
  no operation moved by 1% of the time
where the time goes in v5:
time: 41.3 us; the launch traced here: 41.1 us
  Pallas kernels  19.6 us (47%)
  starting transfers between devices  17.5 us (42%)
  waiting for transfers between devices  2.71 us (7%)
  between operations  0.77 us (2%)
  other arithmetic  0.59 us (1%)
    ppermute x9, starting transfers between devices, across(): return lax.ppermute(value, 'row', [(i, i ^ mask) for i in range(rows)])  9.44 us
    ppermute x5, starting transfers between devices, along(): return lax.ppermute(value, 'col', [(i, i ^ s) for i in range(cols)])  7.36 us
    pallas_call x1, Pallas kernels, first_call(): pl.pallas_call(functools.partial(first_kernel, split), out_shape=[jax.Sha...  6.72 us
    pallas_call x1, Pallas kernels, prepare_call(): pl.pallas_call(functools.partial(prepare_kernel, rows, cols), out_shape=[...  2.97 us
    pallas_call x1, Pallas kernels, second_call(): pl.pallas_call(functools.partial(second_kernel, split), out_shape=[jax.Sh...  2.91 us
    pallas_call x2, Pallas kernels, early_call(): pl.pallas_call(functools.partial(early_kernel, plan, len(messages)), out_...  2.7 us
    pallas_call x1, Pallas kernels, third_call(): pl.pallas_call(third_kernel, out_shape=jax.ShapeDtypeStruct((nodes, 128),...  2.62 us
    ppermute x9, waiting for transfers between devices, across(): return lax.ppermute(value, 'row', [(i, i ^ mask) for i in range(rows)])  2.47 us
  transfers between devices with their start and end apart: 15, of which 5 were waited for; matrix products, arithmetic and copies ran while one was open for 0% of the time, Pallas kernels for 36%

profile of v5, /device:TPU:0, one launch (start us, length us, event | category | flops | bytes accessed | tf_op | source)
XLA Modules:
  0.0 41.1 jit_solution(17270599818405805196)
XLA Ops:
  0.6 3.0 %shard_map.113 = (bf16[32,6656]{1,0:T(8,128)(2,1)S(1)}, bf16[32,7168]{1,0:T(8,128)(2,1)S(1)}, bf16[32,6656]{1,0:T(8,128)(2,1)S(1)}, bf16[192,128]{1,0:T(8,128)(2...) custom-call(bf16[1536,128]{1,0:T(8,128)(2,1)} %refs_0_.1, ...), custom_call_target="tpu_custom_call" | custom-call | tf_op jit(solution)/shard_map/pallas_call | solution.py:360
  3.6 3.0 %collective-permute-start = (bf16[32,7168]{1,0:T(8,128)(2,1)S(1)}, bf16[32,7168]{1,0:T(8,128)(2,1)S(1)}, u32[]{:S(2)}, u32[]{:S(2)}) collective-permute-start(bf16[32,7168]{1,0:T(8,128)(2,1)S(1)} %get-tuple-element.65), channel_id=1, source_target_pairs={{0,8},{4,12},{8,0},{12,4},{16,24},{20,28},{24,16},{28,20},{1,9},{5... | collective-permute-start | bytes 1376264 | tf_op jit(solution)/shard_map/ppermute | solution.py:464
  6.6 1.5 %collective-permute-start.1 = (bf16[32,6656]{1,0:T(8,128)(2,1)S(1)}, bf16[32,6656]{1,0:T(8,128)(2,1)S(1)}, u32[]{:S(2)}, u32[]{:S(2)}) collective-permute-start(bf16[32,6656]{1,0:T(8,128)(2,1)S(1)} %get-tuple-element.66), channel_id=1, source_target_pairs={{0,16},{4,20},{8,24},{12,28},{16,0},{20,4},{24,8},{28,12},{1,17},{... | collective-permute-start | bytes 1277960 | tf_op jit(solution)/shard_map/ppermute | solution.py:464
  8.1 1.6 %collective-permute-start.2 = (bf16[192,128]{1,0:T(8,128)(2,1)S(1)}, bf16[192,128]{1,0:T(8,128)(2,1)S(1)}, u32[]{:S(2)}, u32[]{:S(2)}) collective-permute-start(bf16[192,128]{1,0:T(8,128)(2,1)S(1)} %get-tuple-element.67), channel_id=1, source_target_pairs={{0,1},{1,0},{2,3},{3,2},{4,5},{5,4},{6,7},{7,6},{8,9},{9,8},{10,11... | collective-permute-start | bytes 147464 | tf_op jit(solution)/shard_map/ppermute | solution.py:467
  9.7 0.7 %collective-permute-start.3 = (bf16[128,128]{1,0:T(8,128)(2,1)S(1)}, bf16[128,128]{1,0:T(8,128)(2,1)S(1)}, u32[]{:S(2)}, u32[]{:S(2)}) collective-permute-start(bf16[128,128]{1,0:T(8,128)(2,1)S(1)} %get-tuple-element.68), channel_id=1, source_target_pairs={{1,2},{3,4},{5,6},{7,8},{9,10},{11,12},{13,14},{15,16},{17,18},{19... | collective-permute-start | bytes 98312 | tf_op jit(solution)/shard_map/ppermute | solution.py:474
  10.4 6.7 %shard_map.114 = (f32[128,2304]{1,0:T(8,128)S(1)}, bf16[128,2304]{1,0:T(8,128)(2,1)S(1)}, bf16[64,256]{1,0:T(8,128)(2,1)S(1)}, bf16[512,256]{1,0:T(8,128)(2,1)S(...) custom-call(bf16[2048,128]{1,0:T(8,128)(2,1)S(1)} %get-tuple-element.70.disp, ...), custom_call_target="tpu_custom_call" | custom-call | flops 500000000 | bytes 1048576 | tf_op jit(solution)/shard_map/pallas_call | solution.py:230
  17.1 0.8 %collective-permute-done.1.refs_2_ = bf16[32,6656]{1,0:T(8,128)(2,1)S(1)} collective-permute-done((bf16[32,6656]{1,0:T(8,128)(2,1)S(1)}, bf16[32,6656]{1,0:T(8,128)(2,1)S(1)}, u32[]{:S(2)}, u32[]{:S(2)}) %collective-permute-start.1) | collective-permute-done | bytes 426016 | tf_op jit(solution)/shard_map/ppermute | solution.py:464
  17.9 3.1 %collective-permute-start.8 = (bf16[32,7168]{1,0:T(8,128)(2,1)S(1)}, bf16[32,7168]{1,0:T(8,128)(2,1)S(1)}, u32[]{:S(2)}, u32[]{:S(2)}) collective-permute-start(bf16[32,7168]{1,0:T(8,128)(2,1)S(1)} %collective-permute-done.refs_1_), channel_id=1, source_target_pairs={{0,4},{4,0},{8,12},{12,8},{16,20},{20,16},{24,28},{28,24},{1,5},{5... | collective-permute-start | bytes 1376264 | tf_op jit(solution)/shard_map/ppermute | solution.py:464
  21.1 0.6 %collective-permute-start.4 = (bf16[32,3584]{1,0:T(8,128)(2,1)S(1)}, bf16[32,3584]{1,0:T(8,128)(2,1)S(1)}, u32[]{:S(2)}, u32[]{:S(2)}) collective-permute-start(bf16[32,3584]{1,0:T(8,128)(2,1)S(1)} %slice.9), channel_id=1, source_target_pairs={{0,16},{4,20},{8,24},{12,28},{16,0},{20,4},{24,8},{28,12},{1,17},{... | collective-permute-start | bytes 688136 | tf_op jit(solution)/shard_map/ppermute | solution.py:464
  21.7 0.6 %collective-permute-start.5 = (bf16[32,3072]{1,0:T(8,128)(2,1)S(1)}, bf16[32,3072]{1,0:T(8,128)(2,1)S(1)}, u32[]{:S(2)}, u32[]{:S(2)}) collective-permute-start(bf16[32,3072]{1,0:T(8,128)(2,1)S(1)} %slice.10), channel_id=1, source_target_pairs={{0,8},{4,12},{8,0},{12,4},{16,24},{20,28},{24,16},{28,20},{1,9},{5... | collective-permute-start | bytes 589832 | tf_op jit(solution)/shard_map/ppermute | solution.py:464
  22.3 1.3 %collective-permute-start.6 = (bf16[128,128]{1,0:T(8,128)(2,1)S(1)}, bf16[128,128]{1,0:T(8,128)(2,1)S(1)}, u32[]{:S(2)}, u32[]{:S(2)}) collective-permute-start(bf16[128,128]{1,0:T(8,128)(2,1)S(1)} %pad_maximum_fusion.refs_10_), channel_id=1, source_target_pairs={{0,2},{1,3},{2,0},{3,1},{4,6},{5,7},{6,4},{7,5},{8,10},{9,11},{10,... | collective-permute-start | bytes 98312 | tf_op jit(solution)/shard_map/ppermute | solution.py:467
  23.7 2.9 %shard_map.115 = (f32[128,2304]{1,0:T(8,128)S(1)}, bf16[4,2,64,6144]{3,2,1,0:T(8,128)(2,1)S(1)}) custom-call(s32[8,2048]{1,0:T(8,128)S(1)} %get-tuple-element.71.links, f32[8,2048]{1,0:T(8,128)S(1)} %get-tuple-element.73.material, f32[128,2304]{1,0:T(8,128)S(1)} %get-tuple-element.85.before, ...), custom_call_target="tpu_custom_call", output_to_operand_aliasing={{0}: (2, {})} | custom-call | flops 200000000 | bytes 1048576 | tf_op jit(solution)/shard_map/pallas_call | solution.py:249
  26.6 0.9 %shard_map.116.refs_5_ = f32[128,32]{1,0:T(8,128)S(1)} custom-call(bf16[4,2,64,6144]{3,2,1,0:T(8,128)(2,1)S(1)} %get-tuple-element.97.green, bf16[32,6656]{1,0:T(8,128)(2,1)S(1)} %collective-permute-done.7.refs_0_.refs_5_, bf16[32,7168]{1,0:T(8,128)(2,1)S(1)} %collective-permute-done.8.refs_1_.refs_6_), custom_call_target="tpu_custom_call" | custom-call | flops 100000000 | bytes 1048576 | tf_op jit(solution)/shard_map/pallas_call | solution.py:387
  27.6 1.2 %collective-permute-done.5.refs_4_ = bf16[32,3072]{1,0:T(8,128)(2,1)S(1)} collective-permute-done((bf16[32,3072]{1,0:T(8,128)(2,1)S(1)}, bf16[32,3072]{1,0:T(8,128)(2,1)S(1)}, u32[]{:S(2)}, u32[]{:S(2)}) %collective-permute-start.5) | collective-permute-done | bytes 196640 | tf_op jit(solution)/shard_map/ppermute | solution.py:464
  28.8 0.4 collective-permute-done.4.refs_3_
  29.2 0.5 %collective-permute-start.10 = (bf16[32,3584]{1,0:T(8,128)(2,1)S(1)}, bf16[32,3584]{1,0:T(8,128)(2,1)S(1)}, u32[]{:S(2)}, u32[]{:S(2)}) collective-permute-start(bf16[32,3584]{1,0:T(8,128)(2,1)S(1)} %collective-permute-done.4.refs_3_), channel_id=1, source_target_pairs={{0,4},{4,0},{8,12},{12,8},{16,20},{20,16},{24,28},{28,24},{1,5},{5... | collective-permute-start | bytes 688136 | tf_op jit(solution)/shard_map/ppermute | solution.py:464
  29.7 1.8 %shard_map.117.before = f32[128,32]{1,0:T(8,128)S(1)} custom-call(bf16[4,2,64,6144]{3,2,1,0:T(8,128)(2,1)S(1)} %get-tuple-element.98.green, bf16[32,6656]{1,0:T(8,128)(2,1)S(1)} %get-tuple-element.99.refs_0_, bf16[32,7168]{1,0:T(8,128)(2,1)S(1)} %collective-permute-done.refs_1_, bf16[32,6656]{1,0:T(8,128)(2,1)S(1)} %collective-permute-done.1.refs_2_, ...), custom_call_target="tpu_custom_call" | custom-call | flops 100000000 | bytes 1048576 | tf_op jit(solution)/shard_map/pallas_call | solution.py:387
  31.5 1.6 %shard_map.118 = (f32[4,128]{1,0:T(4,128)S(1)}, f32[4,128]{1,0:T(4,128)S(1)}, f32[4,128]{1,0:T(4,128)S(1)}, f32[4,128]{1,0:T(4,128)S(1)}) custom-call(bf16[4,2,64,6144]{3,2,1,0:T(8,128)(2,1)S(1)} %get-tuple-element.97.green, f32[128,32]{1,0:T(8,128)S(1)} %shard_map.117.before, bf16[32,6656]{1,0:T(8,128)(2,1)S(1)} %get-tuple-element.99.refs_0_, ...), custom_call_target="tpu_custom_call" | custom-call | flops 100000000 | bytes 1048576 | tf_op jit(solution)/shard_map/pallas_call | solution.py:437
  33.2 0.7 %collective-permute-start.12 = (f32[4,128]{1,0:T(4,128)S(1)}, f32[4,128]{1,0:T(4,128)S(1)}, u32[]{:S(2)}, u32[]{:S(2)}) collective-permute-start(f32[4,128]{1,0:T(4,128)S(1)} %get-tuple-element.115), channel_id=1, source_target_pairs={{0,1},{1,0},{2,3},{3,2},{4,5},{5,4},{6,7},{7,6},{8,9},{9,8},{10,11... | collective-permute-start | bytes 6152 | tf_op jit(solution)/shard_map/ppermute | solution.py:467
  33.9 1.3 %collective-permute-start.13 = (f32[4,128]{1,0:T(4,128)S(1)}, f32[4,128]{1,0:T(4,128)S(1)}, u32[]{:S(2)}, u32[]{:S(2)}) collective-permute-start(f32[4,128]{1,0:T(4,128)S(1)} %get-tuple-element.116), channel_id=1, source_target_pairs={{0,2},{1,3},{2,0},{3,1},{4,6},{5,7},{6,4},{7,5},{8,10},{9,11},{10,... | collective-permute-start | bytes 6152 | tf_op jit(solution)/shard_map/ppermute | solution.py:467
  35.1 2.5 %collective-permute-start.14 = (f32[4,128]{1,0:T(4,128)S(1)}, f32[4,128]{1,0:T(4,128)S(1)}, u32[]{:S(2)}, u32[]{:S(2)}) collective-permute-start(f32[4,128]{1,0:T(4,128)S(1)} %get-tuple-element.117), channel_id=1, source_target_pairs={{0,3},{1,2},{2,1},{3,0},{4,7},{5,6},{6,5},{7,4},{8,11},{9,10},{10,... | collective-permute-start | bytes 6152 | tf_op jit(solution)/shard_map/ppermute | solution.py:467
  37.6 2.6 %shard_map.119 = bf16[2048,128]{1,0:T(8,128)(2,1)} custom-call(s32[8,2048]{1,0:T(8,128)S(1)} %get-tuple-element.71.links, f32[8,2048]{1,0:T(8,128)S(1)} %get-tuple-element.73.material, f32[128,2304]{1,0:T(8,128)S(1)} %get-tuple-element.120.acc, bf16[128,2304]{1,0:T(8,128)(2,1)S(1)} %get-tuple-element.86.xt, bf16[64,256]{1,0:T(8,128)(2,1)S(1)} %get-tuple-element.87.wcat, ...), custom_call_target="tpu_custom_call" | custom-call | flops 100000000 | bytes 1048576 | tf_op jit(solution)/shard_map/pallas_call | solution.py:265
  40.3 0.2 collective-permute-done.14
  40.5 0.6 %add_add_fusion = f32[4,128]{1,0:T(4,128)} fusion(f32[4,128]{1,0:T(4,128)S(1)} %collective-permute-done.14, f32[4,128]{1,0:T(4,128)S(1)} %collective-permute-done.13, f32[4,128]{1,0:T(4,128)S(1)} %get-tuple-element.122, f32[4,128]{1,0:T(4,128)S(1)} %collective-permute-done.12), kind=kLoop, calls=%fused_computation.1 | loop fusion | flops 1536 | bytes 10240 | tf_op jit(solution)/shard_map/add | solution.py:510
  (18 shorter events, 0.3 us)
Async XLA Ops:
  3.6 14.3 %collective-permute-start = (bf16[32,7168]{1,0:T(8,128)(2,1)S(1)}, bf16[32,7168]{1,0:T(8,128)(2,1)S(1)}, u32[]{:S(2)}, u32[]{:S(2)}) collective-permute-start(bf16[32,7168]{1,0:T(8,128)(2,1)S(1)} %get-tuple-element.65), channel_id=1, source_target_pairs={{0,8},{4,12},{8,0},{12,4},{16,24},{20,28},{24,16},{28,20},{1,9},{5... | collective-permute-start | bytes 1376264 | tf_op jit(solution)/shard_map/ppermute | solution.py:464
  6.6 11.3 %collective-permute-start.1 = (bf16[32,6656]{1,0:T(8,128)(2,1)S(1)}, bf16[32,6656]{1,0:T(8,128)(2,1)S(1)}, u32[]{:S(2)}, u32[]{:S(2)}) collective-permute-start(bf16[32,6656]{1,0:T(8,128)(2,1)S(1)} %get-tuple-element.66), channel_id=1, source_target_pairs={{0,16},{4,20},{8,24},{12,28},{16,0},{20,4},{24,8},{28,12},{1,17},{... | collective-permute-start | bytes 1277960 | tf_op jit(solution)/shard_map/ppermute | solution.py:464
  8.1 9.0 %collective-permute-start.2 = (bf16[192,128]{1,0:T(8,128)(2,1)S(1)}, bf16[192,128]{1,0:T(8,128)(2,1)S(1)}, u32[]{:S(2)}, u32[]{:S(2)}) collective-permute-start(bf16[192,128]{1,0:T(8,128)(2,1)S(1)} %get-tuple-element.67), channel_id=1, source_target_pairs={{0,1},{1,0},{2,3},{3,2},{4,5},{5,4},{6,7},{7,6},{8,9},{9,8},{10,11... | collective-permute-start | bytes 147464 | tf_op jit(solution)/shard_map/ppermute | solution.py:467
  9.7 7.4 %collective-permute-start.3 = (bf16[128,128]{1,0:T(8,128)(2,1)S(1)}, bf16[128,128]{1,0:T(8,128)(2,1)S(1)}, u32[]{:S(2)}, u32[]{:S(2)}) collective-permute-start(bf16[128,128]{1,0:T(8,128)(2,1)S(1)} %get-tuple-element.68), channel_id=1, source_target_pairs={{1,2},{3,4},{5,6},{7,8},{9,10},{11,12},{13,14},{15,16},{17,18},{19... | collective-permute-start | bytes 98312 | tf_op jit(solution)/shard_map/ppermute | solution.py:474
  17.9 8.7 %collective-permute-start.8 = (bf16[32,7168]{1,0:T(8,128)(2,1)S(1)}, bf16[32,7168]{1,0:T(8,128)(2,1)S(1)}, u32[]{:S(2)}, u32[]{:S(2)}) collective-permute-start(bf16[32,7168]{1,0:T(8,128)(2,1)S(1)} %collective-permute-done.refs_1_), channel_id=1, source_target_pairs={{0,4},{4,0},{8,12},{12,8},{16,20},{20,16},{24,28},{28,24},{1,5},{5... | collective-permute-start | bytes 1376264 | tf_op jit(solution)/shard_map/ppermute | solution.py:464
  21.0 5.6 %collective-permute-start.7 = (bf16[32,6656]{1,0:T(8,128)(2,1)S(1)}, bf16[32,6656]{1,0:T(8,128)(2,1)S(1)}, u32[]{:S(2)}, u32[]{:S(2)}) collective-permute-start(bf16[32,6656]{1,0:T(8,128)(2,1)S(1)} %get-tuple-element.99.refs_0_), channel_id=1, source_target_pairs={{0,4},{4,0},{8,12},{12,8},{16,20},{20,16},{24,28},{28,24},{1,5},{5... | collective-permute-start | bytes 1277960 | tf_op jit(solution)/shard_map/ppermute | solution.py:464
  21.1 8.0 %collective-permute-start.4 = (bf16[32,3584]{1,0:T(8,128)(2,1)S(1)}, bf16[32,3584]{1,0:T(8,128)(2,1)S(1)}, u32[]{:S(2)}, u32[]{:S(2)}) collective-permute-start(bf16[32,3584]{1,0:T(8,128)(2,1)S(1)} %slice.9), channel_id=1, source_target_pairs={{0,16},{4,20},{8,24},{12,28},{16,0},{20,4},{24,8},{28,12},{1,17},{... | collective-permute-start | bytes 688136 | tf_op jit(solution)/shard_map/ppermute | solution.py:464
  21.7 7.0 %collective-permute-start.5 = (bf16[32,3072]{1,0:T(8,128)(2,1)S(1)}, bf16[32,3072]{1,0:T(8,128)(2,1)S(1)}, u32[]{:S(2)}, u32[]{:S(2)}) collective-permute-start(bf16[32,3072]{1,0:T(8,128)(2,1)S(1)} %slice.10), channel_id=1, source_target_pairs={{0,8},{4,12},{8,0},{12,4},{16,24},{20,28},{24,16},{28,20},{1,9},{5... | collective-permute-start | bytes 589832 | tf_op jit(solution)/shard_map/ppermute | solution.py:464
  22.3 5.2 %collective-permute-start.6 = (bf16[128,128]{1,0:T(8,128)(2,1)S(1)}, bf16[128,128]{1,0:T(8,128)(2,1)S(1)}, u32[]{:S(2)}, u32[]{:S(2)}) collective-permute-start(bf16[128,128]{1,0:T(8,128)(2,1)S(1)} %pad_maximum_fusion.refs_10_), channel_id=1, source_target_pairs={{0,2},{1,3},{2,0},{3,1},{4,6},{5,7},{6,4},{7,5},{8,10},{9,11},{10,... | collective-permute-start | bytes 98312 | tf_op jit(solution)/shard_map/ppermute | solution.py:467
  29.2 2.4 %collective-permute-start.9 = (bf16[32,6656]{1,0:T(8,128)(2,1)S(1)}, bf16[32,6656]{1,0:T(8,128)(2,1)S(1)}, u32[]{:S(2)}, u32[]{:S(2)}) collective-permute-start(bf16[32,6656]{1,0:T(8,128)(2,1)S(1)} %collective-permute-done.1.refs_2_), channel_id=1, source_target_pairs={{0,4},{4,0},{8,12},{12,8},{16,20},{20,16},{24,28},{28,24},{1,5},{5... | collective-permute-start | bytes 1277960 | tf_op jit(solution)/shard_map/ppermute | solution.py:464
  29.2 2.4 %collective-permute-start.10 = (bf16[32,3584]{1,0:T(8,128)(2,1)S(1)}, bf16[32,3584]{1,0:T(8,128)(2,1)S(1)}, u32[]{:S(2)}, u32[]{:S(2)}) collective-permute-start(bf16[32,3584]{1,0:T(8,128)(2,1)S(1)} %collective-permute-done.4.refs_3_), channel_id=1, source_target_pairs={{0,4},{4,0},{8,12},{12,8},{16,20},{20,16},{24,28},{28,24},{1,5},{5... | collective-permute-start | bytes 688136 | tf_op jit(solution)/shard_map/ppermute | solution.py:464
  29.7 1.9 %collective-permute-start.11 = (bf16[32,3072]{1,0:T(8,128)(2,1)S(1)}, bf16[32,3072]{1,0:T(8,128)(2,1)S(1)}, u32[]{:S(2)}, u32[]{:S(2)}) collective-permute-start(bf16[32,3072]{1,0:T(8,128)(2,1)S(1)} %collective-permute-done.5.refs_4_), channel_id=1, source_target_pairs={{0,4},{4,0},{8,12},{12,8},{16,20},{20,16},{24,28},{28,24},{1,5},{5... | collective-permute-start | bytes 589832 | tf_op jit(solution)/shard_map/ppermute | solution.py:464
  33.2 7.1 %collective-permute-start.12 = (f32[4,128]{1,0:T(4,128)S(1)}, f32[4,128]{1,0:T(4,128)S(1)}, u32[]{:S(2)}, u32[]{:S(2)}) collective-permute-start(f32[4,128]{1,0:T(4,128)S(1)} %get-tuple-element.115), channel_id=1, source_target_pairs={{0,1},{1,0},{2,3},{3,2},{4,5},{5,4},{6,7},{7,6},{8,9},{9,8},{10,11... | collective-permute-start | bytes 6152 | tf_op jit(solution)/shard_map/ppermute | solution.py:467
  33.9 6.4 %collective-permute-start.13 = (f32[4,128]{1,0:T(4,128)S(1)}, f32[4,128]{1,0:T(4,128)S(1)}, u32[]{:S(2)}, u32[]{:S(2)}) collective-permute-start(f32[4,128]{1,0:T(4,128)S(1)} %get-tuple-element.116), channel_id=1, source_target_pairs={{0,2},{1,3},{2,0},{3,1},{4,6},{5,7},{6,4},{7,5},{8,10},{9,11},{10,... | collective-permute-start | bytes 6152 | tf_op jit(solution)/shard_map/ppermute | solution.py:467
  35.1 5.4 %collective-permute-start.14 = (f32[4,128]{1,0:T(4,128)S(1)}, f32[4,128]{1,0:T(4,128)S(1)}, u32[]{:S(2)}, u32[]{:S(2)}) collective-permute-start(f32[4,128]{1,0:T(4,128)S(1)} %get-tuple-element.117), channel_id=1, source_target_pairs={{0,3},{1,2},{2,1},{3,0},{4,7},{5,6},{6,5},{7,4},{8,11},{9,10},{10,... | collective-permute-start | bytes 6152 | tf_op jit(solution)/shard_map/ppermute | solution.py:467
